TPU v7x, 32 devices: a whole 2x2x4 slice. The times are simulated.
32 devices in a mesh: gx: 2 (over x), gy: 4 (over y, core), gz: 4 (over z).
Axes of the slice: x: 2, y: 2, z: 4, core: 2. Of those that a mesh axis runs over, the one named last changes fastest.
Arguments:
- body_local: float32 [3, 4, 8, 16, 128], P(None, 'gx', 'gy', 'gz'), as said below
- charges: float32 [4, 8, 16, 128], P('gx', 'gy', 'gz'), may hold values from -1 to 1
- radii: float32 [4, 8, 16, 128], P('gx', 'gy', 'gz'), may hold values from 0.05 to 0.15
- body_slot: int32 [4, 8, 16, 128], P('gx', 'gy', 'gz'), may hold values from 0 to 647, as said below
- cell_counts: int32 [4, 8, 16], P('gx', 'gy', 'gz'), may hold values from 16 to 128, as said below
- poses: float32 [12, 768], P(None, ('gx', 'gy', 'gz')), as said below
- mobility: float32 [2, 768], P(None, ('gx', 'gy', 'gz')), may hold values from 0.5 to 2
- noise: float32 [6, 768], P(None, ('gx', 'gy', 'gz')), may hold values from -1 to 1
Outputs:
- stepped_poses: float32 [12, 768], P(None, ('gx', 'gy', 'gz'))
- positions: float32 [3, 4, 8, 16, 128], P(None, 'gx', 'gy', 'gz')
Inputs may be any that keep to these rules, and one draw needn't show every extreme that they name: Every atom slot belongs to a body owned by its own device or by one of the devices next to it along each axis, periodically; body_slot = (9 (dx + 1) + 3 (dy + 1) + (dz + 1)) * 24 + k names body k of the device at offset (dx, dy, dz). `cell_counts`: slots 0 to count - 1 of a cell hold atoms; the other slots are empty. `poses`: rows 0 to 8 form a rotation matrix; the centre lies inside the brick of the owner device. `body_local`: R local + t of every slot lies, up to whole periods of the box, inside the slot's cell.
All inputs are finite; a program needn't handle non-finite values.
Results may differ from a plain program's by a relative error of at most 0.0003.
Values sent between devices are 32-bit elements; how exact they have to be, the bound alone decides.
No kernel may reach another device: no remote copies, remote signals or barrier semaphores. Data moves between devices by JAX's collectives and lax.ppermute only.
A program may use at most 64 MiB of HBM per device.

v0:
```python
import jax
import jax.numpy as jnp
from jax import lax
from jax.sharding import PartitionSpec as P

min_reach = 0.15
clash_gain = 20.0
debye_length = 0.5
move_gain = 0.02
turn_gain = 0.01


def extended_2(block, sides, width):
    for axis, dim in sides:
        count = lax.axis_size(axis)
        forward = [(i, i + 1) for i in range(count - 1)]
        forward.append((count - 1, 0))
        backward = [(target, source) for source, target in forward]
        low = lax.ppermute(
            lax.slice_in_dim(block, block.shape[dim] - width, None, axis=dim), axis, forward
        )
        high = lax.ppermute(lax.slice_in_dim(block, 0, width, axis=dim), axis, backward)
        block = jnp.concatenate([low, block, high], axis=dim)
    return block


def shifted(block, axis, distance):
    devices = range(lax.axis_size(axis))
    route = [((i - distance) % len(devices), i) for i in devices]
    return lax.ppermute(block, axis, route)


def pair_force(own_cells, other_cells, domain_extent):
    delta = own_cells[0:3, :, :, None] - other_cells[0:3, :, None, :]
    delta = delta - domain_extent * jnp.floor(delta / domain_extent + 0.5)
    dist_sq = jnp.sum(delta * delta, axis=0)
    dist = jnp.sqrt(dist_sq)
    reach = jnp.maximum(dist, min_reach)
    switch = jnp.square(jnp.maximum(1.0 - dist_sq, 0.0))
    sigma = own_cells[4][:, :, None] + other_cells[4][:, None, :]
    clash = clash_gain * jnp.maximum(sigma - dist, 0.0)
    screened = (
        own_cells[3][:, :, None]
        * other_cells[3][:, None, :]
        * jnp.exp(-dist / debye_length)
        * (1.0 / reach + 1.0 / debye_length)
        / reach
        * switch
    )
    weight = own_cells[5][:, :, None] * other_cells[5][:, None, :] * (clash + screened) / reach
    return jnp.sum(weight[None] * delta, axis=-1)


def place_atoms(pose_rows, resident_rows):
    arm_rows = jnp.stack(
        [
            pose_rows[3 * row_at] * resident_rows[0]
            + pose_rows[3 * row_at + 1] * resident_rows[1]
            + pose_rows[3 * row_at + 2] * resident_rows[2]
            for row_at in range(3)
        ]
    )
    return (arm_rows, arm_rows + pose_rows[9:12])


def cross_rows(first_rows, second_rows):
    return jnp.stack(
        [
            first_rows[1] * second_rows[2] - first_rows[2] * second_rows[1],
            first_rows[2] * second_rows[0] - first_rows[0] * second_rows[2],
            first_rows[0] * second_rows[1] - first_rows[1] * second_rows[0],
        ]
    )


def advance(pose_rows, totals, mobility, noise):
    centre = pose_rows[9:12] + move_gain * mobility[0] * totals[0:3] + noise[0:3]
    spin = 0.5 * (turn_gain * mobility[1] * totals[3:6] + noise[3:6])
    spin_sq = jnp.sum(spin * spin, axis=0)
    factor = 2.0 / (1.0 + spin_sq)
    skew_mat = [[None, -spin[2], spin[1]], [spin[2], None, -spin[0]], [-spin[1], spin[0], None]]
    turn = []
    for row_at in range(3):
        line = []
        for col_at in range(3):
            inner = spin[row_at] * spin[col_at]
            if row_at == col_at:
                line.append(1.0 + factor * (inner - spin_sq))
            else:
                line.append(factor * (skew_mat[row_at][col_at] + inner))
        turn.append(line)
    rotated = []
    for row_at in range(3):
        for col_at in range(3):
            rotated.append(
                turn[row_at][0] * pose_rows[col_at]
                + turn[row_at][1] * pose_rows[3 + col_at]
                + turn[row_at][2] * pose_rows[6 + col_at]
            )
    return jnp.concatenate([jnp.stack(rotated), centre], axis=0)


def per_device(body_local, charges, radii, body_slot, cell_counts, poses, mobility, noise):
    cells_x, cells_y, cells_z, width = charges.shape
    owned = poses.shape[1]
    slots = body_slot.reshape(-1)
    resident_rows = body_local.reshape(3, -1)
    near_poses = extended_2(poses.reshape(12, 1, 1, 1, owned), (("gx", 1), ("gy", 2), ("gz", 3)), 1)
    arm_rows, placement_index = place_atoms(
        jnp.take(near_poses.reshape(12, 27 * owned), slots, axis=1), resident_rows
    )
    slot_iota = lax.broadcasted_iota(jnp.int32, (cells_x, cells_y, cells_z, width), 3)
    filled_slots = (slot_iota < cell_counts[..., None]).astype(jnp.float32)
    message_rows = jnp.concatenate(
        [
            placement_index.reshape(3, cells_x, cells_y, cells_z, width),
            charges[None],
            radii[None],
            filled_slots[None],
        ],
        axis=0,
    )
    extended = extended_2(message_rows, (("gx", 1), ("gy", 2), ("gz", 3)), 1)
    domain_extent = jnp.array(
        [
            cells_x * lax.axis_size("gx"),
            cells_y * lax.axis_size("gy"),
            cells_z * lax.axis_size("gz"),
        ],
        jnp.float32,
    )[:, None, None, None]
    own_slabs = jnp.moveaxis(message_rows, 1, 0).reshape(cells_x, 6, cells_y * cells_z, width)

    def visit(offset_code, running):
        step_x = offset_code // 9
        step_y = offset_code // 3 % 3
        step_z = offset_code % 3
        neighbour_block = lax.dynamic_slice(
            extended, (0, step_x, step_y, step_z, 0), (6, cells_x, cells_y, cells_z, width)
        )
        other_slabs = jnp.moveaxis(neighbour_block, 1, 0).reshape(
            cells_x, 6, cells_y * cells_z, width
        )
        part_force = lax.map(
            lambda pair: pair_force(pair[0], pair[1], domain_extent), (own_slabs, other_slabs)
        )
        return running + part_force

    force_slabs = lax.fori_loop(
        0, 27, visit, jnp.zeros((cells_x, 3, cells_y * cells_z, width), jnp.float32)
    )
    force = jnp.moveaxis(force_slabs, 1, 0).reshape(3, -1)
    torque = cross_rows(arm_rows, force)
    contrib = jnp.concatenate([force, torque], axis=0)
    partial_value = jax.ops.segment_sum(contrib.T, slots, num_segments=27 * owned).T
    layered = partial_value.reshape(6, 3, 3, 3, owned)
    plane_sums = layered[:, 1] + shifted(layered[:, 2], "gx", 1) + shifted(layered[:, 0], "gx", -1)
    line_sums = (
        plane_sums[:, 1] + shifted(plane_sums[:, 2], "gy", 1) + shifted(plane_sums[:, 0], "gy", -1)
    )
    totals = (
        line_sums[:, 1] + shifted(line_sums[:, 2], "gz", 1) + shifted(line_sums[:, 0], "gz", -1)
    )
    stepped_poses = advance(poses, totals, mobility, noise)
    after_poses = extended_2(
        stepped_poses.reshape(12, 1, 1, 1, owned), (("gx", 1), ("gy", 2), ("gz", 3)), 1
    )
    moved_arm, shifted_poses = place_atoms(
        jnp.take(after_poses.reshape(12, 27 * owned), slots, axis=1), resident_rows
    )
    return (stepped_poses, shifted_poses.reshape(3, cells_x, cells_y, cells_z, width))


def solution(mesh):
    placed = (
        P(None, "gx", "gy", "gz", None),
        P("gx", "gy", "gz", None),
        P("gx", "gy", "gz", None),
        P("gx", "gy", "gz", None),
        P("gx", "gy", "gz"),
        P(None, ("gx", "gy", "gz")),
        P(None, ("gx", "gy", "gz")),
        P(None, ("gx", "gy", "gz")),
    )
    return jax.shard_map(
        per_device,
        mesh=mesh,
        in_specs=placed,
        out_specs=(P(None, ("gx", "gy", "gz")), P(None, "gx", "gy", "gz", None)),
        check_vma=False,
    )
```

profile of v0, /device:TPU:0, one launch (start us, length us, event | category | flops | bytes accessed | tf_op | source)
XLA Modules:
  0.0 207.2 jit_solution(4449134142025507900)
XLA Ops:
  21.1 5.5 %gather_fusion = f32[2048,12]{1,0:T(8,128)S(1)} fusion(f32[12,648]{0,1:T(8,128)S(1)} %bitcast.161, s32[2048]{0:T(1024)S(1)} %fusion.25), kind=kCustom, calls=%fused_computation.clone | custom fusion | bytes 204800 | tf_op jit(solution)/shard_map/jit(_take)/gather | solution.py:110
  42.3 116.0 %while.58 = (s32[]{:T(128)}, f32[2,3,8,128]{3,2,1,0:T(8,128)S(1)}, f32[6,4,4,6,128]{4,3,2,0,1:T(8,128)S(1)}, f32[2,6,8,128]{3,2,1,0:T(8,128)S(1)}, s32[]{:T(128)...) while((s32[]{:T(128)}, f32[2,3,8,128]{3,2,1,0:T(8,128)S(1)}, ...), condition=%wide.region_5.7_spmd.clone.clone.clone, body=%wide.region_0.6_spmd.clone.clone.sunk.clone | while | flops 8922153 | bytes 2478868 | solution.py:149
  42.4 4.1 %while.57 = (s32[]{:T(128)}, f32[2,3,8,128]{3,2,1,0:T(8,128)S(1)}, f32[2,6,8,128]{3,2,1,0:T(8,128)S(1)}, f32[2,6,8,128]{3,2,1,0:T(8,128)S(1)}, f32[3,1,1,1]{0,3,...) while((s32[]{:T(128)}, f32[2,3,8,128]{3,2,1,0:T(8,128)S(1)}, f32[2,6,8,128]{3,2,1,0:T(8,128)S(1)}, ...), condition=%wide.region_4.5_spmd, body=%wide.region_1.4_spmd.sunk | while | flops 8909829 | bytes 2306233 | solution.py:144
  46.7 4.1 %while.57 = (s32[]{:T(128)}, f32[2,3,8,128]{3,2,1,0:T(8,128)S(1)}, f32[2,6,8,128]{3,2,1,0:T(8,128)S(1)}, f32[2,6,8,128]{3,2,1,0:T(8,128)S(1)}, f32[3,1,1,1]{0,3,...) while((s32[]{:T(128)}, f32[2,3,8,128]{3,2,1,0:T(8,128)S(1)}, f32[2,6,8,128]{3,2,1,0:T(8,128)S(1)}, ...), condition=%wide.region_4.5_spmd, body=%wide.region_1.4_spmd.sunk | while | flops 8909829 | bytes 2306233 | solution.py:144
  51.0 4.1 %while.57 = (s32[]{:T(128)}, f32[2,3,8,128]{3,2,1,0:T(8,128)S(1)}, f32[2,6,8,128]{3,2,1,0:T(8,128)S(1)}, f32[2,6,8,128]{3,2,1,0:T(8,128)S(1)}, f32[3,1,1,1]{0,3,...) while((s32[]{:T(128)}, f32[2,3,8,128]{3,2,1,0:T(8,128)S(1)}, f32[2,6,8,128]{3,2,1,0:T(8,128)S(1)}, ...), condition=%wide.region_4.5_spmd, body=%wide.region_1.4_spmd.sunk | while | flops 8909829 | bytes 2306233 | solution.py:144
  55.3 4.1 %while.57 = (s32[]{:T(128)}, f32[2,3,8,128]{3,2,1,0:T(8,128)S(1)}, f32[2,6,8,128]{3,2,1,0:T(8,128)S(1)}, f32[2,6,8,128]{3,2,1,0:T(8,128)S(1)}, f32[3,1,1,1]{0,3,...) while((s32[]{:T(128)}, f32[2,3,8,128]{3,2,1,0:T(8,128)S(1)}, f32[2,6,8,128]{3,2,1,0:T(8,128)S(1)}, ...), condition=%wide.region_4.5_spmd, body=%wide.region_1.4_spmd.sunk | while | flops 8909829 | bytes 2306233 | solution.py:144
  59.6 4.1 %while.57 = (s32[]{:T(128)}, f32[2,3,8,128]{3,2,1,0:T(8,128)S(1)}, f32[2,6,8,128]{3,2,1,0:T(8,128)S(1)}, f32[2,6,8,128]{3,2,1,0:T(8,128)S(1)}, f32[3,1,1,1]{0,3,...) while((s32[]{:T(128)}, f32[2,3,8,128]{3,2,1,0:T(8,128)S(1)}, f32[2,6,8,128]{3,2,1,0:T(8,128)S(1)}, ...), condition=%wide.region_4.5_spmd, body=%wide.region_1.4_spmd.sunk | while | flops 8909829 | bytes 2306233 | solution.py:144
  63.9 4.1 %while.57 = (s32[]{:T(128)}, f32[2,3,8,128]{3,2,1,0:T(8,128)S(1)}, f32[2,6,8,128]{3,2,1,0:T(8,128)S(1)}, f32[2,6,8,128]{3,2,1,0:T(8,128)S(1)}, f32[3,1,1,1]{0,3,...) while((s32[]{:T(128)}, f32[2,3,8,128]{3,2,1,0:T(8,128)S(1)}, f32[2,6,8,128]{3,2,1,0:T(8,128)S(1)}, ...), condition=%wide.region_4.5_spmd, body=%wide.region_1.4_spmd.sunk | while | flops 8909829 | bytes 2306233 | solution.py:144
  68.2 4.1 %while.57 = (s32[]{:T(128)}, f32[2,3,8,128]{3,2,1,0:T(8,128)S(1)}, f32[2,6,8,128]{3,2,1,0:T(8,128)S(1)}, f32[2,6,8,128]{3,2,1,0:T(8,128)S(1)}, f32[3,1,1,1]{0,3,...) while((s32[]{:T(128)}, f32[2,3,8,128]{3,2,1,0:T(8,128)S(1)}, f32[2,6,8,128]{3,2,1,0:T(8,128)S(1)}, ...), condition=%wide.region_4.5_spmd, body=%wide.region_1.4_spmd.sunk | while | flops 8909829 | bytes 2306233 | solution.py:144
  72.5 4.1 %while.57 = (s32[]{:T(128)}, f32[2,3,8,128]{3,2,1,0:T(8,128)S(1)}, f32[2,6,8,128]{3,2,1,0:T(8,128)S(1)}, f32[2,6,8,128]{3,2,1,0:T(8,128)S(1)}, f32[3,1,1,1]{0,3,...) while((s32[]{:T(128)}, f32[2,3,8,128]{3,2,1,0:T(8,128)S(1)}, f32[2,6,8,128]{3,2,1,0:T(8,128)S(1)}, ...), condition=%wide.region_4.5_spmd, body=%wide.region_1.4_spmd.sunk | while | flops 8909829 | bytes 2306233 | solution.py:144
  76.8 4.1 %while.57 = (s32[]{:T(128)}, f32[2,3,8,128]{3,2,1,0:T(8,128)S(1)}, f32[2,6,8,128]{3,2,1,0:T(8,128)S(1)}, f32[2,6,8,128]{3,2,1,0:T(8,128)S(1)}, f32[3,1,1,1]{0,3,...) while((s32[]{:T(128)}, f32[2,3,8,128]{3,2,1,0:T(8,128)S(1)}, f32[2,6,8,128]{3,2,1,0:T(8,128)S(1)}, ...), condition=%wide.region_4.5_spmd, body=%wide.region_1.4_spmd.sunk | while | flops 8909829 | bytes 2306233 | solution.py:144
  81.1 4.1 %while.57 = (s32[]{:T(128)}, f32[2,3,8,128]{3,2,1,0:T(8,128)S(1)}, f32[2,6,8,128]{3,2,1,0:T(8,128)S(1)}, f32[2,6,8,128]{3,2,1,0:T(8,128)S(1)}, f32[3,1,1,1]{0,3,...) while((s32[]{:T(128)}, f32[2,3,8,128]{3,2,1,0:T(8,128)S(1)}, f32[2,6,8,128]{3,2,1,0:T(8,128)S(1)}, ...), condition=%wide.region_4.5_spmd, body=%wide.region_1.4_spmd.sunk | while | flops 8909829 | bytes 2306233 | solution.py:144
  85.4 4.1 %while.57 = (s32[]{:T(128)}, f32[2,3,8,128]{3,2,1,0:T(8,128)S(1)}, f32[2,6,8,128]{3,2,1,0:T(8,128)S(1)}, f32[2,6,8,128]{3,2,1,0:T(8,128)S(1)}, f32[3,1,1,1]{0,3,...) while((s32[]{:T(128)}, f32[2,3,8,128]{3,2,1,0:T(8,128)S(1)}, f32[2,6,8,128]{3,2,1,0:T(8,128)S(1)}, ...), condition=%wide.region_4.5_spmd, body=%wide.region_1.4_spmd.sunk | while | flops 8909829 | bytes 2306233 | solution.py:144
  89.7 4.1 %while.57 = (s32[]{:T(128)}, f32[2,3,8,128]{3,2,1,0:T(8,128)S(1)}, f32[2,6,8,128]{3,2,1,0:T(8,128)S(1)}, f32[2,6,8,128]{3,2,1,0:T(8,128)S(1)}, f32[3,1,1,1]{0,3,...) while((s32[]{:T(128)}, f32[2,3,8,128]{3,2,1,0:T(8,128)S(1)}, f32[2,6,8,128]{3,2,1,0:T(8,128)S(1)}, ...), condition=%wide.region_4.5_spmd, body=%wide.region_1.4_spmd.sunk | while | flops 8909829 | bytes 2306233 | solution.py:144
  94.0 4.1 %while.57 = (s32[]{:T(128)}, f32[2,3,8,128]{3,2,1,0:T(8,128)S(1)}, f32[2,6,8,128]{3,2,1,0:T(8,128)S(1)}, f32[2,6,8,128]{3,2,1,0:T(8,128)S(1)}, f32[3,1,1,1]{0,3,...) while((s32[]{:T(128)}, f32[2,3,8,128]{3,2,1,0:T(8,128)S(1)}, f32[2,6,8,128]{3,2,1,0:T(8,128)S(1)}, ...), condition=%wide.region_4.5_spmd, body=%wide.region_1.4_spmd.sunk | while | flops 8909829 | bytes 2306233 | solution.py:144
  98.3 4.1 %while.57 = (s32[]{:T(128)}, f32[2,3,8,128]{3,2,1,0:T(8,128)S(1)}, f32[2,6,8,128]{3,2,1,0:T(8,128)S(1)}, f32[2,6,8,128]{3,2,1,0:T(8,128)S(1)}, f32[3,1,1,1]{0,3,...) while((s32[]{:T(128)}, f32[2,3,8,128]{3,2,1,0:T(8,128)S(1)}, f32[2,6,8,128]{3,2,1,0:T(8,128)S(1)}, ...), condition=%wide.region_4.5_spmd, body=%wide.region_1.4_spmd.sunk | while | flops 8909829 | bytes 2306233 | solution.py:144
  102.6 4.1 %while.57 = (s32[]{:T(128)}, f32[2,3,8,128]{3,2,1,0:T(8,128)S(1)}, f32[2,6,8,128]{3,2,1,0:T(8,128)S(1)}, f32[2,6,8,128]{3,2,1,0:T(8,128)S(1)}, f32[3,1,1,1]{0,3,...) while((s32[]{:T(128)}, f32[2,3,8,128]{3,2,1,0:T(8,128)S(1)}, f32[2,6,8,128]{3,2,1,0:T(8,128)S(1)}, ...), condition=%wide.region_4.5_spmd, body=%wide.region_1.4_spmd.sunk | while | flops 8909829 | bytes 2306233 | solution.py:144
  106.9 4.1 %while.57 = (s32[]{:T(128)}, f32[2,3,8,128]{3,2,1,0:T(8,128)S(1)}, f32[2,6,8,128]{3,2,1,0:T(8,128)S(1)}, f32[2,6,8,128]{3,2,1,0:T(8,128)S(1)}, f32[3,1,1,1]{0,3,...) while((s32[]{:T(128)}, f32[2,3,8,128]{3,2,1,0:T(8,128)S(1)}, f32[2,6,8,128]{3,2,1,0:T(8,128)S(1)}, ...), condition=%wide.region_4.5_spmd, body=%wide.region_1.4_spmd.sunk | while | flops 8909829 | bytes 2306233 | solution.py:144
  111.2 4.1 %while.57 = (s32[]{:T(128)}, f32[2,3,8,128]{3,2,1,0:T(8,128)S(1)}, f32[2,6,8,128]{3,2,1,0:T(8,128)S(1)}, f32[2,6,8,128]{3,2,1,0:T(8,128)S(1)}, f32[3,1,1,1]{0,3,...) while((s32[]{:T(128)}, f32[2,3,8,128]{3,2,1,0:T(8,128)S(1)}, f32[2,6,8,128]{3,2,1,0:T(8,128)S(1)}, ...), condition=%wide.region_4.5_spmd, body=%wide.region_1.4_spmd.sunk | while | flops 8909829 | bytes 2306233 | solution.py:144
  115.5 4.1 %while.57 = (s32[]{:T(128)}, f32[2,3,8,128]{3,2,1,0:T(8,128)S(1)}, f32[2,6,8,128]{3,2,1,0:T(8,128)S(1)}, f32[2,6,8,128]{3,2,1,0:T(8,128)S(1)}, f32[3,1,1,1]{0,3,...) while((s32[]{:T(128)}, f32[2,3,8,128]{3,2,1,0:T(8,128)S(1)}, f32[2,6,8,128]{3,2,1,0:T(8,128)S(1)}, ...), condition=%wide.region_4.5_spmd, body=%wide.region_1.4_spmd.sunk | while | flops 8909829 | bytes 2306233 | solution.py:144
  119.8 4.1 %while.57 = (s32[]{:T(128)}, f32[2,3,8,128]{3,2,1,0:T(8,128)S(1)}, f32[2,6,8,128]{3,2,1,0:T(8,128)S(1)}, f32[2,6,8,128]{3,2,1,0:T(8,128)S(1)}, f32[3,1,1,1]{0,3,...) while((s32[]{:T(128)}, f32[2,3,8,128]{3,2,1,0:T(8,128)S(1)}, f32[2,6,8,128]{3,2,1,0:T(8,128)S(1)}, ...), condition=%wide.region_4.5_spmd, body=%wide.region_1.4_spmd.sunk | while | flops 8909829 | bytes 2306233 | solution.py:144
  124.1 4.1 %while.57 = (s32[]{:T(128)}, f32[2,3,8,128]{3,2,1,0:T(8,128)S(1)}, f32[2,6,8,128]{3,2,1,0:T(8,128)S(1)}, f32[2,6,8,128]{3,2,1,0:T(8,128)S(1)}, f32[3,1,1,1]{0,3,...) while((s32[]{:T(128)}, f32[2,3,8,128]{3,2,1,0:T(8,128)S(1)}, f32[2,6,8,128]{3,2,1,0:T(8,128)S(1)}, ...), condition=%wide.region_4.5_spmd, body=%wide.region_1.4_spmd.sunk | while | flops 8909829 | bytes 2306233 | solution.py:144
  128.4 4.1 %while.57 = (s32[]{:T(128)}, f32[2,3,8,128]{3,2,1,0:T(8,128)S(1)}, f32[2,6,8,128]{3,2,1,0:T(8,128)S(1)}, f32[2,6,8,128]{3,2,1,0:T(8,128)S(1)}, f32[3,1,1,1]{0,3,...) while((s32[]{:T(128)}, f32[2,3,8,128]{3,2,1,0:T(8,128)S(1)}, f32[2,6,8,128]{3,2,1,0:T(8,128)S(1)}, ...), condition=%wide.region_4.5_spmd, body=%wide.region_1.4_spmd.sunk | while | flops 8909829 | bytes 2306233 | solution.py:144
  132.7 4.1 %while.57 = (s32[]{:T(128)}, f32[2,3,8,128]{3,2,1,0:T(8,128)S(1)}, f32[2,6,8,128]{3,2,1,0:T(8,128)S(1)}, f32[2,6,8,128]{3,2,1,0:T(8,128)S(1)}, f32[3,1,1,1]{0,3,...) while((s32[]{:T(128)}, f32[2,3,8,128]{3,2,1,0:T(8,128)S(1)}, f32[2,6,8,128]{3,2,1,0:T(8,128)S(1)}, ...), condition=%wide.region_4.5_spmd, body=%wide.region_1.4_spmd.sunk | while | flops 8909829 | bytes 2306233 | solution.py:144
  137.0 4.1 %while.57 = (s32[]{:T(128)}, f32[2,3,8,128]{3,2,1,0:T(8,128)S(1)}, f32[2,6,8,128]{3,2,1,0:T(8,128)S(1)}, f32[2,6,8,128]{3,2,1,0:T(8,128)S(1)}, f32[3,1,1,1]{0,3,...) while((s32[]{:T(128)}, f32[2,3,8,128]{3,2,1,0:T(8,128)S(1)}, f32[2,6,8,128]{3,2,1,0:T(8,128)S(1)}, ...), condition=%wide.region_4.5_spmd, body=%wide.region_1.4_spmd.sunk | while | flops 8909829 | bytes 2306233 | solution.py:144
  141.3 4.1 %while.57 = (s32[]{:T(128)}, f32[2,3,8,128]{3,2,1,0:T(8,128)S(1)}, f32[2,6,8,128]{3,2,1,0:T(8,128)S(1)}, f32[2,6,8,128]{3,2,1,0:T(8,128)S(1)}, f32[3,1,1,1]{0,3,...) while((s32[]{:T(128)}, f32[2,3,8,128]{3,2,1,0:T(8,128)S(1)}, f32[2,6,8,128]{3,2,1,0:T(8,128)S(1)}, ...), condition=%wide.region_4.5_spmd, body=%wide.region_1.4_spmd.sunk | while | flops 8909829 | bytes 2306233 | solution.py:144
  145.6 4.1 %while.57 = (s32[]{:T(128)}, f32[2,3,8,128]{3,2,1,0:T(8,128)S(1)}, f32[2,6,8,128]{3,2,1,0:T(8,128)S(1)}, f32[2,6,8,128]{3,2,1,0:T(8,128)S(1)}, f32[3,1,1,1]{0,3,...) while((s32[]{:T(128)}, f32[2,3,8,128]{3,2,1,0:T(8,128)S(1)}, f32[2,6,8,128]{3,2,1,0:T(8,128)S(1)}, ...), condition=%wide.region_4.5_spmd, body=%wide.region_1.4_spmd.sunk | while | flops 8909829 | bytes 2306233 | solution.py:144
  149.9 4.1 %while.57 = (s32[]{:T(128)}, f32[2,3,8,128]{3,2,1,0:T(8,128)S(1)}, f32[2,6,8,128]{3,2,1,0:T(8,128)S(1)}, f32[2,6,8,128]{3,2,1,0:T(8,128)S(1)}, f32[3,1,1,1]{0,3,...) while((s32[]{:T(128)}, f32[2,3,8,128]{3,2,1,0:T(8,128)S(1)}, f32[2,6,8,128]{3,2,1,0:T(8,128)S(1)}, ...), condition=%wide.region_4.5_spmd, body=%wide.region_1.4_spmd.sunk | while | flops 8909829 | bytes 2306233 | solution.py:144
  154.2 4.1 %while.57 = (s32[]{:T(128)}, f32[2,3,8,128]{3,2,1,0:T(8,128)S(1)}, f32[2,6,8,128]{3,2,1,0:T(8,128)S(1)}, f32[2,6,8,128]{3,2,1,0:T(8,128)S(1)}, f32[3,1,1,1]{0,3,...) while((s32[]{:T(128)}, f32[2,3,8,128]{3,2,1,0:T(8,128)S(1)}, f32[2,6,8,128]{3,2,1,0:T(8,128)S(1)}, ...), condition=%wide.region_4.5_spmd, body=%wide.region_1.4_spmd.sunk | while | flops 8909829 | bytes 2306233 | solution.py:144
  158.9 11.6 %scatter_custom_fusion = f32[648,6]{1,0:T(8,128)S(1)} fusion(s32[2048]{0:T(1024)} %bitcast.196, f32[2048,6]{1,0:T(8,128)S(1)} %copy.138, f32[]{:T(128)} %constant.152.clone.1), kind=kCustom, calls=%fused_computation.30 | custom fusion | flops 12288 | bytes 16064 | tf_op jit(solution)/shard_map/scatter-add | solution.py:155
  179.4 3.9 %collective-permute-start.17 = (f32[6,24]{1,0:T(8,128)S(1)}, f32[6,24]{1,0:T(8,128)S(1)}, u32[]{:S(2)}, u32[]{:S(2)}) collective-permute-start(f32[6,24]{1,0:T(8,128)S(1)} %get-tuple-element.317), channel_id=1, source_target_pairs={{1,0},{2,1},{3,2},{0,3},{5,4},{6,5},{7,6},{4,7},{9,8},{10,9},{11,1... | collective-permute-start | bytes 1736 | tf_op jit(solution)/shard_map/ppermute | solution.py:30
  200.6 5.5 %gather_fusion.1 = f32[2048,12]{1,0:T(8,128)S(1)} fusion(f32[12,648]{0,1:T(8,128)S(1)} %bitcast.160, s32[2048]{0:T(1024)S(1)} %fusion.25), kind=kCustom, calls=%fused_computation.1.clone | custom fusion | bytes 204800 | tf_op jit(solution)/shard_map/jit(_take)/gather | solution.py:169
  (518 shorter events, 173.4 us)
Async XLA Ops:
  0.6 4.8 %collective-permute-start = (f32[12,1,1,1,24]{4,0,3,2,1:T(8,128)}, f32[12,1,1,1,24]{4,0,3,2,1:T(8,128)S(1)}, u32[]{:S(2)}, u32[]{:S(2)}) collective-permute-start(f32[12,1,1,1,24]{4,0,3,2,1:T(8,128)} %bitcast.167), channel_id=1, source_target_pairs={{0,16},{16,0},{1,17},{17,1},{2,18},{18,2},{3,19},{19,3},{4,20},{20... | collective-permute-start | bytes 3464 | tf_op jit(solution)/shard_map/ppermute | solution.py:19
  3.6 3.9 %collective-permute-start.1 = (f32[12,1,1,1,24]{4,0,3,2,1:T(8,128)}, f32[12,1,1,1,24]{4,0,3,2,1:T(8,128)S(1)}, u32[]{:S(2)}, u32[]{:S(2)}) collective-permute-start(f32[12,1,1,1,24]{4,0,3,2,1:T(8,128)} %bitcast.168), channel_id=1, source_target_pairs={{16,0},{0,16},{17,1},{1,17},{18,2},{2,18},{19,3},{3,19},{20,4},{4,... | collective-permute-start | bytes 3464 | tf_op jit(solution)/shard_map/ppermute | solution.py:22
  8.2 3.3 %collective-permute-start.2 = (f32[12,3,1,1,24]{4,0,3,2,1:T(8,128)S(1)}, f32[12,3,1,1,24]{4,0,3,2,1:T(8,128)S(1)}, u32[]{:S(2)}, u32[]{:S(2)}) collective-permute-start(f32[12,3,1,1,24]{4,0,3,2,1:T(8,128)S(1)} %pad_maximum_fusion.8), channel_id=1, source_target_pairs={{0,4},{4,8},{8,12},{12,0},{1,5},{5,9},{9,13},{13,1},{2,6},{6,10},{... | collective-permute-start | bytes 10376 | tf_op jit(solution)/shard_map/ppermute | solution.py:19
  8.2 3.3 %collective-permute-start.3 = (f32[12,3,1,1,24]{4,0,3,2,1:T(8,128)S(1)}, f32[12,3,1,1,24]{4,0,3,2,1:T(8,128)S(1)}, u32[]{:S(2)}, u32[]{:S(2)}) collective-permute-start(f32[12,3,1,1,24]{4,0,3,2,1:T(8,128)S(1)} %pad_maximum_fusion.8), channel_id=1, source_target_pairs={{4,0},{8,4},{12,8},{0,12},{5,1},{9,5},{13,9},{1,13},{6,2},{10,6},{... | collective-permute-start | bytes 10376 | tf_op jit(solution)/shard_map/ppermute | solution.py:22
  12.2 6.4 %collective-permute-start.4 = (f32[12,3,3,1,24]{4,0,3,2,1:T(8,128)S(1)}, f32[12,3,3,1,24]{4,0,3,2,1:T(8,128)S(1)}, u32[]{:S(2)}, u32[]{:S(2)}) collective-permute-start(f32[12,3,3,1,24]{4,0,3,2,1:T(8,128)S(1)} %pad_maximum_fusion.5), channel_id=1, source_target_pairs={{0,1},{1,2},{2,3},{3,0},{4,5},{5,6},{6,7},{7,4},{8,9},{9,10},{10,1... | collective-permute-start | bytes 31112 | tf_op jit(solution)/shard_map/ppermute | solution.py:19
  13.7 6.4 %collective-permute-start.5 = (f32[12,3,3,1,24]{4,0,3,2,1:T(8,128)S(1)}, f32[12,3,3,1,24]{4,0,3,2,1:T(8,128)S(1)}, u32[]{:S(2)}, u32[]{:S(2)}) collective-permute-start(f32[12,3,3,1,24]{4,0,3,2,1:T(8,128)S(1)} %pad_maximum_fusion.5), channel_id=1, source_target_pairs={{1,0},{2,1},{3,2},{0,3},{5,4},{6,5},{7,6},{4,7},{9,8},{10,9},{11,1... | collective-permute-start | bytes 31112 | tf_op jit(solution)/shard_map/ppermute | solution.py:22
  26.6 0.7 copy-start.2
  26.6 0.7 copy-start.3
  27.0 15.3 %copy-start = (f32[3,1,1,1]{0,3,2,1:T(1,128)S(1)}, f32[3,1,1,1]{0,3,2,1:T(1,128)}, u32[]{:S(2)}) copy-start(f32[3,1,1,1]{0,3,2,1:T(1,128)} %constant.287) | copy-start | bytes 40
  27.3 3.9 %collective-permute-start.6 = (f32[6,1,2,4,128]{4,3,2,0,1:T(4,128)S(1)}, f32[6,1,2,4,128]{4,3,2,0,1:T(4,128)S(1)}, u32[]{:S(2)}, u32[]{:S(2)}) collective-permute-start(f32[6,1,2,4,128]{4,3,2,0,1:T(4,128)S(1)} %get-tuple-element.301), channel_id=1, source_target_pairs={{0,16},{16,0},{1,17},{17,1},{2,18},{18,2},{3,19},{19,3},{4,20},{20... | collective-permute-start | bytes 73736 | tf_op jit(solution)/shard_map/ppermute | solution.py:19
  28.1 3.8 %collective-permute-start.7 = (f32[6,1,2,4,128]{4,3,2,0,1:T(4,128)S(1)}, f32[6,1,2,4,128]{4,3,2,0,1:T(4,128)S(1)}, u32[]{:S(2)}, u32[]{:S(2)}) collective-permute-start(f32[6,1,2,4,128]{4,3,2,0,1:T(4,128)S(1)} %get-tuple-element.302), channel_id=1, source_target_pairs={{16,0},{0,16},{17,1},{1,17},{18,2},{2,18},{19,3},{3,19},{20,4},{4,... | collective-permute-start | bytes 73736 | tf_op jit(solution)/shard_map/ppermute | solution.py:22
  32.0 3.6 %collective-permute-start.8 = (f32[6,4,1,4,128]{4,3,2,0,1:T(4,128)S(1)}, f32[6,4,1,4,128]{4,3,2,0,1:T(4,128)S(1)}, u32[]{:S(2)}, u32[]{:S(2)}) collective-permute-start(f32[6,4,1,4,128]{4,3,2,0,1:T(4,128)S(1)} %get-tuple-element.299), channel_id=1, source_target_pairs={{0,4},{4,8},{8,12},{12,0},{1,5},{5,9},{9,13},{13,1},{2,6},{6,10},{... | collective-permute-start | bytes 147464 | tf_op jit(solution)/shard_map/ppermute | solution.py:19
  32.1 3.5 %collective-permute-start.9 = (f32[6,4,1,4,128]{4,3,2,0,1:T(4,128)S(1)}, f32[6,4,1,4,128]{4,3,2,0,1:T(4,128)S(1)}, u32[]{:S(2)}, u32[]{:S(2)}) collective-permute-start(f32[6,4,1,4,128]{4,3,2,0,1:T(4,128)S(1)} %get-tuple-element.300), channel_id=1, source_target_pairs={{4,0},{8,4},{12,8},{0,12},{5,1},{9,5},{13,9},{1,13},{6,2},{10,6},{... | collective-permute-start | bytes 147464 | tf_op jit(solution)/shard_map/ppermute | solution.py:22
  35.7 6.4 %collective-permute-start.10 = (f32[6,4,4,1,128]{4,3,2,0,1:T(1,128)S(1)}, f32[6,4,4,1,128]{4,3,2,0,1:T(1,128)S(1)}, u32[]{:S(2)}, u32[]{:S(2)}) collective-permute-start(f32[6,4,4,1,128]{4,3,2,0,1:T(1,128)S(1)} %get-tuple-element.291), channel_id=1, source_target_pairs={{0,1},{1,2},{2,3},{3,0},{4,5},{5,6},{6,7},{7,4},{8,9},{9,10},{10,1... | collective-permute-start | bytes 147464 | tf_op jit(solution)/shard_map/ppermute | solution.py:19
  36.6 5.6 %collective-permute-start.11 = (f32[6,4,4,1,128]{4,3,2,0,1:T(1,128)S(1)}, f32[6,4,4,1,128]{4,3,2,0,1:T(1,128)S(1)}, u32[]{:S(2)}, u32[]{:S(2)}) collective-permute-start(f32[6,4,4,1,128]{4,3,2,0,1:T(1,128)S(1)} %get-tuple-element.292), channel_id=1, source_target_pairs={{1,0},{2,1},{3,2},{0,3},{5,4},{6,5},{7,6},{4,7},{9,8},{10,9},{11,1... | collective-permute-start | bytes 147464 | tf_op jit(solution)/shard_map/ppermute | solution.py:22
  158.9 24.4 %copy-start.6 = (f32[2,24]{1,0:T(2,128)S(1)}, f32[2,24]{1,0:T(2,128)}, u32[]{:S(2)}) copy-start(f32[2,24]{1,0:T(2,128)} %param.21) | copy-start | bytes 580
  158.9 25.9 %copy-start.1 = (f32[12,24]{1,0:T(8,128)S(1)}, f32[12,24]{1,0:T(8,128)}, u32[]{:S(2)}) copy-start(f32[12,24]{1,0:T(8,128)} %param.20) | copy-start | bytes 3460
  158.9 25.9 %copy-start.5 = (f32[6,24]{1,0:T(8,128)S(1)}, f32[6,24]{1,0:T(8,128)}, u32[]{:S(2)}) copy-start(f32[6,24]{1,0:T(8,128)} %param.22) | copy-start | bytes 1732
  170.7 4.0 %collective-permute-start.12 = (f32[6,3,3,24]{3,0,2,1:T(8,128)S(1)}, f32[6,3,3,24]{3,0,2,1:T(8,128)S(1)}, u32[]{:S(2)}, u32[]{:S(2)}) collective-permute-start(f32[6,3,3,24]{3,0,2,1:T(8,128)S(1)} %bitcast.192), channel_id=1, source_target_pairs={{16,0},{0,16},{17,1},{1,17},{18,2},{2,18},{19,3},{3,19},{20,4},{4,... | collective-permute-start | bytes 15560 | tf_op jit(solution)/shard_map/ppermute | solution.py:30
  172.1 4.0 %collective-permute-start.13 = (f32[6,3,3,24]{3,0,2,1:T(8,128)S(1)}, f32[6,3,3,24]{3,0,2,1:T(8,128)S(1)}, u32[]{:S(2)}, u32[]{:S(2)}) collective-permute-start(f32[6,3,3,24]{3,0,2,1:T(8,128)S(1)} %bitcast.193), channel_id=1, source_target_pairs={{16,0},{0,16},{17,1},{1,17},{18,2},{2,18},{19,3},{3,19},{20,4},{4,... | collective-permute-start | bytes 15560 | tf_op jit(solution)/shard_map/ppermute | solution.py:30
  176.1 3.2 %collective-permute-start.14 = (f32[6,3,24]{2,0,1:T(8,128)S(1)}, f32[6,3,24]{2,0,1:T(8,128)S(1)}, u32[]{:S(2)}, u32[]{:S(2)}) collective-permute-start(f32[6,3,24]{2,0,1:T(8,128)S(1)} %get-tuple-element.303), channel_id=1, source_target_pairs={{12,0},{0,4},{4,8},{8,12},{13,1},{1,5},{5,9},{9,13},{14,2},{2,6},{... | collective-permute-start | bytes 5192 | tf_op jit(solution)/shard_map/ppermute | solution.py:30
  176.2 3.1 %collective-permute-start.15 = (f32[6,3,24]{2,0,1:T(8,128)S(1)}, f32[6,3,24]{2,0,1:T(8,128)S(1)}, u32[]{:S(2)}, u32[]{:S(2)}) collective-permute-start(f32[6,3,24]{2,0,1:T(8,128)S(1)} %get-tuple-element.304), channel_id=1, source_target_pairs={{4,0},{8,4},{12,8},{0,12},{5,1},{9,5},{13,9},{1,13},{6,2},{10,6},{... | collective-permute-start | bytes 5192 | tf_op jit(solution)/shard_map/ppermute | solution.py:30
  179.3 5.5 %collective-permute-start.16 = (f32[6,24]{1,0:T(8,128)S(1)}, f32[6,24]{1,0:T(8,128)S(1)}, u32[]{:S(2)}, u32[]{:S(2)}) collective-permute-start(f32[6,24]{1,0:T(8,128)S(1)} %get-tuple-element.316), channel_id=1, source_target_pairs={{3,0},{0,1},{1,2},{2,3},{7,4},{4,5},{5,6},{6,7},{11,8},{8,9},{9,10... | collective-permute-start | bytes 1736 | tf_op jit(solution)/shard_map/ppermute | solution.py:30
  179.4 5.4 %collective-permute-start.17 = (f32[6,24]{1,0:T(8,128)S(1)}, f32[6,24]{1,0:T(8,128)S(1)}, u32[]{:S(2)}, u32[]{:S(2)}) collective-permute-start(f32[6,24]{1,0:T(8,128)S(1)} %get-tuple-element.317), channel_id=1, source_target_pairs={{1,0},{2,1},{3,2},{0,3},{5,4},{6,5},{7,6},{4,7},{9,8},{10,9},{11,1... | collective-permute-start | bytes 1736 | tf_op jit(solution)/shard_map/ppermute | solution.py:30
  185.0 21.1 %copy-start.4 = (f32[12,24]{1,0:T(8,128)}, f32[12,24]{1,0:T(8,128)S(1)}, u32[]{:S(2)}) copy-start(f32[12,24]{1,0:T(8,128)S(1)} %concatenate.44) | copy-start | bytes 3460
  185.0 3.7 %collective-permute-start.18 = (f32[12,1,1,1,24]{4,0,3,2,1:T(8,128)S(1)}, f32[12,1,1,1,24]{4,0,3,2,1:T(8,128)S(1)}, u32[]{:S(2)}, u32[]{:S(2)}) collective-permute-start(f32[12,1,1,1,24]{4,0,3,2,1:T(8,128)S(1)} %bitcast.180), channel_id=1, source_target_pairs={{0,16},{16,0},{1,17},{17,1},{2,18},{18,2},{3,19},{19,3},{4,20},{20... | collective-permute-start | bytes 3464 | tf_op jit(solution)/shard_map/ppermute | solution.py:19
  185.8 3.7 %collective-permute-start.19 = (f32[12,1,1,1,24]{4,0,3,2,1:T(8,128)S(1)}, f32[12,1,1,1,24]{4,0,3,2,1:T(8,128)S(1)}, u32[]{:S(2)}, u32[]{:S(2)}) collective-permute-start(f32[12,1,1,1,24]{4,0,3,2,1:T(8,128)S(1)} %bitcast.181), channel_id=1, source_target_pairs={{16,0},{0,16},{17,1},{1,17},{18,2},{2,18},{19,3},{3,19},{20,4},{4,... | collective-permute-start | bytes 3464 | tf_op jit(solution)/shard_map/ppermute | solution.py:22
  189.5 3.3 %collective-permute-start.20 = (f32[12,3,1,1,24]{4,0,3,2,1:T(8,128)S(1)}, f32[12,3,1,1,24]{4,0,3,2,1:T(8,128)S(1)}, u32[]{:S(2)}, u32[]{:S(2)}) collective-permute-start(f32[12,3,1,1,24]{4,0,3,2,1:T(8,128)S(1)} %pad_maximum_fusion.9), channel_id=1, source_target_pairs={{0,4},{4,8},{8,12},{12,0},{1,5},{5,9},{9,13},{13,1},{2,6},{6,10},{... | collective-permute-start | bytes 10376 | tf_op jit(solution)/shard_map/ppermute | solution.py:19
  189.5 3.3 %collective-permute-start.21 = (f32[12,3,1,1,24]{4,0,3,2,1:T(8,128)S(1)}, f32[12,3,1,1,24]{4,0,3,2,1:T(8,128)S(1)}, u32[]{:S(2)}, u32[]{:S(2)}) collective-permute-start(f32[12,3,1,1,24]{4,0,3,2,1:T(8,128)S(1)} %pad_maximum_fusion.9), channel_id=1, source_target_pairs={{4,0},{8,4},{12,8},{0,12},{5,1},{9,5},{13,9},{1,13},{6,2},{10,6},{... | collective-permute-start | bytes 10376 | tf_op jit(solution)/shard_map/ppermute | solution.py:22
  192.8 6.8 %collective-permute-start.22 = (f32[12,3,3,1,24]{4,0,3,2,1:T(8,128)S(1)}, f32[12,3,3,1,24]{4,0,3,2,1:T(8,128)S(1)}, u32[]{:S(2)}, u32[]{:S(2)}) collective-permute-start(f32[12,3,3,1,24]{4,0,3,2,1:T(8,128)S(1)} %pad_maximum_fusion.6), channel_id=1, source_target_pairs={{0,1},{1,2},{2,3},{3,0},{4,5},{5,6},{6,7},{7,4},{8,9},{9,10},{10,1... | collective-permute-start | bytes 31112 | tf_op jit(solution)/shard_map/ppermute | solution.py:19
  193.8 6.5 %collective-permute-start.23 = (f32[12,3,3,1,24]{4,0,3,2,1:T(8,128)S(1)}, f32[12,3,3,1,24]{4,0,3,2,1:T(8,128)S(1)}, u32[]{:S(2)}, u32[]{:S(2)}) collective-permute-start(f32[12,3,3,1,24]{4,0,3,2,1:T(8,128)S(1)} %pad_maximum_fusion.6), channel_id=1, source_target_pairs={{1,0},{2,1},{3,2},{0,3},{5,4},{6,5},{7,6},{4,7},{9,8},{10,9},{11,1... | collective-permute-start | bytes 31112 | tf_op jit(solution)/shard_map/ppermute | solution.py:22
where the time goes:
time: 208 us; the launch traced here: 207 us
  other arithmetic  124 us (60%)
  starting transfers between devices  32 us (15%)
  waiting for transfers between devices  27 us (13%)
  local copies, waits for them, and re-layouts  17.3 us (8%)
  loops' own time  6.39 us (3%)
    reduce_sum x54, other arithmetic, pair_force(): return jnp.sum(weight[None] * delta, axis=-1)  50.4 us
    div x54, other arithmetic, pair_force(): own_cells[5][:, :, None] * other_cells[5][:, None, :] * (clash + screened)  30.3 us
    reduce_sum x54, other arithmetic, pair_force(): dist_sq = jnp.sum(delta * delta, axis=0)  26 us
    ppermute x9, starting transfers between devices, extended_2(): lax.ppermute(lax.slice_in_dim(block, 0, width, axis=dim), axis, backward)  16 us
    ppermute x9, waiting for transfers between devices, extended_2(): lax.ppermute(lax.slice_in_dim(block, block.shape[dim] - width, None, axis...  15 us
    scatter-add x1, other arithmetic, per_device(): jax.ops.segment_sum(contrib.T, slots, num_segments=27 * owned)  11.6 us
    ppermute x9, starting transfers between devices, extended_2(): lax.ppermute(lax.slice_in_dim(block, block.shape[dim] - width, None, axis...  8.18 us
    ppermute x6, starting transfers between devices, shifted(): return lax.ppermute(block, axis, route)  7.88 us
  transfers between devices with their start and end apart: 24, of which 18 were waited for; matrix products, arithmetic and copies ran while one was open for 2% of the time, Pallas kernels for 0%

commit v1 on v0

v1 whole, which is shorter than its diff:
```python
import functools
import math

import jax
import jax.numpy as jnp
from jax import lax
from jax.experimental import pallas as pl
from jax.experimental.pallas import tpu as pltpu
from jax.sharding import PartitionSpec as P

min_reach = 0.15
clash_gain = 20.0
debye_length = 0.5
move_gain = 0.02
turn_gain = 0.01

LANES = 128
ROWS = 8
POSE_ROWS = 24
SEGMENT = 32
SCALE = 1.0 / (debye_length * math.log(2.0))
CHARGE_SCALE = math.sqrt(1.0 / (clash_gain * SCALE))
EMPTY = -20.0

f32 = jnp.float32
i32 = jnp.int32


def window(count):
    return min(count, 4)


def prep_kernel(sizes, coords, counts, local, charges, radii, slots, poses, mobility, noise, own, message):
    cells_x, cells_y, cells_z, owned = sizes
    lane = lax.broadcasted_iota(i32, (cells_z, LANES), 1)
    row = lax.broadcasted_iota(i32, (cells_z, LANES), 0)
    for x in range(cells_x):
        for y in range(cells_y):
            base = (x * cells_y + y) * cells_z * ROWS
            held = jnp.zeros((cells_z, LANES), i32)
            for z in range(cells_z):
                held = jnp.where(row == z, counts[(x * cells_y + y) * cells_z + z], held)
            filled = lane < held
            slot = slots[x, y].astype(f32)
            offset = jnp.floor((slot + 0.5) * (1.0 / owned))
            body = slot - offset * owned
            step_x = jnp.floor((offset + 0.5) * (1.0 / 9.0))
            step_y = jnp.floor((offset - 9.0 * step_x + 0.5) * (1.0 / 3.0))
            step_z = offset - 9.0 * step_x - 3.0 * step_y
            code = body + 32.0 * step_z + 128.0 * step_y + 512.0 * step_x
            rows = [
                local[0, x, y],
                local[1, x, y],
                local[2, x, y],
                jnp.where(filled, charges[x, y], 0.0),
                jnp.where(filled, radii[x, y], EMPTY / SCALE),
                code,
                held.astype(f32),
                jnp.zeros((cells_z, LANES), f32),
            ]
            for k, value in enumerate(rows):
                own[pl.ds(base + k, cells_z, stride=ROWS), :] = value
            face = (x * cells_y + y) * ROWS
            message[face : face + ROWS, :] = own[base : base + ROWS, :]
    at = cells_x * cells_y * ROWS
    message[at:, :] = jnp.zeros((POSE_ROWS, LANES), f32)
    message[at : at + 12, :owned] = poses[...]
    message[at + 12 : at + 14, :owned] = mobility[...]
    message[at + 14 : at + 20, :owned] = noise[...]
    message[at:, :] = pltpu.roll(message[at:, :], coords[2] * SEGMENT, axis=1)


def lookup(table_row, lane_at, chunk_at, chunks):
    value = None
    for chunk in range(chunks):
        row = jnp.broadcast_to(table_row(chunk), lane_at.shape)
        picked = jnp.take_along_axis(row, lane_at, axis=1)
        value = picked if value is None else jnp.where(chunk_at == chunk, picked, value)
    return value


def pair_terms(column, row, dist_floor):
    dx = column[0] - row[0]
    dy = column[1] - row[1]
    dz = column[2] - row[2]
    dist_sq = dx * dx + dy * dy + dz * dz
    inverse = lax.rsqrt(jnp.maximum(dist_sq, 1e-30))
    dist = dist_sq * inverse
    inv_reach = jnp.minimum(inverse, 1.0 / dist_floor)
    gap = (column[3] + row[3]) - dist
    cut = jnp.maximum(SCALE * SCALE - dist_sq, 0.0)
    screened = (column[4] * row[4]) * jnp.exp2(gap) * (cut * cut)
    weight = inv_reach * (jnp.maximum(gap, 0.0) + screened * ((inv_reach + math.log(2.0)) * inv_reach))
    return weight * dx, weight * dy, weight * dz


def pair_kernel(
    sizes, coords, own, halo_z, halo_y, halo_x, table, out,
    raw, pos, arms, lane_at, chunk_at, held, columns, row_force, column_force, moved, contrib,
):
    cells_x, cells_y, cells_z, count_x, count_y, count_z = sizes
    wide_x, wide_y, wide_z = window(count_x), window(count_y), window(count_z)
    chunks = wide_x * wide_y
    ext_y, ext_z = cells_y + 1, cells_z + 1
    cells = (cells_x + 1) * ext_y * ext_z
    padded = raw.shape[0] // ROWS

    def at(x, y, z):
        return (x * ext_y + y) * ext_z + z

    def put(cell, ref, index):
        raw[cell * ROWS : (cell + 1) * ROWS, :] = ref[index * ROWS : (index + 1) * ROWS, :]

    for x in range(cells_x + 1):
        for y in range(ext_y):
            for z in range(ext_z):
                if x == cells_x:
                    put(at(x, y, z), halo_x, y * ext_z + z)
                elif y == cells_y:
                    put(at(x, y, z), halo_y, x * ext_z + z)
                elif z == cells_z:
                    put(at(x, y, z), halo_z, x * cells_y + y)
                else:
                    put(at(x, y, z), own, (x * cells_y + y) * cells_z + z)
    for cell in range(cells, padded):
        raw[cell * ROWS : (cell + 1) * ROWS, :] = jnp.zeros((ROWS, LANES), f32)
    for cell in range(cells):
        held[cell] = jnp.max(raw[cell * ROWS + 6 : cell * ROWS + 7, :]).astype(i32)

    coord_x, coord_y, coord_z = coords[0], coords[1], coords[2]

    def place(group, carry):
        first = pl.multiple_of(group * 64, 64)
        load = lambda k: raw[pl.ds(first + k, 8, stride=ROWS), :]
        cell = group * 8 + lax.broadcasted_iota(i32, (8, LANES), 0)
        cell_x = sum((cell >= n * ext_y * ext_z).astype(i32) for n in range(1, cells_x + 1))
        rest = cell - cell_x * (ext_y * ext_z)
        cell_y = sum((rest >= n * ext_z).astype(i32) for n in range(1, cells_y + 1))
        cell_z = rest - cell_y * ext_z
        code = load(5).astype(i32)
        off_x = (code >> 9) - 1 + (cell_x >= cells_x).astype(i32)
        off_y = ((code >> 7) & 3) - 1 + (cell_y >= cells_y).astype(i32)
        off_z = ((code >> 5) & 3) - 1 + (cell_z >= cells_z).astype(i32)
        lanes = (((coord_z + off_z) & (wide_z - 1)) * SEGMENT) + (code & (SEGMENT - 1))
        near = (((off_x + coords[3]) & (wide_x - 1)) ^ coords[4]) * wide_y + (
            ((off_y + coords[5]) & (wide_y - 1)) ^ coords[6]
        )
        lane_at[pl.ds(pl.multiple_of(group * 8, 8), 8), :] = lanes
        chunk_at[pl.ds(pl.multiple_of(group * 8, 8), 8), :] = (
            (off_x + coord_x) & (wide_x - 1)
        ) * wide_y + ((off_y + coord_y) & (wide_y - 1))
        pose = [
            lookup(lambda n, k=k: table[n * POSE_ROWS + k : n * POSE_ROWS + k + 1, :], lanes, near, chunks)
            for k in range(12)
        ]
        local = [load(k) for k in range(3)]
        cell_at = (cell_x, cell_y, cell_z)
        extents = (cells_x, cells_y, cells_z)
        for k in range(3):
            arm = pose[3 * k] * local[0] + pose[3 * k + 1] * local[1] + pose[3 * k + 2] * local[2]
            arms[k, pl.ds(pl.multiple_of(group * 8, 8), 8), :] = arm
            box = float(extents[k] * (count_x, count_y, count_z)[k])
            corner = ((coord_x, coord_y, coord_z)[k] * extents[k]).astype(f32)
            middle = cell_at[k].astype(f32) + 0.5
            inside = arm + pose[9 + k] - corner - middle
            inside = inside - box * jnp.floor(inside * (1.0 / box) + 0.5)
            pos[pl.ds(first + k, 8, stride=ROWS), :] = (inside + middle) * SCALE
        radius = load(4) * SCALE
        pos[pl.ds(first + 3, 8, stride=ROWS), :] = radius
        pos[pl.ds(first + 4, 8, stride=ROWS), :] = load(3) * CHARGE_SCALE * jnp.exp2(-radius)
        return carry

    for k in range(5, ROWS):
        for group in range(padded // 8):
            pos[pl.ds(group * 64 + k, 8, stride=ROWS), :] = jnp.zeros((8, LANES), f32)
    lax.fori_loop(0, padded // 8, place, 0)
    for block in range(padded // 16):
        span = slice(block * LANES, (block + 1) * LANES)
        columns[span, :] = pos[span, :].T
        moved[span, :] = jnp.zeros((LANES, LANES), f32)
    row_force[...] = jnp.zeros(row_force.shape, f32)

    lane = lax.broadcasted_iota(i32, (8, LANES), 1)
    step_x, step_y, step_z = ext_y * ext_z, ext_z, 1
    groups = (
        (0, (0, step_x, step_y, step_z, step_x + step_y, step_x + step_z, step_y + step_z, step_x + step_y + step_z), 1),
        (step_x, (step_y, step_y + step_z), 4),
        (step_y, (step_z, step_x + step_z), 4),
        (step_z, (step_x, step_x + step_y), 4),
    )

    def visit(base, carry):
        x = base // (cells_y * cells_z)
        y = base // cells_z % cells_y
        cell = at(x, y, base % cells_z)
        for column_step, row_steps, together in groups:
            column_cell = cell + column_step
            block_at = (column_cell // 16) * LANES
            lane_base = (column_cell % 16) * ROWS
            tiles = (held[column_cell] + (8 * together - 1)) // (8 * together)

            def tile_pairs(tile, inner):
                ats, cols = [], []
                for n in range(together):
                    start = pl.multiple_of(block_at + (tile * together + n) * 8, 8)
                    packed = columns[pl.ds(start, 8), :]
                    ats.append(start)
                    cols.append(
                        [
                            jnp.take_along_axis(packed, jnp.full((8, LANES), lane_base + k, i32), axis=1)
                            for k in range(5)
                        ]
                    )
                sums = [[None] * 3 for _ in range(together)]
                for row_step in row_steps:
                    row_cell = cell + row_step
                    row = [
                        jnp.broadcast_to(pos[pl.ds(row_cell * ROWS + k, 1), :], (8, LANES)) for k in range(5)
                    ]
                    back = [None] * 3
                    for n in range(together):
                        parts = pair_terms(cols[n], row, min_reach * SCALE)
                        for k in range(3):
                            sums[n][k] = parts[k] if sums[n][k] is None else sums[n][k] + parts[k]
                            back[k] = parts[k] if back[k] is None else back[k] + parts[k]
                    if row_step != column_step:
                        span = pl.ds(pl.multiple_of(row_cell * ROWS, 8), 8)
                        for k in range(3):
                            row_force[k, span, :] = row_force[k, span, :] - back[k]
                for n in range(together):
                    span = pl.ds(ats[n], 8)
                    total = moved[span, :]
                    for k in range(3):
                        whole = jnp.sum(sums[n][k], axis=1, keepdims=True)
                        total = total + jnp.where(lane == lane_base + k, whole, 0.0)
                    moved[span, :] = total
                return inner

            lax.fori_loop(0, tiles, tile_pairs, 0)
        return carry

    lax.fori_loop(0, cells_x * cells_y * cells_z, visit, 0)

    for block in range(padded // 16):
        span = slice(block * LANES, (block + 1) * LANES)
        column_force[span, :] = moved[span, :].T

    def twist(group, carry):
        first = pl.multiple_of(group * 64, 64)
        span = pl.ds(pl.multiple_of(group * 8, 8), 8)
        force = []
        for k in range(3):
            total = column_force[pl.ds(first + k, 8, stride=ROWS), :]
            for n in range(8):
                total = total + row_force[k, pl.ds(first + n, 8, stride=ROWS), :]
            force.append(total * (clash_gain / SCALE))
        arm = [arms[k, span, :] for k in range(3)]
        rows = force + [
            arm[1] * force[2] - arm[2] * force[1],
            arm[2] * force[0] - arm[0] * force[2],
            arm[0] * force[1] - arm[1] * force[0],
        ]
        for k, value in enumerate(rows):
            contrib[pl.ds(first + k, 8, stride=ROWS), :] = value
        for k in (6, 7):
            contrib[pl.ds(first + k, 8, stride=ROWS), :] = jnp.zeros((8, LANES), f32)
        return carry

    lax.fori_loop(0, padded // 8, twist, 0)

    body = lax.broadcasted_iota(i32, (LANES, LANES), 0)

    def gather_sums(cell, total):
        value = contrib[pl.ds(pl.multiple_of(cell * ROWS, 8), 8), :]
        high = value.astype(jnp.bfloat16).astype(f32)
        low = value - high
        owner = jnp.broadcast_to(chunk_at[pl.ds(cell, 1), :], (8, LANES))
        member = jnp.broadcast_to(lane_at[pl.ds(cell, 1), :], (LANES, LANES)) == body
        pieces = []
        for chunk in range(chunks):
            mine = owner == chunk
            pieces.append(jnp.where(mine, high, 0.0))
            pieces.append(jnp.where(mine, low, 0.0))
        left = jnp.concatenate(pieces, axis=0).astype(jnp.bfloat16)
        right = jnp.where(member, 1.0, 0.0).astype(jnp.bfloat16)
        return total + lax.dot_general(left, right, (((1,), (1,)), ((), ())), preferred_element_type=f32)

    total = lax.fori_loop(0, cells, gather_sums, jnp.zeros((chunks * 16, LANES), f32))
    for chunk in range(chunks):
        out[chunk * 8 : chunk * 8 + 8, :] = total[chunk * 16 : chunk * 16 + 8] + total[chunk * 16 + 8 : chunk * 16 + 16]


def advance_rows(pose, force, torque, mobility, noise):
    centre = [pose[9 + k] + move_gain * mobility[0] * force[k] + noise[k] for k in range(3)]
    spin = [0.5 * (turn_gain * mobility[1] * torque[k] + noise[3 + k]) for k in range(3)]
    spin_sq = spin[0] * spin[0] + spin[1] * spin[1] + spin[2] * spin[2]
    factor = 2.0 / (1.0 + spin_sq)
    skew = [[None, -spin[2], spin[1]], [spin[2], None, -spin[0]], [-spin[1], spin[0], None]]
    rows = []
    for r in range(3):
        turn = []
        for c in range(3):
            inner = spin[r] * spin[c]
            turn.append(1.0 + factor * (inner - spin_sq) if r == c else factor * (skew[r][c] + inner))
        for c in range(3):
            rows.append(turn[0] * pose[c] + turn[1] * pose[3 + c] + turn[2] * pose[6 + c])
    return rows + centre


def move_kernel(sizes, coords, own, table, totals, stepped, positions, poses, fresh):
    cells_x, cells_y, cells_z, count_x, count_y, count_z, owned = sizes
    wide_x, wide_y, wide_z = window(count_x), window(count_y), window(count_z)
    chunks = wide_x * wide_y
    coord_x, coord_y, coord_z = coords[0], coords[1], coords[2]
    for x in range(wide_x):
        near_x = ((x - coord_x + coords[3]) & (wide_x - 1)) ^ coords[4]
        for y in range(wide_y):
            near_y = ((y - coord_y + coords[5]) & (wide_y - 1)) ^ coords[6]
            chunk = x * wide_y + y
            start = pl.multiple_of((near_x * wide_y + near_y) * POSE_ROWS, 8)
            poses[chunk * POSE_ROWS : (chunk + 1) * POSE_ROWS, :] = table[pl.ds(start, POSE_ROWS), :]
    for first in range(0, chunks, 8):
        many = min(8, chunks - first)
        row = [poses[pl.ds(first * POSE_ROWS + k, many, stride=POSE_ROWS), :] for k in range(20)]
        total = [totals[pl.ds(first * 8 + k, many, stride=8), :] for k in range(6)]
        new = advance_rows(row[:12], total[:3], total[3:], row[12:14], row[14:20])
        for k in range(12):
            fresh[pl.ds(first * 16 + k, many, stride=16), :] = new[k]
    mine = ((coord_x & (wide_x - 1)) * wide_y + (coord_y & (wide_y - 1))) * 16
    turned = pltpu.roll(
        fresh[pl.ds(pl.multiple_of(mine, 16), 16), :],
        LANES - (coord_z & (wide_z - 1)) * SEGMENT,
        axis=1,
    )
    stepped[...] = turned[:12, :owned]
    for first in range(0, cells_x * cells_y * cells_z, 8):
        load = lambda k: own[pl.ds(first * ROWS + k, 8, stride=ROWS), :]
        code = load(5).astype(i32)
        off_x = (code >> 9) - 1
        off_y = ((code >> 7) & 3) - 1
        off_z = ((code >> 5) & 3) - 1
        lanes = (((coord_z + off_z) & (wide_z - 1)) * SEGMENT) + (code & (SEGMENT - 1))
        chunk_at = ((off_x + coord_x) & (wide_x - 1)) * wide_y + ((off_y + coord_y) & (wide_y - 1))
        pose = [
            lookup(lambda n, k=k: fresh[n * 16 + k : n * 16 + k + 1, :], lanes, chunk_at, chunks) for k in range(12)
        ]
        local = [load(k) for k in range(3)]
        for k in range(3):
            arm = pose[3 * k] * local[0] + pose[3 * k + 1] * local[1] + pose[3 * k + 2] * local[2]
            positions[k, first : first + 8, :] = arm + pose[9 + k]


def from_offset(block, axis, distance):
    count = lax.axis_size(axis)
    return lax.ppermute(block, axis, [((i + distance) % count, i) for i in range(count)])


def from_partner(block, axis, mask):
    return lax.ppermute(block, axis, [(i ^ mask, i) for i in range(lax.axis_size(axis))])


def collect(face, poses, axis, merge):
    count = lax.axis_size(axis)
    rows = face.shape[0]
    if count == 2:
        got = from_partner(jnp.concatenate([face, poses]), axis, 1)
        return got[:rows], merge(poses, got[rows:])
    if count == 4:
        got = from_partner(jnp.concatenate([face, poses]), axis, 1)
        near, poses = got[:rows], merge(poses, got[rows:])
        got = from_partner(jnp.concatenate([near, poses]), axis, 2)
        even = lax.axis_index(axis) % 2 == 0
        return jnp.where(even, near, got[:rows]), merge(poses, got[rows:])
    got = from_offset(jnp.concatenate([face, poses]), axis, 1)
    all_poses = merge(poses, got[rows:])
    all_poses = merge(all_poses, from_offset(poses, axis, 2))
    return got[:rows], merge(all_poses, from_offset(poses, axis, -1))


def add_up(totals, axis, index):
    count = lax.axis_size(axis)
    if count <= 4:
        step = 1
        while step < count:
            totals = totals + from_partner(totals, axis, step)
            step *= 2
        return totals
    me = lax.axis_index(axis)
    owner = ((index - me + 1) & 3) - 1
    result = totals
    for distance in (-3, -2, -1, 1, 2):
        theirs = ((index - me - distance + 1) & 3) - 1
        result = result + jnp.where(theirs + distance == owner, from_offset(totals, axis, distance), 0.0)
    return result


def per_device(body_local, charges, radii, body_slot, cell_counts, poses, mobility, noise):
    cells_x, cells_y, cells_z, width = charges.shape
    owned = poses.shape[1]
    counts = tuple(lax.axis_size(axis) for axis in ("gx", "gy", "gz"))
    wide = tuple(window(count) for count in counts)
    chunks = wide[0] * wide[1]
    coord = [lax.axis_index(axis).astype(i32) for axis in ("gx", "gy", "gz")]
    turn = []
    for k in range(2):
        by_mask = coord[k] if counts[k] == 4 else jnp.zeros((), i32)
        turn += [by_mask, by_mask]
    coords = jnp.stack(coord + turn + [jnp.zeros((), i32)])
    own_cells = cells_x * cells_y * cells_z
    vmem = pl.BlockSpec(memory_space=pltpu.VMEM)
    smem = pl.BlockSpec(memory_space=pltpu.SMEM)

    own, message = pl.pallas_call(
        functools.partial(prep_kernel, (cells_x, cells_y, cells_z, owned)),
        out_shape=(
            jax.ShapeDtypeStruct((own_cells * ROWS, LANES), f32),
            jax.ShapeDtypeStruct((cells_x * cells_y * ROWS + POSE_ROWS, LANES), f32),
        ),
        in_specs=[smem, smem] + [vmem] * 7,
        out_specs=(vmem, vmem),
    )(
        jnp.stack([coord[0], coord[1], coord[2] & (wide[2] - 1)]),
        cell_counts.reshape(-1), body_local, charges, radii, body_slot, poses, mobility, noise,
    )

    def joined(first, second):
        return jnp.concatenate([first, second], axis=0)

    cell_rows = own.reshape(cells_x, cells_y, cells_z, ROWS, LANES)
    face_rows = cells_x * cells_y * ROWS
    halo_z, table = collect(message[:face_rows], message[face_rows:], "gz", jnp.add)
    high_z = halo_z.reshape(cells_x, cells_y, 1, ROWS, LANES)
    extended = jnp.concatenate([cell_rows, high_z], axis=2)
    halo_y, table = collect(extended[:, 0].reshape(-1, LANES), table, "gy", joined)
    high_y = halo_y.reshape(cells_x, 1, cells_z + 1, ROWS, LANES)
    face_x = jnp.concatenate([extended[0], high_y[0]], axis=0)
    halo_x, table = collect(face_x.reshape(-1, LANES), table, "gx", joined)

    sizes = (cells_x, cells_y, cells_z) + counts
    cells = (cells_x + 1) * (cells_y + 1) * (cells_z + 1)
    padded = -(-cells // 16) * 16
    totals = pl.pallas_call(
        functools.partial(pair_kernel, sizes),
        out_shape=jax.ShapeDtypeStruct((chunks * 8, LANES), f32),
        in_specs=[smem] + [vmem] * 5,
        out_specs=vmem,
        scratch_shapes=[
            pltpu.VMEM((padded * ROWS, LANES), f32),
            pltpu.VMEM((padded * ROWS, LANES), f32),
            pltpu.VMEM((3, padded, LANES), f32),
            pltpu.VMEM((padded, LANES), i32),
            pltpu.VMEM((padded, LANES), i32),
            pltpu.SMEM((padded,), i32),
            pltpu.VMEM((padded * ROWS, LANES), f32),
            pltpu.VMEM((3, padded * ROWS, LANES), f32),
            pltpu.VMEM((padded * ROWS, LANES), f32),
            pltpu.VMEM((padded * ROWS, LANES), f32),
            pltpu.VMEM((padded * ROWS, LANES), f32),
        ],
        compiler_params=pltpu.CompilerParams(vmem_limit_bytes=32 * 1024 * 1024),
    )(coords, own, halo_z, halo_y, halo_x, table)

    shaped = totals.reshape(wide[0], wide[1], 8, LANES)
    index_z = lax.broadcasted_iota(i32, (1, 1, 1, LANES), 3) // SEGMENT
    index_y = lax.broadcasted_iota(i32, (1, wide[1], 1, 1), 1)
    index_x = lax.broadcasted_iota(i32, (wide[0], 1, 1, 1), 0)
    shaped = add_up(shaped, "gy", index_y)
    shaped = add_up(shaped, "gx", index_x)
    shaped = add_up(shaped, "gz", index_z)

    stepped, positions = pl.pallas_call(
        functools.partial(move_kernel, sizes + (owned,)),
        out_shape=(
            jax.ShapeDtypeStruct((12, owned), f32),
            jax.ShapeDtypeStruct((3, own_cells, LANES), f32),
        ),
        in_specs=[smem] + [vmem] * 3,
        out_specs=(vmem, vmem),
        scratch_shapes=[
            pltpu.VMEM((chunks * POSE_ROWS, LANES), f32),
            pltpu.VMEM((chunks * 16, LANES), f32),
        ],
    )(coords, own, table, shaped.reshape(chunks * 8, LANES))
    return (stepped, positions.reshape(3, cells_x, cells_y, cells_z, width))


def solution(mesh):
    placed = (
        P(None, "gx", "gy", "gz", None),
        P("gx", "gy", "gz", None),
        P("gx", "gy", "gz", None),
        P("gx", "gy", "gz", None),
        P("gx", "gy", "gz"),
        P(None, ("gx", "gy", "gz")),
        P(None, ("gx", "gy", "gz")),
        P(None, ("gx", "gy", "gz")),
    )
    return jax.shard_map(
        per_device,
        mesh=mesh,
        in_specs=placed,
        out_specs=(P(None, ("gx", "gy", "gz")), P(None, "gx", "gy", "gz", None)),
        check_vma=False,
    )
```

time: 208 us -> 121 us (0.58)
  other arithmetic: 124 us -> 2.07 us
  Pallas kernels: 0 us -> 75.4 us
  local copies, waits for them, and re-layouts: 17.3 us -> 1.48 us
  starting transfers between devices: 32 us -> 18.2 us
  loops' own time: 6.39 us -> 0 us
  waiting for transfers between devices: 27 us -> 21.9 us
    reduce_sum x109 -> x0, other arithmetic: 76.4 us -> none  [the longest x54 50.4 us: pair_force(): return jnp.sum(weight[None] * delta, axis=-1)]
    pallas_call x0 -> x3, Pallas kernels: none -> 75.4 us  [the longest x1 72.1 us: per_device(): pl.pallas_call(functools.partial(pair_kernel, sizes), out_shape=jax.Shape...]
    div x54 -> x0, other arithmetic: 30.3 us -> none  [pair_force(): own_cells[5][:, :, None] * other_cells[5][:, None, :] * (clash + screened)]
    ppermute x24 -> x10, starting transfers between devices: 32 us -> 18.2 us  [from_partner(): lax.ppermute(block, axis, [(i ^ mask, i) for i in range(lax.axis_size(axi...]
    scatter-add x1 -> x0, other arithmetic: 11.6 us -> none  [per_device(): jax.ops.segment_sum(contrib.T, slots, num_segments=27 * owned)]
    gather x4 -> x0, local copies, waits for them, and re-layouts: 11.6 us -> none  [the longest x2 5.79 us: per_device(): jnp.take(near_poses.reshape(12, 27 * owned), slots, axis=1)]
    another operation x28 -> x0, loops' own time: 6.39 us -> none  [the longest x1 3.35 us: per_device(): lax.fori_loop(0, 27, visit, jnp.zeros((cells_x, 3, cells_y * cells_z, wid...]
    ppermute x24 -> x10, waiting for transfers between devices: 27 us -> 21.9 us  [from_partner(): lax.ppermute(block, axis, [(i ^ mask, i) for i in range(lax.axis_size(axi...]
  transfers between devices with their start and end apart: 24 -> 10, of which waited for: 18 -> 10; matrix products, arithmetic and copies ran while one was open for 2% -> 0% of each run, Pallas kernels for 0% -> 0%
where the time goes in v1:
time: 121 us; the launch traced here: 120 us
  Pallas kernels  75.4 us (62%)
  waiting for transfers between devices  21.9 us (18%)
  starting transfers between devices  18.2 us (15%)
  other arithmetic  2.07 us (2%)
  local copies, waits for them, and re-layouts  1.48 us (1%)
    pallas_call x1, Pallas kernels, per_device(): pl.pallas_call(functools.partial(pair_kernel, sizes), out_shape=jax.Shape...  72.1 us
    ppermute x10, waiting for transfers between devices, from_partner(): lax.ppermute(block, axis, [(i ^ mask, i) for i in range(lax.axis_size(axi...  21.9 us
    ppermute x10, starting transfers between devices, from_partner(): lax.ppermute(block, axis, [(i ^ mask, i) for i in range(lax.axis_size(axi...  18.2 us
  transfers between devices with their start and end apart: 10, of which 10 were waited for; matrix products, arithmetic and copies ran while one was open for 0% of the time, Pallas kernels for 0%

profile of v1, /device:TPU:0, one launch (start us, length us, event | category | flops | bytes accessed | tf_op | source)
XLA Modules:
  0.0 119.8 jit_solution(13897335478649414672)
XLA Ops:
  0.6 0.0 copy-start.3
  0.6 0.7 copy-done.3
  1.3 0.7 reshape.28.counts
  2.0 0.7 pad_add_fusion.coords
  2.7 1.5 %shard_map.95 = (f32[128,128]{1,0:T(8,128)}, f32[56,128]{1,0:T(8,128)}) custom-call(s32[3]{0:T(128)} %pad_add_fusion.coords, s32[16]{0:T(128)} %reshape.28.counts, f32[3,2,2,4,128]{4,3,2,1,0:T(4,128)} %local.1, f32[2,2,4,128]{3,2,1,0:T(4,128)} %charges.1, f32[2,2,4,128]{3,2,1,0:T(4,128)} %radii.1, s32[2,2,4,128]{3,2,1,0:T(4,128)} %slots.1, f32[12,24]{1,0:T(8,128)} %poses.1, ...), custom_call_target="tpu_custom_call" | custom-call | tf_op jit(solution)/shard_map/pallas_call | solution.py:413
  4.1 3.0 %collective-permute-start = (f32[56,128]{1,0:T(8,128)}, f32[56,128]{1,0:T(8,128)S(1)}, u32[]{:S(2)}, u32[]{:S(2)}) collective-permute-start(f32[56,128]{1,0:T(8,128)} %get-tuple-element.7), channel_id=1, source_target_pairs={{1,0},{0,1},{3,2},{2,3},{5,4},{4,5},{7,6},{6,7},{9,8},{8,9},{11,10... | collective-permute-start | bytes 86024 | tf_op jit(solution)/shard_map/ppermute | solution.py:359
  7.2 2.1 %collective-permute-done = f32[56,128]{1,0:T(8,128)S(1)} collective-permute-done((f32[56,128]{1,0:T(8,128)}, f32[56,128]{1,0:T(8,128)S(1)}, u32[]{:S(2)}, u32[]{:S(2)}) %collective-permute-start) | collective-permute-done | bytes 28704 | tf_op jit(solution)/shard_map/ppermute | solution.py:359
  9.2 0.7 slice_add_fusion.1
  10.0 3.1 %collective-permute-start.1 = (f32[56,128]{1,0:T(8,128)S(1)}, f32[56,128]{1,0:T(8,128)S(1)}, u32[]{:S(2)}, u32[]{:S(2)}) collective-permute-start(f32[56,128]{1,0:T(8,128)S(1)} %pad_maximum_fusion.5), channel_id=1, source_target_pairs={{2,0},{3,1},{0,2},{1,3},{6,4},{7,5},{4,6},{5,7},{10,8},{11,9},{8,1... | collective-permute-start | bytes 86024 | tf_op jit(solution)/shard_map/ppermute | solution.py:359
  13.1 0.0 copy-done.1
  13.1 1.8 %collective-permute-done.1 = f32[56,128]{1,0:T(8,128)S(1)} collective-permute-done((f32[56,128]{1,0:T(8,128)S(1)}, f32[56,128]{1,0:T(8,128)S(1)}, u32[]{:S(2)}, u32[]{:S(2)}) %collective-permute-start.1) | collective-permute-done | bytes 28704 | tf_op jit(solution)/shard_map/ppermute | solution.py:359
  14.9 0.1 collective-permute-start.2
  15.0 1.2 %collective-permute-done.2 = f32[104,128]{1,0:T(8,128)S(1)} collective-permute-done((f32[104,128]{1,0:T(8,128)S(1)}, f32[104,128]{1,0:T(8,128)S(1)}, u32[]{:S(2)}, u32[]{:S(2)}) %collective-permute-start.2) | collective-permute-done | bytes 53280 | tf_op jit(solution)/shard_map/ppermute | solution.py:359
  16.3 1.9 %collective-permute-start.3 = (f32[128,128]{1,0:T(8,128)S(1)}, f32[128,128]{1,0:T(8,128)S(1)}, u32[]{:S(2)}, u32[]{:S(2)}) collective-permute-start(f32[128,128]{1,0:T(8,128)S(1)} %pad_maximum_fusion.2), channel_id=1, source_target_pairs={{8,0},{12,4},{0,8},{4,12},{9,1},{13,5},{1,9},{5,13},{10,2},{14,6},... | collective-permute-start | bytes 196616 | tf_op jit(solution)/shard_map/ppermute | solution.py:359
  18.2 2.4 %collective-permute-done.3 = f32[128,128]{1,0:T(8,128)S(1)} collective-permute-done((f32[128,128]{1,0:T(8,128)S(1)}, f32[128,128]{1,0:T(8,128)S(1)}, u32[]{:S(2)}, u32[]{:S(2)}) %collective-permute-start.3) | collective-permute-done | bytes 65568 | tf_op jit(solution)/shard_map/ppermute | solution.py:359
  20.7 1.9 %collective-permute-start.4 = (f32[216,128]{1,0:T(8,128)S(1)}, f32[216,128]{1,0:T(8,128)S(1)}, u32[]{:S(2)}, u32[]{:S(2)}) collective-permute-start(f32[216,128]{1,0:T(8,128)S(1)} %pad_maximum_fusion), channel_id=1, source_target_pairs={{16,0},{0,16},{17,1},{1,17},{18,2},{2,18},{19,3},{3,19},{20,4},{4,... | collective-permute-start | bytes 331784 | tf_op jit(solution)/shard_map/ppermute | solution.py:359
  22.5 0.1 stack.25.coords
  22.6 2.8 %collective-permute-done.4 = f32[216,128]{1,0:T(8,128)S(1)} collective-permute-done((f32[216,128]{1,0:T(8,128)S(1)}, f32[216,128]{1,0:T(8,128)S(1)}, u32[]{:S(2)}, u32[]{:S(2)}) %collective-permute-start.4) | collective-permute-done | bytes 110624 | tf_op jit(solution)/shard_map/ppermute | solution.py:359
  25.5 72.1 %shard_map.96 = f32[64,128]{1,0:T(8,128)S(1)} custom-call(s32[8]{0:T(128)S(1)} %stack.25.coords, f32[128,128]{1,0:T(8,128)S(1)} %copy-done.1, f32[32,128]{1,0:T(8,128)S(1)} %slice_select_fusion.1.halo_z, f32[80,128]{1,0:T(8,128)S(1)} %slice_select_fusion.halo_y, f32[120,128]{1,0:T(8,128)S(1)} %slice.71.halo_x, f32[192,128]{1,0:T(8,128)S(1)} %pad_maximum_fusion.1.table), custom_call_target="tpu_custom_call" | custom-call | tf_op jit(solution)/shard_map/pallas_call | solution.py:442
  97.6 0.0 copy-done
  97.6 0.1 collective-permute-start.5
  97.7 1.2 collective-permute-done.5
  98.9 1.3 %collective-permute-start.6 = (f32[2,4,8,128]{3,2,1,0:T(8,128)S(1)}, f32[2,4,8,128]{3,2,1,0:T(8,128)S(1)}, u32[]{:S(2)}, u32[]{:S(2)}) collective-permute-start(f32[2,4,8,128]{3,2,1,0:T(8,128)S(1)} %add.32), channel_id=1, source_target_pairs={{8,0},{12,4},{0,8},{4,12},{9,1},{13,5},{1,9},{5,13},{10,2},{14,6},... | collective-permute-start | bytes 98312 | tf_op jit(solution)/shard_map/ppermute | solution.py:359
  100.2 2.6 %collective-permute-done.6 = f32[2,4,8,128]{3,2,1,0:T(8,128)S(1)} collective-permute-done((f32[2,4,8,128]{3,2,1,0:T(8,128)S(1)}, f32[2,4,8,128]{3,2,1,0:T(8,128)S(1)}, u32[]{:S(2)}, u32[]{:S(2)}) %collective-permute-start.6) | collective-permute-done | bytes 32800 | tf_op jit(solution)/shard_map/ppermute | solution.py:359
  102.8 0.0 collective-permute-start.7
  102.8 3.9 %collective-permute-done.7 = f32[2,4,8,128]{3,2,1,0:T(8,128)S(1)} collective-permute-done((f32[2,4,8,128]{3,2,1,0:T(8,128)S(1)}, f32[2,4,8,128]{3,2,1,0:T(8,128)S(1)}, u32[]{:S(2)}, u32[]{:S(2)}) %collective-permute-start.7) | collective-permute-done | bytes 32800 | tf_op jit(solution)/shard_map/ppermute | solution.py:359
  106.7 3.8 %collective-permute-start.8 = (f32[2,4,8,128]{3,2,1,0:T(8,128)S(1)}, f32[2,4,8,128]{3,2,1,0:T(8,128)S(1)}, u32[]{:S(2)}, u32[]{:S(2)}) collective-permute-start(f32[2,4,8,128]{3,2,1,0:T(8,128)S(1)} %add.34), channel_id=1, source_target_pairs={{1,0},{0,1},{3,2},{2,3},{5,4},{4,5},{7,6},{6,7},{9,8},{8,9},{11,10... | collective-permute-start | bytes 98312 | tf_op jit(solution)/shard_map/ppermute | solution.py:359
  110.5 1.9 %collective-permute-done.8 = f32[2,4,8,128]{3,2,1,0:T(8,128)S(1)} collective-permute-done((f32[2,4,8,128]{3,2,1,0:T(8,128)S(1)}, f32[2,4,8,128]{3,2,1,0:T(8,128)S(1)}, u32[]{:S(2)}, u32[]{:S(2)}) %collective-permute-start.8) | collective-permute-done | bytes 32800 | tf_op jit(solution)/shard_map/ppermute | solution.py:359
  112.4 3.0 %collective-permute-start.9 = (f32[2,4,8,128]{3,2,1,0:T(8,128)S(1)}, f32[2,4,8,128]{3,2,1,0:T(8,128)S(1)}, u32[]{:S(2)}, u32[]{:S(2)}) collective-permute-start(f32[2,4,8,128]{3,2,1,0:T(8,128)S(1)} %add.35), channel_id=1, source_target_pairs={{2,0},{3,1},{0,2},{1,3},{6,4},{7,5},{4,6},{5,7},{10,8},{11,9},{8,1... | collective-permute-start | bytes 98312 | tf_op jit(solution)/shard_map/ppermute | solution.py:359
  115.4 1.9 %collective-permute-done.9 = f32[2,4,8,128]{3,2,1,0:T(8,128)S(1)} collective-permute-done((f32[2,4,8,128]{3,2,1,0:T(8,128)S(1)}, f32[2,4,8,128]{3,2,1,0:T(8,128)S(1)}, u32[]{:S(2)}, u32[]{:S(2)}) %collective-permute-start.9) | collective-permute-done | bytes 32800 | tf_op jit(solution)/shard_map/ppermute | solution.py:359
  117.3 0.6 add.36
  117.9 1.8 %shard_map.97 = (f32[12,24]{1,0:T(8,128)}, f32[3,16,128]{2,1,0:T(8,128)}) custom-call(s32[8]{0:T(128)} %copy-done.2, f32[128,128]{1,0:T(8,128)} %get-tuple-element.6.own, f32[192,128]{1,0:T(8,128)} %copy-done, f32[64,128]{1,0:T(8,128)} %bitcast.21), custom_call_target="tpu_custom_call" | custom-call | tf_op jit(solution)/shard_map/pallas_call | solution.py:471
  (29 shorter events, 0.1 us)
Async XLA Ops:
  0.6 0.7 copy-start.3
  4.1 8.9 %copy-start.1 = (f32[128,128]{1,0:T(8,128)S(1)}, f32[128,128]{1,0:T(8,128)}, u32[]{:S(2)}) copy-start(f32[128,128]{1,0:T(8,128)} %get-tuple-element.6.own) | copy-start | bytes 196612
  4.1 5.1 %collective-permute-start = (f32[56,128]{1,0:T(8,128)}, f32[56,128]{1,0:T(8,128)S(1)}, u32[]{:S(2)}, u32[]{:S(2)}) collective-permute-start(f32[56,128]{1,0:T(8,128)} %get-tuple-element.7), channel_id=1, source_target_pairs={{1,0},{0,1},{3,2},{2,3},{5,4},{4,5},{7,6},{6,7},{9,8},{8,9},{11,10... | collective-permute-start | bytes 86024 | tf_op jit(solution)/shard_map/ppermute | solution.py:359
  10.0 5.0 %collective-permute-start.1 = (f32[56,128]{1,0:T(8,128)S(1)}, f32[56,128]{1,0:T(8,128)S(1)}, u32[]{:S(2)}, u32[]{:S(2)}) collective-permute-start(f32[56,128]{1,0:T(8,128)S(1)} %pad_maximum_fusion.5), channel_id=1, source_target_pairs={{2,0},{3,1},{0,2},{1,3},{6,4},{7,5},{4,6},{5,7},{10,8},{11,9},{8,1... | collective-permute-start | bytes 86024 | tf_op jit(solution)/shard_map/ppermute | solution.py:359
  14.9 1.3 %collective-permute-start.2 = (f32[104,128]{1,0:T(8,128)S(1)}, f32[104,128]{1,0:T(8,128)S(1)}, u32[]{:S(2)}, u32[]{:S(2)}) collective-permute-start(f32[104,128]{1,0:T(8,128)S(1)} %pad_maximum_fusion.4), channel_id=1, source_target_pairs={{4,0},{0,4},{12,8},{8,12},{5,1},{1,5},{13,9},{9,13},{6,2},{2,6},{1... | collective-permute-start | bytes 159752 | tf_op jit(solution)/shard_map/ppermute | solution.py:359
  16.3 4.3 %collective-permute-start.3 = (f32[128,128]{1,0:T(8,128)S(1)}, f32[128,128]{1,0:T(8,128)S(1)}, u32[]{:S(2)}, u32[]{:S(2)}) collective-permute-start(f32[128,128]{1,0:T(8,128)S(1)} %pad_maximum_fusion.2), channel_id=1, source_target_pairs={{8,0},{12,4},{0,8},{4,12},{9,1},{13,5},{1,9},{5,13},{10,2},{14,6},... | collective-permute-start | bytes 196616 | tf_op jit(solution)/shard_map/ppermute | solution.py:359
  20.7 4.8 %collective-permute-start.4 = (f32[216,128]{1,0:T(8,128)S(1)}, f32[216,128]{1,0:T(8,128)S(1)}, u32[]{:S(2)}, u32[]{:S(2)}) collective-permute-start(f32[216,128]{1,0:T(8,128)S(1)} %pad_maximum_fusion), channel_id=1, source_target_pairs={{16,0},{0,16},{17,1},{1,17},{18,2},{2,18},{19,3},{3,19},{20,4},{4,... | collective-permute-start | bytes 331784 | tf_op jit(solution)/shard_map/ppermute | solution.py:359
  22.6 2.9 %copy-start.2 = (s32[8]{0:T(128)}, s32[8]{0:T(128)S(1)}, u32[]{:S(2)}) copy-start(s32[8]{0:T(128)S(1)} %stack.25.coords) | copy-start | bytes 100
  25.5 72.1 %copy-start = (f32[192,128]{1,0:T(8,128)}, f32[192,128]{1,0:T(8,128)S(1)}, u32[]{:S(2)}) copy-start(f32[192,128]{1,0:T(8,128)S(1)} %pad_maximum_fusion.1.table) | copy-start | bytes 294916
  97.6 1.3 %collective-permute-start.5 = (f32[2,4,8,128]{3,2,1,0:T(8,128)S(1)}, f32[2,4,8,128]{3,2,1,0:T(8,128)S(1)}, u32[]{:S(2)}, u32[]{:S(2)}) collective-permute-start(f32[2,4,8,128]{3,2,1,0:T(8,128)S(1)} %bitcast.17), channel_id=1, source_target_pairs={{4,0},{0,4},{12,8},{8,12},{5,1},{1,5},{13,9},{9,13},{6,2},{2,6},{1... | collective-permute-start | bytes 98312 | tf_op jit(solution)/shard_map/ppermute | solution.py:359
  98.9 3.9 %collective-permute-start.6 = (f32[2,4,8,128]{3,2,1,0:T(8,128)S(1)}, f32[2,4,8,128]{3,2,1,0:T(8,128)S(1)}, u32[]{:S(2)}, u32[]{:S(2)}) collective-permute-start(f32[2,4,8,128]{3,2,1,0:T(8,128)S(1)} %add.32), channel_id=1, source_target_pairs={{8,0},{12,4},{0,8},{4,12},{9,1},{13,5},{1,9},{5,13},{10,2},{14,6},... | collective-permute-start | bytes 98312 | tf_op jit(solution)/shard_map/ppermute | solution.py:359
  102.8 3.9 %collective-permute-start.7 = (f32[2,4,8,128]{3,2,1,0:T(8,128)S(1)}, f32[2,4,8,128]{3,2,1,0:T(8,128)S(1)}, u32[]{:S(2)}, u32[]{:S(2)}) collective-permute-start(f32[2,4,8,128]{3,2,1,0:T(8,128)S(1)} %add.33), channel_id=1, source_target_pairs={{16,0},{0,16},{17,1},{1,17},{18,2},{2,18},{19,3},{3,19},{20,4},{4,... | collective-permute-start | bytes 98312 | tf_op jit(solution)/shard_map/ppermute | solution.py:359
  106.7 5.7 %collective-permute-start.8 = (f32[2,4,8,128]{3,2,1,0:T(8,128)S(1)}, f32[2,4,8,128]{3,2,1,0:T(8,128)S(1)}, u32[]{:S(2)}, u32[]{:S(2)}) collective-permute-start(f32[2,4,8,128]{3,2,1,0:T(8,128)S(1)} %add.34), channel_id=1, source_target_pairs={{1,0},{0,1},{3,2},{2,3},{5,4},{4,5},{7,6},{6,7},{9,8},{8,9},{11,10... | collective-permute-start | bytes 98312 | tf_op jit(solution)/shard_map/ppermute | solution.py:359
  112.4 4.9 %collective-permute-start.9 = (f32[2,4,8,128]{3,2,1,0:T(8,128)S(1)}, f32[2,4,8,128]{3,2,1,0:T(8,128)S(1)}, u32[]{:S(2)}, u32[]{:S(2)}) collective-permute-start(f32[2,4,8,128]{3,2,1,0:T(8,128)S(1)} %add.35), channel_id=1, source_target_pairs={{2,0},{3,1},{0,2},{1,3},{6,4},{7,5},{4,6},{5,7},{10,8},{11,9},{8,1... | collective-permute-start | bytes 98312 | tf_op jit(solution)/shard_map/ppermute | solution.py:359

commit v2 on v1

--- a/solution.py
+++ b/solution.py
@@ -24,6 +24,9 @@
 
 f32 = jnp.float32
 i32 = jnp.int32
+
+TG0, TG1 = 2, 4
+SP, FO, GA = 4, 4, 8
 
 
 def window(count):
@@ -96,7 +99,7 @@
 
 def pair_kernel(
     sizes, coords, own, halo_z, halo_y, halo_x, table, out,
-    raw, pos, arms, lane_at, chunk_at, held, columns, row_force, column_force, moved, contrib,
+    raw, pos, arms, lane_at, chunk_at, held, order, wide, row_force, column_force, contrib,
 ):
     cells_x, cells_y, cells_z, count_x, count_y, count_z = sizes
     wide_x, wide_y, wide_z = window(count_x), window(count_y), window(count_z)
@@ -174,86 +177,121 @@
         for group in range(padded // 8):
             pos[pl.ds(group * 64 + k, 8, stride=ROWS), :] = jnp.zeros((8, LANES), f32)
     lax.fori_loop(0, padded // 8, place, 0)
-    for block in range(padded // 16):
-        span = slice(block * LANES, (block + 1) * LANES)
-        columns[span, :] = pos[span, :].T
-        moved[span, :] = jnp.zeros((LANES, LANES), f32)
     row_force[...] = jnp.zeros(row_force.shape, f32)
-
-    lane = lax.broadcasted_iota(i32, (8, LANES), 1)
+    listed = [
+        at(x, y, z)
+        for x in range(cells_x + 1)
+        for y in range(ext_y)
+        for z in range(ext_z)
+        if (x == cells_x) + (y == cells_y) + (z == cells_z) < 2
+    ]
+    for n, cell in enumerate(listed):
+        order[n] = cell
+    kind = lax.broadcasted_iota(i32, (32, 5 * LANES), 1) // LANES
+    part = lax.broadcasted_iota(i32, (32, 5 * LANES), 0)
+    picker = jnp.where((part % 8 == kind) & (part < 24), 1.0, 0.0).astype(jnp.bfloat16)
+
+    def spread(step, carry):
+        for n in range(SP):
+            cell = order[step * SP + n]
+            value = pos[pl.ds(pl.multiple_of(cell * ROWS, 8), 8), :]
+            high = value.astype(jnp.bfloat16).astype(f32)
+            rest = value - high
+            middle = rest.astype(jnp.bfloat16).astype(f32)
+            low = rest - middle
+            parts = jnp.concatenate([high, middle, low, jnp.zeros_like(low)], axis=0).astype(jnp.bfloat16)
+            out_wide = lax.dot_general(parts, picker, (((0,), (0,)), ((), ())), preferred_element_type=f32)
+            for k in range(5):
+                wide[cell, k, :, :] = out_wide[:, k * LANES : (k + 1) * LANES]
+        return carry
+
+    assert len(listed) % SP == 0 and len(listed) % FO == 0
+    lax.fori_loop(0, len(listed) // SP, spread, 0)
+
     step_x, step_y, step_z = ext_y * ext_z, ext_z, 1
     groups = (
-        (0, (0, step_x, step_y, step_z, step_x + step_y, step_x + step_z, step_y + step_z, step_x + step_y + step_z), 1),
-        (step_x, (step_y, step_y + step_z), 4),
-        (step_y, (step_z, step_x + step_z), 4),
-        (step_z, (step_x, step_x + step_y), 4),
+        (0, (0, step_x, step_y, step_z, step_x + step_y, step_x + step_z, step_y + step_z, step_x + step_y + step_z), TG0),
+        (step_x, (step_y, step_y + step_z), TG1),
+        (step_y, (step_z, step_x + step_z), TG1),
+        (step_z, (step_x, step_x + step_y), TG1),
     )
 
-    def visit(base, carry):
+    def visit(group, base, carry):
         x = base // (cells_y * cells_z)
         y = base // cells_z % cells_y
-        cell = at(x, y, base % cells_z)
-        for column_step, row_steps, together in groups:
-            column_cell = cell + column_step
-            block_at = (column_cell // 16) * LANES
-            lane_base = (column_cell % 16) * ROWS
-            tiles = (held[column_cell] + (8 * together - 1)) // (8 * together)
-
-            def tile_pairs(tile, inner):
-                ats, cols = [], []
+        z = base % cells_z
+        cell = at(x, y, z)
+        column_step, row_steps, together = groups[group]
+        column_cell = cell + column_step
+        tiles = (held[column_cell] + (8 * together - 1)) // (8 * together)
+        if group:
+            fresh_cell = ((x, y, z)[group - 1] == (cells_x, cells_y, cells_z)[group - 1] - 1)
+
+        def tile_pairs(tile, inner):
+            spans, cols = [], []
+            for n in range(together):
+                span = pl.ds(pl.multiple_of((tile * together + n) * 8, 8), 8)
+                spans.append(span)
+                cols.append([wide[column_cell, k, span, :] for k in range(5)])
+            sums = [[None] * 3 for _ in range(together)]
+            for row_step in row_steps:
+                row_cell = cell + row_step
+                row = [
+                    jnp.broadcast_to(pos[pl.ds(row_cell * ROWS + k, 1), :], (8, LANES)) for k in range(5)
+                ]
+                back = [None] * 3
                 for n in range(together):
-                    start = pl.multiple_of(block_at + (tile * together + n) * 8, 8)
-                    packed = columns[pl.ds(start, 8), :]
-                    ats.append(start)
-                    cols.append(
-                        [
-                            jnp.take_along_axis(packed, jnp.full((8, LANES), lane_base + k, i32), axis=1)
-                            for k in range(5)
-                        ]
-                    )
-                sums = [[None] * 3 for _ in range(together)]
-                for row_step in row_steps:
-                    row_cell = cell + row_step
-                    row = [
-                        jnp.broadcast_to(pos[pl.ds(row_cell * ROWS + k, 1), :], (8, LANES)) for k in range(5)
-                    ]
-                    back = [None] * 3
-                    for n in range(together):
-                        parts = pair_terms(cols[n], row, min_reach * SCALE)
-                        for k in range(3):
-                            sums[n][k] = parts[k] if sums[n][k] is None else sums[n][k] + parts[k]
-                            back[k] = parts[k] if back[k] is None else back[k] + parts[k]
-                    if row_step != column_step:
-                        span = pl.ds(pl.multiple_of(row_cell * ROWS, 8), 8)
-                        for k in range(3):
-                            row_force[k, span, :] = row_force[k, span, :] - back[k]
-                for n in range(together):
-                    span = pl.ds(ats[n], 8)
-                    total = moved[span, :]
+                    parts = pair_terms(cols[n], row, min_reach * SCALE)
                     for k in range(3):
-                        whole = jnp.sum(sums[n][k], axis=1, keepdims=True)
-                        total = total + jnp.where(lane == lane_base + k, whole, 0.0)
-                    moved[span, :] = total
-                return inner
-
-            lax.fori_loop(0, tiles, tile_pairs, 0)
+                        sums[n][k] = parts[k] if sums[n][k] is None else sums[n][k] + parts[k]
+                        back[k] = parts[k] if back[k] is None else back[k] + parts[k]
+                if row_step != column_step:
+                    span = pl.ds(pl.multiple_of(row_cell * ROWS, 8), 8)
+                    for k in range(3):
+                        row_force[k, span, :] = row_force[k, span, :] - back[k]
+            for n in range(together):
+                for k in range(3):
+                    total = sums[n][k]
+                    if group:
+                        total = total + jnp.where(fresh_cell, 0.0, column_force[column_cell, k, spans[n], :])
+                    column_force[column_cell, k, spans[n], :] = total
+            return inner
+
+        lax.fori_loop(0, tiles, tile_pairs, 0)
         return carry
 
-    lax.fori_loop(0, cells_x * cells_y * cells_z, visit, 0)
-
-    for block in range(padded // 16):
-        span = slice(block * LANES, (block + 1) * LANES)
-        column_force[span, :] = moved[span, :].T
+    for group in range(len(groups)):
+        lax.fori_loop(0, cells_x * cells_y * cells_z, functools.partial(visit, group), 0)
+
+    ones = jnp.where(lax.broadcasted_iota(i32, (16, 2 * LANES), 0) == 0, 1.0, 0.0).astype(jnp.bfloat16)
+
+    def fold(step, carry):
+        lines = []
+        for n in range(FO):
+            cell = order[step * FO + n]
+            value = column_force[cell].reshape(3 * LANES, LANES)
+            high = value.astype(jnp.bfloat16)
+            low = (value - high.astype(f32)).astype(jnp.bfloat16)
+            both = jnp.concatenate([high, low], axis=1)
+            lines.append(lax.dot_general(ones, both, (((1,), (1,)), ((), ())), preferred_element_type=f32))
+        for n in range(FO):
+            span = pl.ds(pl.multiple_of(order[step * FO + n] * ROWS, 8), 8)
+            for k in range(3):
+                row_force[k, span, :] += lines[n][:8, k * LANES : (k + 1) * LANES]
+        return carry
+
+    lax.fori_loop(0, len(listed) // FO, fold, 0)
 
     def twist(group, carry):
         first = pl.multiple_of(group * 64, 64)
         span = pl.ds(pl.multiple_of(group * 8, 8), 8)
         force = []
+        filled = lax.broadcasted_iota(i32, (8, LANES), 1).astype(f32) < raw[pl.ds(first + 6, 8, stride=ROWS), :]
         for k in range(3):
-            total = column_force[pl.ds(first + k, 8, stride=ROWS), :]
-            for n in range(8):
+            total = row_force[k, pl.ds(first, 8, stride=ROWS), :]
+            for n in range(1, 8):
                 total = total + row_force[k, pl.ds(first + n, 8, stride=ROWS), :]
-            force.append(total * (clash_gain / SCALE))
+            force.append(jnp.where(filled, total * (clash_gain / SCALE), 0.0))
         arm = [arms[k, span, :] for k in range(3)]
         rows = force + [
             arm[1] * force[2] - arm[2] * force[1],
@@ -270,22 +308,27 @@
 
     body = lax.broadcasted_iota(i32, (LANES, LANES), 0)
 
-    def gather_sums(cell, total):
-        value = contrib[pl.ds(pl.multiple_of(cell * ROWS, 8), 8), :]
-        high = value.astype(jnp.bfloat16).astype(f32)
-        low = value - high
-        owner = jnp.broadcast_to(chunk_at[pl.ds(cell, 1), :], (8, LANES))
-        member = jnp.broadcast_to(lane_at[pl.ds(cell, 1), :], (LANES, LANES)) == body
-        pieces = []
-        for chunk in range(chunks):
-            mine = owner == chunk
-            pieces.append(jnp.where(mine, high, 0.0))
-            pieces.append(jnp.where(mine, low, 0.0))
-        left = jnp.concatenate(pieces, axis=0).astype(jnp.bfloat16)
-        right = jnp.where(member, 1.0, 0.0).astype(jnp.bfloat16)
+    def gather_sums(step, total):
+        lefts, rights = [], []
+        for n in range(GA):
+            cell = step * GA + n
+            value = contrib[pl.ds(pl.multiple_of(cell * ROWS, 8), 8), :]
+            high = value.astype(jnp.bfloat16).astype(f32)
+            low = value - high
+            owner = jnp.broadcast_to(chunk_at[pl.ds(cell, 1), :], (8, LANES))
+            member = jnp.broadcast_to(lane_at[pl.ds(cell, 1), :], (LANES, LANES)) == body
+            pieces = []
+            for chunk in range(chunks):
+                mine = owner == chunk
+                pieces.append(jnp.where(mine, high, 0.0))
+                pieces.append(jnp.where(mine, low, 0.0))
+            lefts.append(jnp.concatenate(pieces, axis=0).astype(jnp.bfloat16))
+            rights.append(jnp.where(member, 1.0, 0.0).astype(jnp.bfloat16))
+        left = jnp.concatenate(lefts, axis=1)
+        right = jnp.concatenate(rights, axis=1)
         return total + lax.dot_general(left, right, (((1,), (1,)), ((), ())), preferred_element_type=f32)
 
-    total = lax.fori_loop(0, cells, gather_sums, jnp.zeros((chunks * 16, LANES), f32))
+    total = lax.fori_loop(0, padded // GA, gather_sums, jnp.zeros((chunks * 16, LANES), f32))
     for chunk in range(chunks):
         out[chunk * 8 : chunk * 8 + 8, :] = total[chunk * 16 : chunk * 16 + 8] + total[chunk * 16 + 8 : chunk * 16 + 16]
 
@@ -350,6 +393,35 @@
             positions[k, first : first + 8, :] = arm + pose[9 + k]
 
 
+def pair_sums(sizes, coords, own, halo_z, halo_y, halo_x, table):
+    cells_x, cells_y, cells_z = sizes[:3]
+    chunks = window(sizes[3]) * window(sizes[4])
+    vmem = pl.BlockSpec(memory_space=pltpu.VMEM)
+    smem = pl.BlockSpec(memory_space=pltpu.SMEM)
+    cells = (cells_x + 1) * (cells_y + 1) * (cells_z + 1)
+    padded = -(-cells // 16) * 16
+    return pl.pallas_call(
+        functools.partial(pair_kernel, sizes),
+        out_shape=jax.ShapeDtypeStruct((chunks * 8, LANES), f32),
+        in_specs=[smem] + [vmem] * 5,
+        out_specs=vmem,
+        scratch_shapes=[
+            pltpu.VMEM((padded * ROWS, LANES), f32),
+            pltpu.VMEM((padded * ROWS, LANES), f32),
+            pltpu.VMEM((3, padded, LANES), f32),
+            pltpu.VMEM((padded, LANES), i32),
+            pltpu.VMEM((padded, LANES), i32),
+            pltpu.SMEM((padded,), i32),
+            pltpu.SMEM((padded,), i32),
+            pltpu.VMEM((cells, 5, LANES, LANES), f32),
+            pltpu.VMEM((3, padded * ROWS, LANES), f32),
+            pltpu.VMEM((cells, 3, LANES, LANES), f32),
+            pltpu.VMEM((padded * ROWS, LANES), f32),
+        ],
+        compiler_params=pltpu.CompilerParams(vmem_limit_bytes=48 * 1024 * 1024),
+    )(coords, own, halo_z, halo_y, halo_x, table)
+
+
 def from_offset(block, axis, distance):
     count = lax.axis_size(axis)
     return lax.ppermute(block, axis, [((i + distance) % count, i) for i in range(count)])
@@ -437,28 +509,7 @@
     halo_x, table = collect(face_x.reshape(-1, LANES), table, "gx", joined)
 
     sizes = (cells_x, cells_y, cells_z) + counts
-    cells = (cells_x + 1) * (cells_y + 1) * (cells_z + 1)
-    padded = -(-cells // 16) * 16
-    totals = pl.pallas_call(
-        functools.partial(pair_kernel, sizes),
-        out_shape=jax.ShapeDtypeStruct((chunks * 8, LANES), f32),
-        in_specs=[smem] + [vmem] * 5,
-        out_specs=vmem,
-        scratch_shapes=[
-            pltpu.VMEM((padded * ROWS, LANES), f32),
-            pltpu.VMEM((padded * ROWS, LANES), f32),
-            pltpu.VMEM((3, padded, LANES), f32),
-            pltpu.VMEM((padded, LANES), i32),
-            pltpu.VMEM((padded, LANES), i32),
-            pltpu.SMEM((padded,), i32),
-            pltpu.VMEM((padded * ROWS, LANES), f32),
-            pltpu.VMEM((3, padded * ROWS, LANES), f32),
-            pltpu.VMEM((padded * ROWS, LANES), f32),
-            pltpu.VMEM((padded * ROWS, LANES), f32),
-            pltpu.VMEM((padded * ROWS, LANES), f32),
-        ],
-        compiler_params=pltpu.CompilerParams(vmem_limit_bytes=32 * 1024 * 1024),
-    )(coords, own, halo_z, halo_y, halo_x, table)
+    totals = pair_sums(sizes, coords, own, halo_z, halo_y, halo_x, table)
 
     shaped = totals.reshape(wide[0], wide[1], 8, LANES)
     index_z = lax.broadcasted_iota(i32, (1, 1, 1, LANES), 3) // SEGMENT

time: 121 us -> 73.5 us (0.61)
  Pallas kernels: 75.4 us -> 29.6 us
    pallas_call x1, Pallas kernels: 72.1 us -> 26.3 us  [pair_sums(): pl.pallas_call(functools.partial(pair_kernel, sizes), out_shape=jax.Shape...]
where the time goes in v2:
time: 73.5 us; the launch traced here: 72.9 us
  Pallas kernels  29.6 us (40%)
  waiting for transfers between devices  21.9 us (30%)
  starting transfers between devices  17.1 us (23%)
  other arithmetic  2.07 us (3%)
  local copies, waits for them, and re-layouts  1.48 us (2%)
  between operations  0.79 us (1%)
    pallas_call x1, Pallas kernels, pair_sums(): pl.pallas_call(functools.partial(pair_kernel, sizes), out_shape=jax.Shape...  26.3 us
    ppermute x10, waiting for transfers between devices, from_partner(): lax.ppermute(block, axis, [(i ^ mask, i) for i in range(lax.axis_size(axi...  21.9 us
    ppermute x10, starting transfers between devices, from_partner(): lax.ppermute(block, axis, [(i ^ mask, i) for i in range(lax.axis_size(axi...  17.1 us
    pallas_call x1, Pallas kernels, per_device(): pl.pallas_call(functools.partial(move_kernel, sizes + (owned,)), out_shap...  1.84 us
    pallas_call x1, Pallas kernels, per_device(): pl.pallas_call(functools.partial(prep_kernel, (cells_x, cells_y, cells_z,...  1.49 us
  transfers between devices with their start and end apart: 10, of which 10 were waited for; matrix products, arithmetic and copies ran while one was open for 0% of the time, Pallas kernels for 0%

profile of v2, /device:TPU:0, one launch (start us, length us, event | category | flops | bytes accessed | tf_op | source)
XLA Modules:
  0.0 72.9 jit_solution(1064473228849662076)
XLA Ops:
  0.6 0.0 copy-start.3
  0.6 0.7 copy-done.3
  1.3 0.7 reshape.28.counts
  2.0 0.7 pad_add_fusion.coords
  2.7 1.5 %shard_map.95 = (f32[128,128]{1,0:T(8,128)}, f32[56,128]{1,0:T(8,128)}) custom-call(s32[3]{0:T(128)} %pad_add_fusion.coords, s32[16]{0:T(128)} %reshape.28.counts, f32[3,2,2,4,128]{4,3,2,1,0:T(4,128)} %local.1, f32[2,2,4,128]{3,2,1,0:T(4,128)} %charges.1, f32[2,2,4,128]{3,2,1,0:T(4,128)} %radii.1, s32[2,2,4,128]{3,2,1,0:T(4,128)} %slots.1, f32[12,24]{1,0:T(8,128)} %poses.1, ...), custom_call_target="tpu_custom_call" | custom-call | tf_op jit(solution)/shard_map/pallas_call | solution.py:485
  4.1 3.0 %collective-permute-start = (f32[56,128]{1,0:T(8,128)}, f32[56,128]{1,0:T(8,128)S(1)}, u32[]{:S(2)}, u32[]{:S(2)}) collective-permute-start(f32[56,128]{1,0:T(8,128)} %get-tuple-element.7), channel_id=1, source_target_pairs={{1,0},{0,1},{3,2},{2,3},{5,4},{4,5},{7,6},{6,7},{9,8},{8,9},{11,10... | collective-permute-start | bytes 86024 | tf_op jit(solution)/shard_map/ppermute | solution.py:431
  7.2 2.1 %collective-permute-done = f32[56,128]{1,0:T(8,128)S(1)} collective-permute-done((f32[56,128]{1,0:T(8,128)}, f32[56,128]{1,0:T(8,128)S(1)}, u32[]{:S(2)}, u32[]{:S(2)}) %collective-permute-start) | collective-permute-done | bytes 28704 | tf_op jit(solution)/shard_map/ppermute | solution.py:431
  9.2 0.7 slice_add_fusion.1
  10.0 3.1 %collective-permute-start.1 = (f32[56,128]{1,0:T(8,128)S(1)}, f32[56,128]{1,0:T(8,128)S(1)}, u32[]{:S(2)}, u32[]{:S(2)}) collective-permute-start(f32[56,128]{1,0:T(8,128)S(1)} %pad_maximum_fusion.5), channel_id=1, source_target_pairs={{2,0},{3,1},{0,2},{1,3},{6,4},{7,5},{4,6},{5,7},{10,8},{11,9},{8,1... | collective-permute-start | bytes 86024 | tf_op jit(solution)/shard_map/ppermute | solution.py:431
  13.1 0.0 copy-done.1
  13.1 1.8 %collective-permute-done.1 = f32[56,128]{1,0:T(8,128)S(1)} collective-permute-done((f32[56,128]{1,0:T(8,128)S(1)}, f32[56,128]{1,0:T(8,128)S(1)}, u32[]{:S(2)}, u32[]{:S(2)}) %collective-permute-start.1) | collective-permute-done | bytes 28704 | tf_op jit(solution)/shard_map/ppermute | solution.py:431
  14.9 0.1 collective-permute-start.2
  15.0 1.2 %collective-permute-done.2 = f32[104,128]{1,0:T(8,128)S(1)} collective-permute-done((f32[104,128]{1,0:T(8,128)S(1)}, f32[104,128]{1,0:T(8,128)S(1)}, u32[]{:S(2)}, u32[]{:S(2)}) %collective-permute-start.2) | collective-permute-done | bytes 53280 | tf_op jit(solution)/shard_map/ppermute | solution.py:431
  16.3 1.9 %collective-permute-start.3 = (f32[128,128]{1,0:T(8,128)S(1)}, f32[128,128]{1,0:T(8,128)S(1)}, u32[]{:S(2)}, u32[]{:S(2)}) collective-permute-start(f32[128,128]{1,0:T(8,128)S(1)} %pad_maximum_fusion.2), channel_id=1, source_target_pairs={{8,0},{12,4},{0,8},{4,12},{9,1},{13,5},{1,9},{5,13},{10,2},{14,6},... | collective-permute-start | bytes 196616 | tf_op jit(solution)/shard_map/ppermute | solution.py:431
  18.2 2.4 %collective-permute-done.3 = f32[128,128]{1,0:T(8,128)S(1)} collective-permute-done((f32[128,128]{1,0:T(8,128)S(1)}, f32[128,128]{1,0:T(8,128)S(1)}, u32[]{:S(2)}, u32[]{:S(2)}) %collective-permute-start.3) | collective-permute-done | bytes 65568 | tf_op jit(solution)/shard_map/ppermute | solution.py:431
  20.7 1.9 %collective-permute-start.4 = (f32[216,128]{1,0:T(8,128)S(1)}, f32[216,128]{1,0:T(8,128)S(1)}, u32[]{:S(2)}, u32[]{:S(2)}) collective-permute-start(f32[216,128]{1,0:T(8,128)S(1)} %pad_maximum_fusion), channel_id=1, source_target_pairs={{16,0},{0,16},{17,1},{1,17},{18,2},{2,18},{19,3},{3,19},{20,4},{4,... | collective-permute-start | bytes 331784 | tf_op jit(solution)/shard_map/ppermute | solution.py:431
  22.5 0.1 stack.25.coords
  22.6 2.8 %collective-permute-done.4 = f32[216,128]{1,0:T(8,128)S(1)} collective-permute-done((f32[216,128]{1,0:T(8,128)S(1)}, f32[216,128]{1,0:T(8,128)S(1)}, u32[]{:S(2)}, u32[]{:S(2)}) %collective-permute-start.4) | collective-permute-done | bytes 110624 | tf_op jit(solution)/shard_map/ppermute | solution.py:431
  25.5 0.0 copy-start
  25.5 26.3 %shard_map.96 = f32[64,128]{1,0:T(8,128)S(1)} custom-call(s32[8]{0:T(128)S(1)} %stack.25.coords, f32[128,128]{1,0:T(8,128)S(1)} %copy-done.1, f32[32,128]{1,0:T(8,128)S(1)} %slice_select_fusion.1.halo_z, f32[80,128]{1,0:T(8,128)S(1)} %slice_select_fusion.halo_y, f32[120,128]{1,0:T(8,128)S(1)} %slice.71.halo_x, f32[192,128]{1,0:T(8,128)S(1)} %pad_maximum_fusion.1.table), custom_call_target="tpu_custom_call" | custom-call | tf_op jit(solution)/shard_map/pallas_call | solution.py:403
  51.8 0.1 collective-permute-start.5
  51.9 1.2 %collective-permute-done.5 = f32[2,4,8,128]{3,2,1,0:T(8,128)S(1)} collective-permute-done((f32[2,4,8,128]{3,2,1,0:T(8,128)S(1)}, f32[2,4,8,128]{3,2,1,0:T(8,128)S(1)}, u32[]{:S(2)}, u32[]{:S(2)}) %collective-permute-start.5) | collective-permute-done | bytes 32800 | tf_op jit(solution)/shard_map/ppermute | solution.py:431
  53.1 0.7 collective-permute-start.6
  53.8 3.2 %collective-permute-done.6 = f32[2,4,8,128]{3,2,1,0:T(8,128)S(1)} collective-permute-done((f32[2,4,8,128]{3,2,1,0:T(8,128)S(1)}, f32[2,4,8,128]{3,2,1,0:T(8,128)S(1)}, u32[]{:S(2)}, u32[]{:S(2)}) %collective-permute-start.6) | collective-permute-done | bytes 32800 | tf_op jit(solution)/shard_map/ppermute | solution.py:431
  57.0 2.1 %collective-permute-start.7 = (f32[2,4,8,128]{3,2,1,0:T(8,128)S(1)}, f32[2,4,8,128]{3,2,1,0:T(8,128)S(1)}, u32[]{:S(2)}, u32[]{:S(2)}) collective-permute-start(f32[2,4,8,128]{3,2,1,0:T(8,128)S(1)} %add.33), channel_id=1, source_target_pairs={{16,0},{0,16},{17,1},{1,17},{18,2},{2,18},{19,3},{3,19},{20,4},{4,... | collective-permute-start | bytes 98312 | tf_op jit(solution)/shard_map/ppermute | solution.py:431
  59.1 1.9 %collective-permute-done.7 = f32[2,4,8,128]{3,2,1,0:T(8,128)S(1)} collective-permute-done((f32[2,4,8,128]{3,2,1,0:T(8,128)S(1)}, f32[2,4,8,128]{3,2,1,0:T(8,128)S(1)}, u32[]{:S(2)}, u32[]{:S(2)}) %collective-permute-start.7) | collective-permute-done | bytes 32800 | tf_op jit(solution)/shard_map/ppermute | solution.py:431
  61.0 0.6 collective-permute-start.8
  61.6 3.3 %collective-permute-done.8 = f32[2,4,8,128]{3,2,1,0:T(8,128)S(1)} collective-permute-done((f32[2,4,8,128]{3,2,1,0:T(8,128)S(1)}, f32[2,4,8,128]{3,2,1,0:T(8,128)S(1)}, u32[]{:S(2)}, u32[]{:S(2)}) %collective-permute-start.8) | collective-permute-done | bytes 32800 | tf_op jit(solution)/shard_map/ppermute | solution.py:431
  65.0 3.6 %collective-permute-start.9 = (f32[2,4,8,128]{3,2,1,0:T(8,128)S(1)}, f32[2,4,8,128]{3,2,1,0:T(8,128)S(1)}, u32[]{:S(2)}, u32[]{:S(2)}) collective-permute-start(f32[2,4,8,128]{3,2,1,0:T(8,128)S(1)} %add.35), channel_id=1, source_target_pairs={{2,0},{3,1},{0,2},{1,3},{6,4},{7,5},{4,6},{5,7},{10,8},{11,9},{8,1... | collective-permute-start | bytes 98312 | tf_op jit(solution)/shard_map/ppermute | solution.py:431
  68.6 1.9 %collective-permute-done.9 = f32[2,4,8,128]{3,2,1,0:T(8,128)S(1)} collective-permute-done((f32[2,4,8,128]{3,2,1,0:T(8,128)S(1)}, f32[2,4,8,128]{3,2,1,0:T(8,128)S(1)}, u32[]{:S(2)}, u32[]{:S(2)}) %collective-permute-start.9) | collective-permute-done | bytes 32800 | tf_op jit(solution)/shard_map/ppermute | solution.py:431
  70.5 0.6 add.36
  71.1 1.8 %shard_map.97 = (f32[12,24]{1,0:T(8,128)}, f32[3,16,128]{2,1,0:T(8,128)}) custom-call(s32[8]{0:T(128)} %copy-done.2, f32[128,128]{1,0:T(8,128)} %get-tuple-element.6.own, f32[192,128]{1,0:T(8,128)} %copy-done, f32[64,128]{1,0:T(8,128)} %bitcast.21), custom_call_target="tpu_custom_call" | custom-call | tf_op jit(solution)/shard_map/pallas_call | solution.py:522
  (29 shorter events, 0.1 us)
Async XLA Ops:
  0.6 0.7 copy-start.3
  4.1 8.9 %copy-start.1 = (f32[128,128]{1,0:T(8,128)S(1)}, f32[128,128]{1,0:T(8,128)}, u32[]{:S(2)}) copy-start(f32[128,128]{1,0:T(8,128)} %get-tuple-element.6.own) | copy-start | bytes 196612
  4.1 5.1 %collective-permute-start = (f32[56,128]{1,0:T(8,128)}, f32[56,128]{1,0:T(8,128)S(1)}, u32[]{:S(2)}, u32[]{:S(2)}) collective-permute-start(f32[56,128]{1,0:T(8,128)} %get-tuple-element.7), channel_id=1, source_target_pairs={{1,0},{0,1},{3,2},{2,3},{5,4},{4,5},{7,6},{6,7},{9,8},{8,9},{11,10... | collective-permute-start | bytes 86024 | tf_op jit(solution)/shard_map/ppermute | solution.py:431
  10.0 5.0 %collective-permute-start.1 = (f32[56,128]{1,0:T(8,128)S(1)}, f32[56,128]{1,0:T(8,128)S(1)}, u32[]{:S(2)}, u32[]{:S(2)}) collective-permute-start(f32[56,128]{1,0:T(8,128)S(1)} %pad_maximum_fusion.5), channel_id=1, source_target_pairs={{2,0},{3,1},{0,2},{1,3},{6,4},{7,5},{4,6},{5,7},{10,8},{11,9},{8,1... | collective-permute-start | bytes 86024 | tf_op jit(solution)/shard_map/ppermute | solution.py:431
  14.9 1.3 %collective-permute-start.2 = (f32[104,128]{1,0:T(8,128)S(1)}, f32[104,128]{1,0:T(8,128)S(1)}, u32[]{:S(2)}, u32[]{:S(2)}) collective-permute-start(f32[104,128]{1,0:T(8,128)S(1)} %pad_maximum_fusion.4), channel_id=1, source_target_pairs={{4,0},{0,4},{12,8},{8,12},{5,1},{1,5},{13,9},{9,13},{6,2},{2,6},{1... | collective-permute-start | bytes 159752 | tf_op jit(solution)/shard_map/ppermute | solution.py:431
  16.3 4.3 %collective-permute-start.3 = (f32[128,128]{1,0:T(8,128)S(1)}, f32[128,128]{1,0:T(8,128)S(1)}, u32[]{:S(2)}, u32[]{:S(2)}) collective-permute-start(f32[128,128]{1,0:T(8,128)S(1)} %pad_maximum_fusion.2), channel_id=1, source_target_pairs={{8,0},{12,4},{0,8},{4,12},{9,1},{13,5},{1,9},{5,13},{10,2},{14,6},... | collective-permute-start | bytes 196616 | tf_op jit(solution)/shard_map/ppermute | solution.py:431
  20.7 4.8 %collective-permute-start.4 = (f32[216,128]{1,0:T(8,128)S(1)}, f32[216,128]{1,0:T(8,128)S(1)}, u32[]{:S(2)}, u32[]{:S(2)}) collective-permute-start(f32[216,128]{1,0:T(8,128)S(1)} %pad_maximum_fusion), channel_id=1, source_target_pairs={{16,0},{0,16},{17,1},{1,17},{18,2},{2,18},{19,3},{3,19},{20,4},{4,... | collective-permute-start | bytes 331784 | tf_op jit(solution)/shard_map/ppermute | solution.py:431
  22.6 2.9 %copy-start.2 = (s32[8]{0:T(128)}, s32[8]{0:T(128)S(1)}, u32[]{:S(2)}) copy-start(s32[8]{0:T(128)S(1)} %stack.25.coords) | copy-start | bytes 100
  25.5 26.3 %copy-start = (f32[192,128]{1,0:T(8,128)}, f32[192,128]{1,0:T(8,128)S(1)}, u32[]{:S(2)}) copy-start(f32[192,128]{1,0:T(8,128)S(1)} %pad_maximum_fusion.1.table) | copy-start | bytes 294916
  51.8 1.3 %collective-permute-start.5 = (f32[2,4,8,128]{3,2,1,0:T(8,128)S(1)}, f32[2,4,8,128]{3,2,1,0:T(8,128)S(1)}, u32[]{:S(2)}, u32[]{:S(2)}) collective-permute-start(f32[2,4,8,128]{3,2,1,0:T(8,128)S(1)} %bitcast.17), channel_id=1, source_target_pairs={{4,0},{0,4},{12,8},{8,12},{5,1},{1,5},{13,9},{9,13},{6,2},{2,6},{1... | collective-permute-start | bytes 98312 | tf_op jit(solution)/shard_map/ppermute | solution.py:431
  53.1 3.9 %collective-permute-start.6 = (f32[2,4,8,128]{3,2,1,0:T(8,128)S(1)}, f32[2,4,8,128]{3,2,1,0:T(8,128)S(1)}, u32[]{:S(2)}, u32[]{:S(2)}) collective-permute-start(f32[2,4,8,128]{3,2,1,0:T(8,128)S(1)} %add.32), channel_id=1, source_target_pairs={{8,0},{12,4},{0,8},{4,12},{9,1},{13,5},{1,9},{5,13},{10,2},{14,6},... | collective-permute-start | bytes 98312 | tf_op jit(solution)/shard_map/ppermute | solution.py:431
  57.0 4.0 %collective-permute-start.7 = (f32[2,4,8,128]{3,2,1,0:T(8,128)S(1)}, f32[2,4,8,128]{3,2,1,0:T(8,128)S(1)}, u32[]{:S(2)}, u32[]{:S(2)}) collective-permute-start(f32[2,4,8,128]{3,2,1,0:T(8,128)S(1)} %add.33), channel_id=1, source_target_pairs={{16,0},{0,16},{17,1},{1,17},{18,2},{2,18},{19,3},{3,19},{20,4},{4,... | collective-permute-start | bytes 98312 | tf_op jit(solution)/shard_map/ppermute | solution.py:431
  61.0 3.9 %collective-permute-start.8 = (f32[2,4,8,128]{3,2,1,0:T(8,128)S(1)}, f32[2,4,8,128]{3,2,1,0:T(8,128)S(1)}, u32[]{:S(2)}, u32[]{:S(2)}) collective-permute-start(f32[2,4,8,128]{3,2,1,0:T(8,128)S(1)} %add.34), channel_id=1, source_target_pairs={{1,0},{0,1},{3,2},{2,3},{5,4},{4,5},{7,6},{6,7},{9,8},{8,9},{11,10... | collective-permute-start | bytes 98312 | tf_op jit(solution)/shard_map/ppermute | solution.py:431
  65.0 5.5 %collective-permute-start.9 = (f32[2,4,8,128]{3,2,1,0:T(8,128)S(1)}, f32[2,4,8,128]{3,2,1,0:T(8,128)S(1)}, u32[]{:S(2)}, u32[]{:S(2)}) collective-permute-start(f32[2,4,8,128]{3,2,1,0:T(8,128)S(1)} %add.35), channel_id=1, source_target_pairs={{2,0},{3,1},{0,2},{1,3},{6,4},{7,5},{4,6},{5,7},{10,8},{11,9},{8,1... | collective-permute-start | bytes 98312 | tf_op jit(solution)/shard_map/ppermute | solution.py:431

commit v3 on v2

v3 whole, which is shorter than its diff:
```python
import functools
import itertools
import math

import jax
import jax.numpy as jnp
from jax import lax
from jax.experimental import pallas as pl
from jax.experimental.pallas import tpu as pltpu
from jax.sharding import PartitionSpec as P

min_reach = 0.15
clash_gain = 20.0
debye_length = 0.5
move_gain = 0.02
turn_gain = 0.01

LANES = 128
ROWS = 8
BODY_ROWS = 20
PACKED = 4
SEGMENT = 32
SCALE = 1.0 / (debye_length * math.log(2.0))
CHARGE_SCALE = math.sqrt(1.0 / (clash_gain * SCALE))
EMPTY = -20.0

f32 = jnp.float32
i32 = jnp.int32

T_ALL = (4, 4, 4, 4, 4, 4, 2, 2, 2, 2, 2, 2)
SP, FO, GA = 4, 4, 8
HALO_ORDER = (1, 0, 2)


def unpack(packed, owned, spread_rows, table):
    per_row = BODY_ROWS // PACKED
    row = lax.broadcasted_iota(i32, (8, LANES), 0)
    lane = lax.broadcasted_iota(i32, (8, LANES), 1)
    for first in range(0, packed.shape[0], 8):
        value = packed[first : first + 8, :]
        segment = ((first + row) // PACKED) % 4
        inside = lane - segment * SEGMENT
        valid = (inside >= 0) & (inside < owned)
        for j in range(per_row):
            index = jnp.where(valid, inside + j * owned, 0)
            picked = jnp.take_along_axis(value, index, axis=1)
            spread_rows[j, first : first + 8, :] = jnp.where(valid, picked, 0.0)
    chunks = table.shape[1]
    for m in range(BODY_ROWS):
        for first in range(0, chunks, 8):
            many = min(8, chunks - first)
            parts = [
                spread_rows[m % per_row, pl.ds((first * 4 + c) * PACKED + m // per_row, many, stride=4 * PACKED), :]
                for c in range(4)
            ]
            table[m, first : first + many, :] = (parts[0] + parts[1]) + (parts[2] + parts[3])


def owner_at(code, coords, counts, beyond=(0, 0, 0)):
    steps = ((code >> 9) - 1, ((code >> 7) & 3) - 1, ((code >> 5) & 3) - 1)
    x, y, z = [(step + coords[k] + beyond[k]) & (counts[k] - 1) for k, step in enumerate(steps)]
    chunk = (x * counts[1] + y) * (counts[2] // 4) + (z >> 2)
    return chunk, (z & 3) * SEGMENT + (code & (SEGMENT - 1))


def prep_kernel(sizes, axis, counts, local, charges, radii, slots, poses, mobility, noise, own, face, bodies, rows):
    cells_x, cells_y, cells_z, owned = sizes
    per_row = BODY_ROWS // PACKED
    rows[...] = jnp.zeros(rows.shape, f32)
    rows[0:12, :owned] = poses[...]
    rows[12:14, :owned] = mobility[...]
    rows[14:20, :owned] = noise[...]
    packed = rows[pl.ds(0, PACKED, stride=per_row), :]
    for j in range(1, per_row):
        packed = packed + pltpu.roll(rows[pl.ds(j, PACKED, stride=per_row), :], j * owned, axis=1)
    for device in range(bodies.shape[0]):
        bodies[device] = packed
    lane = lax.broadcasted_iota(i32, (cells_z, LANES), 1)
    row = lax.broadcasted_iota(i32, (cells_z, LANES), 0)
    for x in range(cells_x):
        for y in range(cells_y):
            base = (x * cells_y + y) * cells_z * ROWS
            held = jnp.zeros((cells_z, LANES), i32)
            for z in range(cells_z):
                held = jnp.where(row == z, counts[x, y, z], held)
            filled = lane < held
            slot = slots[x, y].astype(f32)
            offset = jnp.floor((slot + 0.5) * (1.0 / owned))
            body = slot - offset * owned
            step_x = jnp.floor((offset + 0.5) * (1.0 / 9.0))
            step_y = jnp.floor((offset - 9.0 * step_x + 0.5) * (1.0 / 3.0))
            step_z = offset - 9.0 * step_x - 3.0 * step_y
            code = body + 32.0 * step_z + 128.0 * step_y + 512.0 * step_x
            rows = [
                local[0, x, y],
                local[1, x, y],
                local[2, x, y],
                jnp.where(filled, charges[x, y], 0.0),
                jnp.where(filled, radii[x, y], EMPTY / SCALE),
                code,
                held.astype(f32),
                jnp.zeros((cells_z, LANES), f32),
            ]
            for k, value in enumerate(rows):
                own[pl.ds(base + k, cells_z, stride=ROWS), :] = value
    at = 0
    for x in range(1 if axis == 0 else cells_x):
        for y in range(1 if axis == 1 else cells_y):
            for z in range(1 if axis == 2 else cells_z):
                base = ((x * cells_y + y) * cells_z + z) * ROWS
                face[at : at + ROWS, :] = own[base : base + ROWS, :]
                at += ROWS


def lookup(table_row, lane_at, chunk_at, chunks):
    value = None
    for chunk in range(chunks):
        row = jnp.broadcast_to(table_row(chunk), lane_at.shape)
        picked = jnp.take_along_axis(row, lane_at, axis=1)
        value = picked if value is None else jnp.where(chunk_at == chunk, picked, value)
    return value


def tiles_together(rows):
    return T_ALL[min(rows, len(T_ALL)) - 1]


@functools.cache
def pair_plan(cells_x, cells_y, cells_z):
    corners = [(x, y, z) for x in (0, 1) for y in (0, 1) for z in (0, 1)]
    kinds = [
        (low, high)
        for n, low in enumerate(corners)
        for high in corners[n:]
        if all(min(i, j) == 0 for i, j in zip(low, high))
    ]
    own = [(x, y, z) for x in range(cells_x) for y in range(cells_y) for z in range(cells_z)]
    pairs = [
        tuple(tuple(i + j for i, j in zip(base, corner)) for corner in kind) for base in own for kind in kinds
    ]
    rows = {cell: [] for cell in own}
    later = []
    for low, high in pairs:
        if low in rows and high not in rows:
            rows[low].append(high)
        elif high in rows and low not in rows:
            rows[high].append(low)
        elif low == high:
            rows[low].append(high)
        else:
            later.append((low, high))
    outside = [pair for pair in later if pair[0] not in rows]
    for low, high in later:
        if low in rows:
            short, other = sorted((low, high), key=lambda cell: (len(rows[cell]), cell))
            rows[short].append(other)
    while outside:
        names = sorted({cell for pair in outside for cell in pair})
        best = max(names, key=lambda cell: sum(cell in pair for pair in outside))
        rows[best] = [pair[1] if pair[0] == best else pair[0] for pair in outside if best in pair]
        outside = [pair for pair in outside if best not in pair]
    return tuple((cell, tuple(others)) for cell, others in rows.items())


def pair_terms(column, row, dist_floor):
    dx = column[0] - row[0]
    dy = column[1] - row[1]
    dz = column[2] - row[2]
    dist_sq = dx * dx + dy * dy + dz * dz
    inverse = lax.rsqrt(jnp.maximum(dist_sq, 1e-30))
    dist = dist_sq * inverse
    inv_reach = jnp.minimum(inverse, 1.0 / dist_floor)
    gap = (column[3] + row[3]) - dist
    cut = jnp.maximum(SCALE * SCALE - dist_sq, 0.0)
    screened = (column[4] * row[4]) * jnp.exp2(gap) * (cut * cut)
    weight = inv_reach * (jnp.maximum(gap, 0.0) + screened * ((inv_reach + math.log(2.0)) * inv_reach))
    return weight * dx, weight * dy, weight * dz


def pair_kernel(
    sizes, coords, own, first_halo, second_halo, third_halo, packed, out, table,
    spread_rows, raw, pos, arms, lane_at, chunk_at, held, order, wide, row_force, column_force, contrib,
):
    cells_x, cells_y, cells_z, count_x, count_y, count_z, owned = sizes
    chunks = table.shape[1]
    unpack(packed, owned, spread_rows, table)
    ext_y, ext_z = cells_y + 1, cells_z + 1
    cells = (cells_x + 1) * ext_y * ext_z
    padded = raw.shape[0] // ROWS

    def at(x, y, z):
        return (x * ext_y + y) * ext_z + z

    def put(cell, ref, index):
        raw[cell * ROWS : (cell + 1) * ROWS, :] = ref[index * ROWS : (index + 1) * ROWS, :]

    extents = (cells_x, cells_y, cells_z)
    halos = (first_halo, second_halo, third_halo)
    for place_at in itertools.product(*[range(extent + 1) for extent in extents]):
        source, shape = own, list(extents)
        for step, axis in enumerate(HALO_ORDER):
            if place_at[axis] == extents[axis]:
                source = halos[step]
                shape = [extent + (HALO_ORDER.index(k) < step) for k, extent in enumerate(extents)]
                shape[axis] = 1
        index = 0
        for k in range(3):
            index = index * shape[k] + (0 if shape[k] == 1 else place_at[k])
        put(at(*place_at), source, index)
    for cell in range(cells, padded):
        raw[cell * ROWS : (cell + 1) * ROWS, :] = jnp.zeros((ROWS, LANES), f32)
    for cell in range(cells):
        held[cell] = jnp.max(raw[cell * ROWS + 6 : cell * ROWS + 7, :]).astype(i32)

    coord_x, coord_y, coord_z = coords[0], coords[1], coords[2]

    def place(group, carry):
        first = pl.multiple_of(group * 64, 64)
        load = lambda k: raw[pl.ds(first + k, 8, stride=ROWS), :]
        cell = group * 8 + lax.broadcasted_iota(i32, (8, LANES), 0)
        cell_x = sum((cell >= n * ext_y * ext_z).astype(i32) for n in range(1, cells_x + 1))
        rest = cell - cell_x * (ext_y * ext_z)
        cell_y = sum((rest >= n * ext_z).astype(i32) for n in range(1, cells_y + 1))
        cell_z = rest - cell_y * ext_z
        code = load(5).astype(i32)
        beyond = [
            (cell_now >= cells_now).astype(i32)
            for cell_now, cells_now in ((cell_x, cells_x), (cell_y, cells_y), (cell_z, cells_z))
        ]
        owners, lanes = owner_at(code, (coord_x, coord_y, coord_z), (count_x, count_y, count_z), beyond)
        lane_at[pl.ds(pl.multiple_of(group * 8, 8), 8), :] = lanes
        chunk_at[pl.ds(pl.multiple_of(group * 8, 8), 8), :] = owners
        pose = [lookup(lambda n, k=k: table[k, n : n + 1, :], lanes, owners, chunks) for k in range(12)]
        local = [load(k) for k in range(3)]
        cell_at = (cell_x, cell_y, cell_z)
        extents = (cells_x, cells_y, cells_z)
        for k in range(3):
            arm = pose[3 * k] * local[0] + pose[3 * k + 1] * local[1] + pose[3 * k + 2] * local[2]
            arms[k, pl.ds(pl.multiple_of(group * 8, 8), 8), :] = arm
            box = float(extents[k] * (count_x, count_y, count_z)[k])
            corner = ((coord_x, coord_y, coord_z)[k] * extents[k]).astype(f32)
            middle = cell_at[k].astype(f32) + 0.5
            inside = arm + pose[9 + k] - corner - middle
            inside = inside - box * jnp.floor(inside * (1.0 / box) + 0.5)
            pos[pl.ds(first + k, 8, stride=ROWS), :] = (inside + middle) * SCALE
        radius = load(4) * SCALE
        pos[pl.ds(first + 3, 8, stride=ROWS), :] = radius
        pos[pl.ds(first + 4, 8, stride=ROWS), :] = load(3) * CHARGE_SCALE * jnp.exp2(-radius)
        return carry

    for k in range(5, ROWS):
        for group in range(padded // 8):
            pos[pl.ds(group * 64 + k, 8, stride=ROWS), :] = jnp.zeros((8, LANES), f32)
    lax.fori_loop(0, padded // 8, place, 0)
    row_force[...] = jnp.zeros(row_force.shape, f32)
    plan = pair_plan(cells_x, cells_y, cells_z)
    listed = [at(*column) for column, _ in plan]
    listed += [listed[-1]] * (-len(listed) % 4)
    for n, cell in enumerate(listed):
        order[n] = cell
    kind = lax.broadcasted_iota(i32, (32, 5 * LANES), 1) // LANES
    part = lax.broadcasted_iota(i32, (32, 5 * LANES), 0)
    picker = jnp.where((part % 8 == kind) & (part < 24), 1.0, 0.0).astype(jnp.bfloat16)

    def spread(step, carry):
        for n in range(SP):
            cell = order[step * SP + n]
            value = pos[pl.ds(pl.multiple_of(cell * ROWS, 8), 8), :]
            high = value.astype(jnp.bfloat16).astype(f32)
            rest = value - high
            middle = rest.astype(jnp.bfloat16).astype(f32)
            low = rest - middle
            parts = jnp.concatenate([high, middle, low, jnp.zeros_like(low)], axis=0).astype(jnp.bfloat16)
            out_wide = lax.dot_general(parts, picker, (((0,), (0,)), ((), ())), preferred_element_type=f32)
            for k in range(5):
                wide[cell, k, :, :] = out_wide[:, k * LANES : (k + 1) * LANES]
        return carry

    lax.fori_loop(0, len(listed) // SP, spread, 0)

    for column, rows in plan:
        column_cell = at(*column)
        row_cells = [at(*row) for row in rows]

        def tile_pairs(first, together, step, inner, column_cell=column_cell, row_cells=row_cells):
            spans, cols = [], []
            for n in range(together):
                span = pl.ds(pl.multiple_of((first + step * together + n) * 8, 8), 8)
                spans.append(span)
                cols.append([wide[column_cell, k, span, :] for k in range(5)])
            sums = [[None] * 3 for _ in range(together)]
            for row_cell in row_cells:
                row = [
                    jnp.broadcast_to(pos[row_cell * ROWS + k : row_cell * ROWS + k + 1, :], (8, LANES))
                    for k in range(5)
                ]
                back = [None] * 3
                for n in range(together):
                    parts = pair_terms(cols[n], row, min_reach * SCALE)
                    for k in range(3):
                        sums[n][k] = parts[k] if sums[n][k] is None else sums[n][k] + parts[k]
                        back[k] = parts[k] if back[k] is None else back[k] + parts[k]
                if row_cell != column_cell:
                    span = slice(row_cell * ROWS, row_cell * ROWS + ROWS)
                    for k in range(3):
                        row_force[k, span, :] = row_force[k, span, :] - back[k]
            for n in range(together):
                for k in range(3):
                    column_force[column_cell, k, spans[n], :] = sums[n][k]
            return inner

        tiles = (held[column_cell] + 7) // 8
        together = tiles_together(len(rows))
        whole = tiles // together
        lax.fori_loop(0, whole, functools.partial(tile_pairs, 0, together), 0)
        rest = tiles - whole * together
        if together >= 4:
            lax.fori_loop(0, (rest + 1) // 2, functools.partial(tile_pairs, whole * together, 2), 0)
        elif together > 1:
            lax.fori_loop(0, rest, functools.partial(tile_pairs, whole * together, 1), 0)

    ones = jnp.where(lax.broadcasted_iota(i32, (16, 2 * LANES), 0) == 0, 1.0, 0.0).astype(jnp.bfloat16)

    def fold_line(cell):
        value = column_force[cell].reshape(3 * LANES, LANES)
        high = value.astype(jnp.bfloat16)
        low = (value - high.astype(f32)).astype(jnp.bfloat16)
        both = jnp.concatenate([high, low], axis=1)
        return lax.dot_general(ones, both, (((1,), (1,)), ((), ())), preferred_element_type=f32)

    def fold(cells_now):
        lines = [fold_line(cell) for cell in cells_now]
        for cell, line in zip(cells_now, lines):
            span = pl.ds(pl.multiple_of(cell * ROWS, 8), 8)
            for k in range(3):
                row_force[k, span, :] += line[:8, k * LANES : (k + 1) * LANES]

    def fold_step(step, carry):
        fold([order[step * FO + n] for n in range(FO)])
        return carry

    even = len(plan) // FO
    lax.fori_loop(0, even, fold_step, 0)
    fold([order[n] for n in range(even * FO, len(plan))])

    def twist(group, carry):
        first = pl.multiple_of(group * 64, 64)
        span = pl.ds(pl.multiple_of(group * 8, 8), 8)
        force = []
        filled = lax.broadcasted_iota(i32, (8, LANES), 1).astype(f32) < raw[pl.ds(first + 6, 8, stride=ROWS), :]
        for k in range(3):
            total = row_force[k, pl.ds(first, 8, stride=ROWS), :]
            for n in range(1, 8):
                total = total + row_force[k, pl.ds(first + n, 8, stride=ROWS), :]
            force.append(jnp.where(filled, total * (clash_gain / SCALE), 0.0))
        arm = [arms[k, span, :] for k in range(3)]
        rows = force + [
            arm[1] * force[2] - arm[2] * force[1],
            arm[2] * force[0] - arm[0] * force[2],
            arm[0] * force[1] - arm[1] * force[0],
        ]
        for k, value in enumerate(rows):
            contrib[pl.ds(first + k, 8, stride=ROWS), :] = value
        for k in (6, 7):
            contrib[pl.ds(first + k, 8, stride=ROWS), :] = jnp.zeros((8, LANES), f32)
        return carry

    lax.fori_loop(0, padded // 8, twist, 0)

    body = lax.broadcasted_iota(i32, (LANES, LANES), 0)

    def gather_sums(step, total):
        lefts, rights = [], []
        for n in range(GA):
            cell = step * GA + n
            value = contrib[pl.ds(pl.multiple_of(cell * ROWS, 8), 8), :]
            high = value.astype(jnp.bfloat16).astype(f32)
            low = value - high
            owner = jnp.broadcast_to(chunk_at[pl.ds(cell, 1), :], (8, LANES))
            member = jnp.broadcast_to(lane_at[pl.ds(cell, 1), :], (LANES, LANES)) == body
            pieces = []
            for chunk in range(chunks):
                mine = owner == chunk
                pieces.append(jnp.where(mine, high, 0.0))
                pieces.append(jnp.where(mine, low, 0.0))
            lefts.append(jnp.concatenate(pieces, axis=0).astype(jnp.bfloat16))
            rights.append(jnp.where(member, 1.0, 0.0).astype(jnp.bfloat16))
        left = jnp.concatenate(lefts, axis=1)
        right = jnp.concatenate(rights, axis=1)
        return total + lax.dot_general(left, right, (((1,), (1,)), ((), ())), preferred_element_type=f32)

    total = lax.fori_loop(0, padded // GA, gather_sums, jnp.zeros((chunks * 16, LANES), f32))
    for chunk in range(chunks):
        out[chunk * 8 : chunk * 8 + 8, :] = total[chunk * 16 : chunk * 16 + 8] + total[chunk * 16 + 8 : chunk * 16 + 16]


def advance_rows(pose, force, torque, mobility, noise):
    centre = [pose[9 + k] + move_gain * mobility[0] * force[k] + noise[k] for k in range(3)]
    spin = [0.5 * (turn_gain * mobility[1] * torque[k] + noise[3 + k]) for k in range(3)]
    spin_sq = spin[0] * spin[0] + spin[1] * spin[1] + spin[2] * spin[2]
    factor = 2.0 / (1.0 + spin_sq)
    skew = [[None, -spin[2], spin[1]], [spin[2], None, -spin[0]], [-spin[1], spin[0], None]]
    rows = []
    for r in range(3):
        turn = []
        for c in range(3):
            inner = spin[r] * spin[c]
            turn.append(1.0 + factor * (inner - spin_sq) if r == c else factor * (skew[r][c] + inner))
        for c in range(3):
            rows.append(turn[0] * pose[c] + turn[1] * pose[3 + c] + turn[2] * pose[6 + c])
    return rows + centre


def move_kernel(sizes, coords, own, table, totals, others, stepped, positions, fresh):
    cells_x, cells_y, cells_z, count_x, count_y, count_z, owned = sizes
    chunks = table.shape[1]
    for first in range(0, chunks, 8):
        many = min(8, chunks - first)
        row = [table[k, first : first + many, :] for k in range(BODY_ROWS)]
        total = [
            totals[pl.ds(first * 8 + k, many, stride=8), :] + others[pl.ds(first * 8 + k, many, stride=8), :]
            for k in range(6)
        ]
        new = advance_rows(row[:12], total[:3], total[3:], row[12:14], row[14:20])
        for k in range(12):
            fresh[pl.ds(first * 16 + k, many, stride=16), :] = new[k]
    mine = ((coords[0] * count_y + coords[1]) * (count_z // 4) + (coords[2] >> 2)) * 16
    turned = pltpu.roll(
        fresh[pl.ds(pl.multiple_of(mine, 16), 16), :], (4 - (coords[2] & 3)) * SEGMENT, axis=1
    )
    stepped[...] = turned[:12, :owned]
    for first in range(0, cells_x * cells_y * cells_z, 8):
        load = lambda k: own[pl.ds(first * ROWS + k, 8, stride=ROWS), :]
        owners, lanes = owner_at(
            load(5).astype(i32), (coords[0], coords[1], coords[2]), (count_x, count_y, count_z)
        )
        pose = [
            lookup(lambda n, k=k: fresh[n * 16 + k : n * 16 + k + 1, :], lanes, owners, chunks) for k in range(12)
        ]
        local = [load(k) for k in range(3)]
        for k in range(3):
            arm = pose[3 * k] * local[0] + pose[3 * k + 1] * local[1] + pose[3 * k + 2] * local[2]
            positions[k, first : first + 8, :] = arm + pose[9 + k]


def pair_sums(sizes, coords, own, first_halo, second_halo, third_halo, packed):
    cells_x, cells_y, cells_z = sizes[:3]
    chunks = packed.shape[0] // (4 * PACKED)
    vmem = pl.BlockSpec(memory_space=pltpu.VMEM)
    smem = pl.BlockSpec(memory_space=pltpu.SMEM)
    cells = (cells_x + 1) * (cells_y + 1) * (cells_z + 1)
    padded = -(-cells // 16) * 16
    return pl.pallas_call(
        functools.partial(pair_kernel, sizes),
        out_shape=(
            jax.ShapeDtypeStruct((chunks * 8, LANES), f32),
            jax.ShapeDtypeStruct((BODY_ROWS, chunks, LANES), f32),
        ),
        in_specs=[smem] + [vmem] * 5,
        out_specs=(vmem, vmem),
        scratch_shapes=[
            pltpu.VMEM((BODY_ROWS // PACKED,) + packed.shape, f32),
            pltpu.VMEM((padded * ROWS, LANES), f32),
            pltpu.VMEM((padded * ROWS, LANES), f32),
            pltpu.VMEM((3, padded, LANES), f32),
            pltpu.VMEM((padded, LANES), i32),
            pltpu.VMEM((padded, LANES), i32),
            pltpu.SMEM((padded,), i32),
            pltpu.SMEM((padded,), i32),
            pltpu.VMEM((cells, 5, LANES, LANES), f32),
            pltpu.VMEM((3, padded * ROWS, LANES), f32),
            pltpu.VMEM((cells, 3, LANES, LANES), f32),
            pltpu.VMEM((padded * ROWS, LANES), f32),
        ],
        compiler_params=pltpu.CompilerParams(vmem_limit_bytes=48 * 1024 * 1024),
    )(coords, own, first_halo, second_halo, third_halo, packed)


def from_next(block, axis):
    count = lax.axis_size(axis)
    return lax.ppermute(block, axis, [((i + 1) % count, i) for i in range(count)])


def from_partner(block, axis, mask):
    return lax.ppermute(block, axis, [(i ^ mask, i) for i in range(lax.axis_size(axis))])


def per_device(body_local, charges, radii, body_slot, cell_counts, poses, mobility, noise):
    cells_x, cells_y, cells_z, width = charges.shape
    owned = poses.shape[1]
    axes = ("gx", "gy", "gz")
    counts = tuple(lax.axis_size(axis) for axis in axes)
    devices = math.prod(counts)
    assert owned <= SEGMENT and BODY_ROWS // PACKED * owned <= LANES and width == LANES
    assert counts[2] % 4 == 0 and all(count & (count - 1) == 0 for count in counts)
    coords = jnp.stack([lax.axis_index(axis).astype(i32) for axis in axes])
    own_cells = cells_x * cells_y * cells_z
    vmem = pl.BlockSpec(memory_space=pltpu.VMEM)
    smem = pl.BlockSpec(memory_space=pltpu.SMEM)

    first_axis = HALO_ORDER[0]
    face_cells = own_cells // (cells_x, cells_y, cells_z)[first_axis]
    own, face, bodies = pl.pallas_call(
        functools.partial(prep_kernel, (cells_x, cells_y, cells_z, owned), first_axis),
        out_shape=(
            jax.ShapeDtypeStruct((own_cells * ROWS, LANES), f32),
            jax.ShapeDtypeStruct((face_cells * ROWS, LANES), f32),
            jax.ShapeDtypeStruct((devices, PACKED, LANES), f32),
        ),
        in_specs=[smem] + [vmem] * 7,
        out_specs=(vmem, vmem, vmem),
        scratch_shapes=[pltpu.VMEM((24, LANES), f32)],
    )(cell_counts, body_local, charges, radii, body_slot, poses, mobility, noise)
    packed = lax.all_to_all(bodies, axes, 0, 0).reshape(devices * PACKED, LANES)

    extended = own.reshape(cells_x, cells_y, cells_z, ROWS, LANES)
    halos = []
    for axis in HALO_ORDER:
        shape = extended.shape[:axis] + (1,) + extended.shape[axis + 1 :]
        if halos:
            face = lax.slice_in_dim(extended, 0, 1, axis=axis).reshape(-1, LANES)
        halos.append(from_next(face, axes[axis]))
        extended = jnp.concatenate([extended, halos[-1].reshape(shape)], axis=axis)

    sizes = (cells_x, cells_y, cells_z) + counts + (owned,)
    totals, table = pair_sums(sizes, coords, own, *halos, packed)

    others = jnp.zeros_like(totals)
    for axis in ("gy", "gx", "gz"):
        step = 1
        while step < lax.axis_size(axis):
            totals = totals + others
            others = from_partner(totals, axis, step)
            step *= 2

    stepped, positions = pl.pallas_call(
        functools.partial(move_kernel, sizes),
        out_shape=(
            jax.ShapeDtypeStruct((12, owned), f32),
            jax.ShapeDtypeStruct((3, own_cells, LANES), f32),
        ),
        in_specs=[smem] + [vmem] * 4,
        out_specs=(vmem, vmem),
        scratch_shapes=[pltpu.VMEM((table.shape[1] * 16, LANES), f32)],
    )(coords, own, table, totals, others)
    return (stepped, positions.reshape(3, cells_x, cells_y, cells_z, width))


def solution(mesh):
    placed = (
        P(None, "gx", "gy", "gz", None),
        P("gx", "gy", "gz", None),
        P("gx", "gy", "gz", None),
        P("gx", "gy", "gz", None),
        P("gx", "gy", "gz"),
        P(None, ("gx", "gy", "gz")),
        P(None, ("gx", "gy", "gz")),
        P(None, ("gx", "gy", "gz")),
    )
    return jax.shard_map(
        per_device,
        mesh=mesh,
        in_specs=placed,
        out_specs=(P(None, ("gx", "gy", "gz")), P(None, "gx", "gy", "gz", None)),
        check_vma=False,
    )
```

time: 73.5 us -> 62.3 us (0.85)
  Pallas kernels: 29.6 us -> 23.9 us
  waiting for transfers between devices: 21.9 us -> 18.9 us
  other arithmetic: 2.07 us -> 0.1 us
    ppermute x10 -> x5, starting transfers between devices: 17.1 us -> 4.18 us  [from_partner(): lax.ppermute(block, axis, [(i ^ mask, i) for i in range(lax.axis_size(axi...]
    ppermute x10 -> x5, waiting for transfers between devices: 21.9 us -> 13.8 us  [from_partner(): lax.ppermute(block, axis, [(i ^ mask, i) for i in range(lax.axis_size(axi...]
    ppermute x0 -> x3, starting transfers between devices: none -> 7.63 us  [from_next(): lax.ppermute(block, axis, [((i + 1) % count, i) for i in range(count)])]
    pallas_call x2, Pallas kernels: 28.1 us -> 22.3 us  [the longest x1 20.5 us: pair_sums(): pl.pallas_call(functools.partial(pair_kernel, sizes), out_shape=(jax.Shap...]
    all_to_all x0 -> x1, starting transfers between devices: none -> 4.76 us  [per_device(): packed = lax.all_to_all(bodies, axes, 0, 0).reshape(devices * PACKED, LANES)]
    ppermute x0 -> x3, waiting for transfers between devices: none -> 2.63 us  [from_next(): lax.ppermute(block, axis, [((i + 1) % count, i) for i in range(count)])]
    all_to_all x0 -> x1, waiting for transfers between devices: none -> 2.47 us  [per_device(): packed = lax.all_to_all(bodies, axes, 0, 0).reshape(devices * PACKED, LANES)]
    add x7 -> x4, other arithmetic: 1.35 us -> 0.02 us  [per_device(): totals = totals + others]
  transfers between devices with their start and end apart: 10 -> 9, of which waited for: 10 -> 8; matrix products, arithmetic and copies ran while one was open for 0% -> 1% of each run, Pallas kernels for 0% -> 0%
where the time goes in v3:
time: 62.3 us; the launch traced here: 61.7 us
  Pallas kernels  23.9 us (38%)
  waiting for transfers between devices  18.9 us (30%)
  starting transfers between devices  16.6 us (27%)
  local copies, waits for them, and re-layouts  1.47 us (2%)
  between operations  0.72 us (1%)
    pallas_call x1, Pallas kernels, pair_sums(): pl.pallas_call(functools.partial(pair_kernel, sizes), out_shape=(jax.Shap...  20.5 us
    ppermute x5, waiting for transfers between devices, from_partner(): lax.ppermute(block, axis, [(i ^ mask, i) for i in range(lax.axis_size(axi...  13.8 us
    ppermute x3, starting transfers between devices, from_next(): lax.ppermute(block, axis, [((i + 1) % count, i) for i in range(count)])  7.63 us
    all_to_all x1, starting transfers between devices, per_device(): packed = lax.all_to_all(bodies, axes, 0, 0).reshape(devices * PACKED, LANES)  4.76 us
    ppermute x5, starting transfers between devices, from_partner(): lax.ppermute(block, axis, [(i ^ mask, i) for i in range(lax.axis_size(axi...  4.18 us
    ppermute x3, waiting for transfers between devices, from_next(): lax.ppermute(block, axis, [((i + 1) % count, i) for i in range(count)])  2.63 us
    all_to_all x1, waiting for transfers between devices, per_device(): packed = lax.all_to_all(bodies, axes, 0, 0).reshape(devices * PACKED, LANES)  2.47 us
    pallas_call x1, Pallas kernels, per_device(): pl.pallas_call(functools.partial(move_kernel, sizes), out_shape=(jax.Shap...  1.83 us
  transfers between devices with their start and end apart: 9, of which 8 were waited for; matrix products, arithmetic and copies ran while one was open for 1% of the time, Pallas kernels for 0%

profile of v3, /device:TPU:0, one launch (start us, length us, event | category | flops | bytes accessed | tf_op | source)
XLA Modules:
  0.0 61.7 jit_solution(3183398442979209306)
XLA Ops:
  0.6 1.6 %shard_map.95 = (f32[128,128]{1,0:T(8,128)}, f32[64,128]{1,0:T(8,128)}, f32[32,4,128]{2,1,0:T(4,128)}) custom-call(s32[2,2,4]{2,1,0:T(2,128)} %counts.1, f32[3,2,2,4,128]{4,3,2,1,0:T(4,128)} %local.1, f32[2,2,4,128]{3,2,1,0:T(4,128)} %charges.1, f32[2,2,4,128]{3,2,1,0:T(4,128)} %radii.1, s32[2,2,4,128]{3,2,1,0:T(4,128)} %slots.1, f32[12,24]{1,0:T(8,128)} %poses.1, ...), custom_call_target="tpu_custom_call" | custom-call | tf_op jit(solution)/shard_map/pallas_call | solution.py:503
  2.2 2.4 %collective-permute-start = (f32[64,128]{1,0:T(8,128)}, f32[64,128]{1,0:T(8,128)S(1)}, u32[]{:S(2)}, u32[]{:S(2)}) collective-permute-start(f32[64,128]{1,0:T(8,128)} %get-tuple-element.10), channel_id=1, source_target_pairs={{4,0},{8,4},{12,8},{0,12},{5,1},{9,5},{13,9},{1,13},{6,2},{10,6},{... | collective-permute-start | bytes 98312 | tf_op jit(solution)/shard_map/ppermute | solution.py:481
  4.6 0.8 %copy_dynamic-update-slice_fusion = f32[2,3,4,8,128]{4,3,1,0,2:T(8,128)S(1)} fusion(f32[2,2,4,8,128]{4,3,2,1,0:T(8,128)} %bitcast.10), kind=kLoop, calls=%fused_computation | loop fusion | bytes 131072
  5.4 1.1 %collective-permute-done.first_halo = f32[64,128]{1,0:T(8,128)S(1)} collective-permute-done((f32[64,128]{1,0:T(8,128)}, f32[64,128]{1,0:T(8,128)S(1)}, u32[]{:S(2)}, u32[]{:S(2)}) %collective-permute-start) | collective-permute-done | bytes 32800 | tf_op jit(solution)/shard_map/ppermute | solution.py:481
  6.5 1.6 %collective-permute-start.1 = (f32[96,128]{1,0:T(8,128)S(1)}, f32[96,128]{1,0:T(8,128)S(1)}, u32[]{:S(2)}, u32[]{:S(2)}) collective-permute-start(f32[96,128]{1,0:T(8,128)S(1)} %bitcast.14), channel_id=1, source_target_pairs={{16,0},{0,16},{17,1},{1,17},{18,2},{2,18},{19,3},{3,19},{20,4},{4,... | collective-permute-start | bytes 147464 | tf_op jit(solution)/shard_map/ppermute | solution.py:481
  8.1 4.8 %all-to-all-start = ((f32[32,4,128]{2,1,0:T(4,128)}), f32[32,4,128]{2,1,0:T(4,128)S(1)}, u32[]{:S(2)}, u32[]{:S(2)}) async-start(f32[32,4,128]{2,1,0:T(4,128)} %get-tuple-element.11), calls=%async_computation | async-start | bytes 131072 | tf_op jit(solution)/shard_map/all_to_all | solution.py:514
  12.9 0.0 collective-permute-done.1.second_halo
  12.9 0.0 copy-start
  12.9 3.7 %collective-permute-start.2 = (f32[72,128]{1,0:T(8,128)S(1)}, f32[72,128]{1,0:T(8,128)S(1)}, u32[]{:S(2)}, u32[]{:S(2)}) collective-permute-start(f32[72,128]{1,0:T(8,128)S(1)} %bitcast.15), channel_id=1, source_target_pairs={{1,0},{2,1},{3,2},{0,3},{5,4},{6,5},{7,6},{4,7},{9,8},{10,9},{11,1... | collective-permute-start | bytes 110600 | tf_op jit(solution)/shard_map/ppermute | solution.py:481
  16.6 0.1 pad_add_fusion.coords
  16.6 0.0 copy-start.2
  16.6 1.6 %collective-permute-done.2.third_halo = f32[72,128]{1,0:T(8,128)S(1)} collective-permute-done((f32[72,128]{1,0:T(8,128)S(1)}, f32[72,128]{1,0:T(8,128)S(1)}, u32[]{:S(2)}, u32[]{:S(2)}) %collective-permute-start.2) | collective-permute-done | bytes 36896 | tf_op jit(solution)/shard_map/ppermute | solution.py:481
  18.2 2.5 %all-to-all-done = f32[32,4,128]{2,1,0:T(4,128)S(1)} async-done(((f32[32,4,128]{2,1,0:T(4,128)}), f32[32,4,128]{2,1,0:T(4,128)S(1)}, u32[]{:S(2)}, u32[]{:S(2)}) %all-to-all-start) | async-done | bytes 65568 | tf_op jit(solution)/shard_map/all_to_all | solution.py:514
  20.7 0.0 copy-done.2
  20.7 0.0 copy-done
  20.7 20.5 %shard_map.96 = (f32[64,128]{1,0:T(8,128)S(1)}, f32[20,8,128]{2,1,0:T(8,128)S(1)}) custom-call(s32[3]{0:T(128)S(1)} %pad_add_fusion.coords, f32[128,128]{1,0:T(8,128)S(1)} %copy-done, f32[64,128]{1,0:T(8,128)S(1)} %collective-permute-done.first_halo, f32[96,128]{1,0:T(8,128)S(1)} %collective-permute-done.1.second_halo, ...), custom_call_target="tpu_custom_call" | custom-call | tf_op jit(solution)/shard_map/pallas_call | solution.py:453
  41.2 0.0 copy-start.1
  41.2 0.3 collective-permute-start.3
  41.5 1.0 %collective-permute-done.3 = f32[64,128]{1,0:T(8,128)S(1)} collective-permute-done((f32[64,128]{1,0:T(8,128)S(1)}, f32[64,128]{1,0:T(8,128)S(1)}, u32[]{:S(2)}, u32[]{:S(2)}) %collective-permute-start.3) | collective-permute-done | bytes 32800 | tf_op jit(solution)/shard_map/ppermute | solution.py:485
  42.5 2.0 %collective-permute-start.4 = (f32[64,128]{1,0:T(8,128)S(1)}, f32[64,128]{1,0:T(8,128)S(1)}, u32[]{:S(2)}, u32[]{:S(2)}) collective-permute-start(f32[64,128]{1,0:T(8,128)S(1)} %add.12), channel_id=1, source_target_pairs={{8,0},{12,4},{0,8},{4,12},{9,1},{13,5},{1,9},{5,13},{10,2},{14,6},... | collective-permute-start | bytes 98312 | tf_op jit(solution)/shard_map/ppermute | solution.py:485
  44.5 1.9 %collective-permute-done.4 = f32[64,128]{1,0:T(8,128)S(1)} collective-permute-done((f32[64,128]{1,0:T(8,128)S(1)}, f32[64,128]{1,0:T(8,128)S(1)}, u32[]{:S(2)}, u32[]{:S(2)}) %collective-permute-start.4) | collective-permute-done | bytes 32800 | tf_op jit(solution)/shard_map/ppermute | solution.py:485
  46.4 0.0 copy-done.1
  46.4 0.5 collective-permute-start.5
  47.0 3.4 %collective-permute-done.5 = f32[64,128]{1,0:T(8,128)S(1)} collective-permute-done((f32[64,128]{1,0:T(8,128)S(1)}, f32[64,128]{1,0:T(8,128)S(1)}, u32[]{:S(2)}, u32[]{:S(2)}) %collective-permute-start.5) | collective-permute-done | bytes 32800 | tf_op jit(solution)/shard_map/ppermute | solution.py:485
  50.4 0.9 %collective-permute-start.6 = (f32[64,128]{1,0:T(8,128)S(1)}, f32[64,128]{1,0:T(8,128)S(1)}, u32[]{:S(2)}, u32[]{:S(2)}) collective-permute-start(f32[64,128]{1,0:T(8,128)S(1)} %add.14), channel_id=1, source_target_pairs={{1,0},{0,1},{3,2},{2,3},{5,4},{4,5},{7,6},{6,7},{9,8},{8,9},{11,10... | collective-permute-start | bytes 98312 | tf_op jit(solution)/shard_map/ppermute | solution.py:485
  51.3 3.0 %collective-permute-done.6 = f32[64,128]{1,0:T(8,128)S(1)} collective-permute-done((f32[64,128]{1,0:T(8,128)S(1)}, f32[64,128]{1,0:T(8,128)S(1)}, u32[]{:S(2)}, u32[]{:S(2)}) %collective-permute-start.6) | collective-permute-done | bytes 32800 | tf_op jit(solution)/shard_map/ppermute | solution.py:485
  54.3 0.0 copy-start.3
  54.3 0.4 collective-permute-start.7
  54.8 4.5 %collective-permute-done.7.others = f32[64,128]{1,0:T(8,128)S(1)} collective-permute-done((f32[64,128]{1,0:T(8,128)S(1)}, f32[64,128]{1,0:T(8,128)S(1)}, u32[]{:S(2)}, u32[]{:S(2)}) %collective-permute-start.7) | collective-permute-done | bytes 32800 | tf_op jit(solution)/shard_map/ppermute | solution.py:485
  59.2 0.0 copy-done.3
  59.2 0.6 copy-done.4
  59.8 1.8 %shard_map.97 = (f32[12,24]{1,0:T(8,128)}, f32[3,16,128]{2,1,0:T(8,128)}) custom-call(s32[3]{0:T(128)} %copy-done.2, f32[128,128]{1,0:T(8,128)} %get-tuple-element.9.own, f32[20,8,128]{2,1,0:T(8,128)} %copy-done.1, f32[64,128]{1,0:T(8,128)} %copy-done.3, f32[64,128]{1,0:T(8,128)} %copy-done.4), custom_call_target="tpu_custom_call" | custom-call | tf_op jit(solution)/shard_map/pallas_call | solution.py:536
  (9 shorter events, 0.0 us)
Async XLA Ops:
  2.2 4.3 %collective-permute-start = (f32[64,128]{1,0:T(8,128)}, f32[64,128]{1,0:T(8,128)S(1)}, u32[]{:S(2)}, u32[]{:S(2)}) collective-permute-start(f32[64,128]{1,0:T(8,128)} %get-tuple-element.10), channel_id=1, source_target_pairs={{4,0},{8,4},{12,8},{0,12},{5,1},{9,5},{13,9},{1,13},{6,2},{10,6},{... | collective-permute-start | bytes 98312 | tf_op jit(solution)/shard_map/ppermute | solution.py:481
  6.5 6.3 %collective-permute-start.1 = (f32[96,128]{1,0:T(8,128)S(1)}, f32[96,128]{1,0:T(8,128)S(1)}, u32[]{:S(2)}, u32[]{:S(2)}) collective-permute-start(f32[96,128]{1,0:T(8,128)S(1)} %bitcast.14), channel_id=1, source_target_pairs={{16,0},{0,16},{17,1},{1,17},{18,2},{2,18},{19,3},{3,19},{20,4},{4,... | collective-permute-start | bytes 147464 | tf_op jit(solution)/shard_map/ppermute | solution.py:481
  8.1 12.6 %all-to-all-start = ((f32[32,4,128]{2,1,0:T(4,128)}), f32[32,4,128]{2,1,0:T(4,128)S(1)}, u32[]{:S(2)}, u32[]{:S(2)}) async-start(f32[32,4,128]{2,1,0:T(4,128)} %get-tuple-element.11), calls=%async_computation | async-start | bytes 131072 | tf_op jit(solution)/shard_map/all_to_all | solution.py:514
  12.9 7.8 %copy-start = (f32[128,128]{1,0:T(8,128)S(1)}, f32[128,128]{1,0:T(8,128)}, u32[]{:S(2)}) copy-start(f32[128,128]{1,0:T(8,128)} %get-tuple-element.9.own) | copy-start | bytes 196612
  12.9 5.3 %collective-permute-start.2 = (f32[72,128]{1,0:T(8,128)S(1)}, f32[72,128]{1,0:T(8,128)S(1)}, u32[]{:S(2)}, u32[]{:S(2)}) collective-permute-start(f32[72,128]{1,0:T(8,128)S(1)} %bitcast.15), channel_id=1, source_target_pairs={{1,0},{2,1},{3,2},{0,3},{5,4},{6,5},{7,6},{4,7},{9,8},{10,9},{11,1... | collective-permute-start | bytes 110600 | tf_op jit(solution)/shard_map/ppermute | solution.py:481
  16.6 4.0 %copy-start.2 = (s32[3]{0:T(128)}, s32[3]{0:T(128)S(1)}, u32[]{:S(2)}) copy-start(s32[3]{0:T(128)S(1)} %pad_add_fusion.coords) | copy-start | bytes 40
  41.2 5.2 %copy-start.1 = (f32[20,8,128]{2,1,0:T(8,128)}, f32[20,8,128]{2,1,0:T(8,128)S(1)}, u32[]{:S(2)}) copy-start(f32[20,8,128]{2,1,0:T(8,128)S(1)} %get-tuple-element.12.table) | copy-start | bytes 245764
  41.2 1.3 %collective-permute-start.3 = (f32[64,128]{1,0:T(8,128)S(1)}, f32[64,128]{1,0:T(8,128)S(1)}, u32[]{:S(2)}, u32[]{:S(2)}) collective-permute-start(f32[64,128]{1,0:T(8,128)S(1)} %get-tuple-element.13), channel_id=1, source_target_pairs={{4,0},{0,4},{12,8},{8,12},{5,1},{1,5},{13,9},{9,13},{6,2},{2,6},{1... | collective-permute-start | bytes 98312 | tf_op jit(solution)/shard_map/ppermute | solution.py:485
  42.5 3.9 %collective-permute-start.4 = (f32[64,128]{1,0:T(8,128)S(1)}, f32[64,128]{1,0:T(8,128)S(1)}, u32[]{:S(2)}, u32[]{:S(2)}) collective-permute-start(f32[64,128]{1,0:T(8,128)S(1)} %add.12), channel_id=1, source_target_pairs={{8,0},{12,4},{0,8},{4,12},{9,1},{13,5},{1,9},{5,13},{10,2},{14,6},... | collective-permute-start | bytes 98312 | tf_op jit(solution)/shard_map/ppermute | solution.py:485
  46.4 4.0 %collective-permute-start.5 = (f32[64,128]{1,0:T(8,128)S(1)}, f32[64,128]{1,0:T(8,128)S(1)}, u32[]{:S(2)}, u32[]{:S(2)}) collective-permute-start(f32[64,128]{1,0:T(8,128)S(1)} %add.13), channel_id=1, source_target_pairs={{16,0},{0,16},{17,1},{1,17},{18,2},{2,18},{19,3},{3,19},{20,4},{4,... | collective-permute-start | bytes 98312 | tf_op jit(solution)/shard_map/ppermute | solution.py:485
  50.4 3.9 %collective-permute-start.6 = (f32[64,128]{1,0:T(8,128)S(1)}, f32[64,128]{1,0:T(8,128)S(1)}, u32[]{:S(2)}, u32[]{:S(2)}) collective-permute-start(f32[64,128]{1,0:T(8,128)S(1)} %add.14), channel_id=1, source_target_pairs={{1,0},{0,1},{3,2},{2,3},{5,4},{4,5},{7,6},{6,7},{9,8},{8,9},{11,10... | collective-permute-start | bytes 98312 | tf_op jit(solution)/shard_map/ppermute | solution.py:485
  54.3 4.9 %copy-start.3 = (f32[64,128]{1,0:T(8,128)}, f32[64,128]{1,0:T(8,128)S(1)}, u32[]{:S(2)}) copy-start(f32[64,128]{1,0:T(8,128)S(1)} %add.15.totals) | copy-start | bytes 98308
  54.3 4.9 %collective-permute-start.7 = (f32[64,128]{1,0:T(8,128)S(1)}, f32[64,128]{1,0:T(8,128)S(1)}, u32[]{:S(2)}, u32[]{:S(2)}) collective-permute-start(f32[64,128]{1,0:T(8,128)S(1)} %add.15.totals), channel_id=1, source_target_pairs={{2,0},{3,1},{0,2},{1,3},{6,4},{7,5},{4,6},{5,7},{10,8},{11,9},{8,1... | collective-permute-start | bytes 98312 | tf_op jit(solution)/shard_map/ppermute | solution.py:485
  59.2 0.6 copy-start.4

commit v4 on v3

--- a/solution.py
+++ b/solution.py
@@ -28,8 +28,10 @@
 i32 = jnp.int32
 
 T_ALL = (4, 4, 4, 4, 4, 4, 2, 2, 2, 2, 2, 2)
-SP, FO, GA = 4, 4, 8
+SP, FO, GA = 12, 6, 16
 HALO_ORDER = (1, 0, 2)
+SMALL_VMEM = 8 * 1024 * 1024
+PAIR_VMEM = 24 * 1024 * 1024
 
 
 def unpack(packed, owned, spread_rows, table):
@@ -80,10 +82,10 @@
     for x in range(cells_x):
         for y in range(cells_y):
             base = (x * cells_y + y) * cells_z * ROWS
-            held = jnp.zeros((cells_z, LANES), i32)
+            count = jnp.zeros((cells_z, LANES), i32)
             for z in range(cells_z):
-                held = jnp.where(row == z, counts[x, y, z], held)
-            filled = lane < held
+                count = jnp.where(row == z, counts[x, y, z], count)
+            filled = lane < count
             slot = slots[x, y].astype(f32)
             offset = jnp.floor((slot + 0.5) * (1.0 / owned))
             body = slot - offset * owned
@@ -98,7 +100,7 @@
                 jnp.where(filled, charges[x, y], 0.0),
                 jnp.where(filled, radii[x, y], EMPTY / SCALE),
                 code,
-                held.astype(f32),
+                count.astype(f32),
                 jnp.zeros((cells_z, LANES), f32),
             ]
             for k, value in enumerate(rows):
@@ -140,8 +142,11 @@
     ]
     rows = {cell: [] for cell in own}
     later = []
+    full = lambda cell: all(i % 2 == 0 for i in cell)
     for low, high in pairs:
-        if low in rows and high not in rows:
+        if low in rows and high in rows and low != high and full(low) != full(high):
+            rows[high if full(low) else low].append(low if full(low) else high)
+        elif low in rows and high not in rows:
             rows[low].append(high)
         elif high in rows and low not in rows:
             rows[high].append(low)
@@ -167,8 +172,8 @@
     dy = column[1] - row[1]
     dz = column[2] - row[2]
     dist_sq = dx * dx + dy * dy + dz * dz
-    inverse = lax.rsqrt(jnp.maximum(dist_sq, 1e-30))
-    dist = dist_sq * inverse
+    inverse = lax.rsqrt(dist_sq)
+    dist = pl.reciprocal(inverse, approx=True)
     inv_reach = jnp.minimum(inverse, 1.0 / dist_floor)
     gap = (column[3] + row[3]) - dist
     cut = jnp.maximum(SCALE * SCALE - dist_sq, 0.0)
@@ -178,8 +183,8 @@
 
 
 def pair_kernel(
-    sizes, coords, own, first_halo, second_halo, third_halo, packed, out, table,
-    spread_rows, raw, pos, arms, lane_at, chunk_at, held, order, wide, row_force, column_force, contrib,
+    sizes, coords, own, first_halo, second_halo, third_halo, packed, out, table, kept,
+    sums, spread_rows, raw, pos, arms, lane_at, chunk_at, held, order, wide, row_force, column_force, contrib,
 ):
     cells_x, cells_y, cells_z, count_x, count_y, count_z, owned = sizes
     chunks = table.shape[1]
@@ -194,6 +199,7 @@
     def put(cell, ref, index):
         raw[cell * ROWS : (cell + 1) * ROWS, :] = ref[index * ROWS : (index + 1) * ROWS, :]
 
+    kept[...] = own[...]
     extents = (cells_x, cells_y, cells_z)
     halos = (first_halo, second_halo, third_halo)
     for place_at in itertools.product(*[range(extent + 1) for extent in extents]):
@@ -255,7 +261,7 @@
     row_force[...] = jnp.zeros(row_force.shape, f32)
     plan = pair_plan(cells_x, cells_y, cells_z)
     listed = [at(*column) for column, _ in plan]
-    listed += [listed[-1]] * (-len(listed) % 4)
+    listed += [listed[-1]] * (-len(listed) % SP)
     for n, cell in enumerate(listed):
         order[n] = cell
     kind = lax.broadcasted_iota(i32, (32, 5 * LANES), 1) // LANES
@@ -273,21 +279,21 @@
             parts = jnp.concatenate([high, middle, low, jnp.zeros_like(low)], axis=0).astype(jnp.bfloat16)
             out_wide = lax.dot_general(parts, picker, (((0,), (0,)), ((), ())), preferred_element_type=f32)
             for k in range(5):
-                wide[cell, k, :, :] = out_wide[:, k * LANES : (k + 1) * LANES]
+                wide[step * SP + n, k, :, :] = out_wide[:, k * LANES : (k + 1) * LANES]
         return carry
 
     lax.fori_loop(0, len(listed) // SP, spread, 0)
 
-    for column, rows in plan:
+    for number, (column, rows) in enumerate(plan):
         column_cell = at(*column)
         row_cells = [at(*row) for row in rows]
 
-        def tile_pairs(first, together, step, inner, column_cell=column_cell, row_cells=row_cells):
+        def tile_pairs(first, together, step, inner, number=number, column_cell=column_cell, row_cells=row_cells):
             spans, cols = [], []
             for n in range(together):
                 span = pl.ds(pl.multiple_of((first + step * together + n) * 8, 8), 8)
                 spans.append(span)
-                cols.append([wide[column_cell, k, span, :] for k in range(5)])
+                cols.append([wide[number, k, span, :] for k in range(5)])
             sums = [[None] * 3 for _ in range(together)]
             for row_cell in row_cells:
                 row = [
@@ -306,7 +312,7 @@
                         row_force[k, span, :] = row_force[k, span, :] - back[k]
             for n in range(together):
                 for k in range(3):
-                    column_force[column_cell, k, spans[n], :] = sums[n][k]
+                    column_force[number, k, spans[n], :] = sums[n][k]
             return inner
 
         tiles = (held[column_cell] + 7) // 8
@@ -321,27 +327,27 @@
 
     ones = jnp.where(lax.broadcasted_iota(i32, (16, 2 * LANES), 0) == 0, 1.0, 0.0).astype(jnp.bfloat16)
 
-    def fold_line(cell):
-        value = column_force[cell].reshape(3 * LANES, LANES)
+    def fold_line(number):
+        value = column_force[number].reshape(3 * LANES, LANES)
         high = value.astype(jnp.bfloat16)
         low = (value - high.astype(f32)).astype(jnp.bfloat16)
         both = jnp.concatenate([high, low], axis=1)
         return lax.dot_general(ones, both, (((1,), (1,)), ((), ())), preferred_element_type=f32)
 
-    def fold(cells_now):
-        lines = [fold_line(cell) for cell in cells_now]
-        for cell, line in zip(cells_now, lines):
-            span = pl.ds(pl.multiple_of(cell * ROWS, 8), 8)
+    def fold(first, many):
+        lines = [fold_line(first + n) for n in range(many)]
+        for n in range(many):
+            span = pl.ds(pl.multiple_of(order[first + n] * ROWS, 8), 8)
             for k in range(3):
-                row_force[k, span, :] += line[:8, k * LANES : (k + 1) * LANES]
+                row_force[k, span, :] += lines[n][:8, k * LANES : (k + 1) * LANES]
 
     def fold_step(step, carry):
-        fold([order[step * FO + n] for n in range(FO)])
+        fold(step * FO, FO)
         return carry
 
     even = len(plan) // FO
     lax.fori_loop(0, even, fold_step, 0)
-    fold([order[n] for n in range(even * FO, len(plan))])
+    fold(even * FO, len(plan) - even * FO)
 
     def twist(group, carry):
         first = pl.multiple_of(group * 64, 64)
@@ -390,8 +396,13 @@
         return total + lax.dot_general(left, right, (((1,), (1,)), ((), ())), preferred_element_type=f32)
 
     total = lax.fori_loop(0, padded // GA, gather_sums, jnp.zeros((chunks * 16, LANES), f32))
-    for chunk in range(chunks):
-        out[chunk * 8 : chunk * 8 + 8, :] = total[chunk * 16 : chunk * 16 + 8] + total[chunk * 16 + 8 : chunk * 16 + 16]
+    sums[...] = total
+    for first in range(0, chunks, 8):
+        many = min(8, chunks - first)
+        for k in range(6):
+            out[k, first : first + many, :] = (
+                sums[pl.ds(first * 16 + k, many, stride=16), :] + sums[pl.ds(first * 16 + 8 + k, many, stride=16), :]
+            )
 
 
 def advance_rows(pose, force, torque, mobility, noise):
@@ -418,7 +429,7 @@
         many = min(8, chunks - first)
         row = [table[k, first : first + many, :] for k in range(BODY_ROWS)]
         total = [
-            totals[pl.ds(first * 8 + k, many, stride=8), :] + others[pl.ds(first * 8 + k, many, stride=8), :]
+            totals[k, first : first + many, :] + others[k, first : first + many, :]
             for k in range(6)
         ]
         new = advance_rows(row[:12], total[:3], total[3:], row[12:14], row[14:20])
@@ -450,15 +461,18 @@
     smem = pl.BlockSpec(memory_space=pltpu.SMEM)
     cells = (cells_x + 1) * (cells_y + 1) * (cells_z + 1)
     padded = -(-cells // 16) * 16
+    columns = -(-len(pair_plan(cells_x, cells_y, cells_z)) // SP) * SP
     return pl.pallas_call(
         functools.partial(pair_kernel, sizes),
         out_shape=(
-            jax.ShapeDtypeStruct((chunks * 8, LANES), f32),
+            jax.ShapeDtypeStruct((6, chunks, LANES), f32),
             jax.ShapeDtypeStruct((BODY_ROWS, chunks, LANES), f32),
+            jax.ShapeDtypeStruct(own.shape, f32),
         ),
         in_specs=[smem] + [vmem] * 5,
-        out_specs=(vmem, vmem),
+        out_specs=(vmem, vmem, vmem),
         scratch_shapes=[
+            pltpu.VMEM((chunks * 16, LANES), f32),
             pltpu.VMEM((BODY_ROWS // PACKED,) + packed.shape, f32),
             pltpu.VMEM((padded * ROWS, LANES), f32),
             pltpu.VMEM((padded * ROWS, LANES), f32),
@@ -467,12 +481,12 @@
             pltpu.VMEM((padded, LANES), i32),
             pltpu.SMEM((padded,), i32),
             pltpu.SMEM((padded,), i32),
-            pltpu.VMEM((cells, 5, LANES, LANES), f32),
+            pltpu.VMEM((columns, 5, LANES, LANES), f32),
             pltpu.VMEM((3, padded * ROWS, LANES), f32),
-            pltpu.VMEM((cells, 3, LANES, LANES), f32),
+            pltpu.VMEM((columns, 3, LANES, LANES), f32),
             pltpu.VMEM((padded * ROWS, LANES), f32),
         ],
-        compiler_params=pltpu.CompilerParams(vmem_limit_bytes=48 * 1024 * 1024),
+        compiler_params=pltpu.CompilerParams(vmem_limit_bytes=PAIR_VMEM),
     )(coords, own, first_halo, second_halo, third_halo, packed)
 
 
@@ -523,7 +537,7 @@
         extended = jnp.concatenate([extended, halos[-1].reshape(shape)], axis=axis)
 
     sizes = (cells_x, cells_y, cells_z) + counts + (owned,)
-    totals, table = pair_sums(sizes, coords, own, *halos, packed)
+    totals, table, kept = pair_sums(sizes, coords, own, *halos, packed)
 
     others = jnp.zeros_like(totals)
     for axis in ("gy", "gx", "gz"):
@@ -542,7 +556,8 @@
         in_specs=[smem] + [vmem] * 4,
         out_specs=(vmem, vmem),
         scratch_shapes=[pltpu.VMEM((table.shape[1] * 16, LANES), f32)],
-    )(coords, own, table, totals, others)
+        compiler_params=pltpu.CompilerParams(vmem_limit_bytes=SMALL_VMEM),
+    )(coords, kept, table, totals, others)
     return (stepped, positions.reshape(3, cells_x, cells_y, cells_z, width))
 
 

time: 62.3 us -> 58.7 us (0.942)
  Pallas kernels: 23.9 us -> 21.3 us
  starting transfers between devices: 16.6 us -> 18.9 us
  waiting for transfers between devices: 18.9 us -> 16.8 us
    ppermute x5, starting transfers between devices: 4.18 us -> 6.51 us  [from_partner(): lax.ppermute(block, axis, [(i ^ mask, i) for i in range(lax.axis_size(axi...]
    pallas_call x1, Pallas kernels: 20.5 us -> 18.3 us  [pair_sums(): pl.pallas_call(functools.partial(pair_kernel, sizes), out_shape=(jax.Shap...]
    ppermute x5, waiting for transfers between devices: 13.8 us -> 11.7 us  [from_partner(): lax.ppermute(block, axis, [(i ^ mask, i) for i in range(lax.axis_size(axi...]
    unnamed x11 -> x3, local copies, waits for them, and re-layouts: 1.46 us -> 0.85 us
  transfers between devices with their start and end apart: 9 -> 9, of which waited for: 8 -> 8; matrix products, arithmetic and copies ran while one was open for 1% -> 2% of each run, Pallas kernels for 0% -> 0%
where the time goes in v4:
time: 58.7 us
  Pallas kernels  21.3 us (36%)
  starting transfers between devices  18.9 us (32%)
  waiting for transfers between devices  16.8 us (29%)
  local copies, waits for them, and re-layouts  0.86 us (1%)
  between operations  0.71 us (1%)
    pallas_call x1, Pallas kernels, pair_sums(): pl.pallas_call(functools.partial(pair_kernel, sizes), out_shape=(jax.Shap...  18.3 us
    ppermute x5, waiting for transfers between devices, from_partner(): lax.ppermute(block, axis, [(i ^ mask, i) for i in range(lax.axis_size(axi...  11.7 us
    ppermute x3, starting transfers between devices, from_next(): lax.ppermute(block, axis, [((i + 1) % count, i) for i in range(count)])  7.63 us
    ppermute x5, starting transfers between devices, from_partner(): lax.ppermute(block, axis, [(i ^ mask, i) for i in range(lax.axis_size(axi...  6.51 us
    all_to_all x1, starting transfers between devices, per_device(): packed = lax.all_to_all(bodies, axes, 0, 0).reshape(devices * PACKED, LANES)  4.76 us
    ppermute x3, waiting for transfers between devices, from_next(): lax.ppermute(block, axis, [((i + 1) % count, i) for i in range(count)])  2.63 us
    all_to_all x1, waiting for transfers between devices, per_device(): packed = lax.all_to_all(bodies, axes, 0, 0).reshape(devices * PACKED, LANES)  2.47 us
    pallas_call x1, Pallas kernels, per_device(): pl.pallas_call(functools.partial(prep_kernel, (cells_x, cells_y, cells_z,...  1.56 us
  transfers between devices with their start and end apart: 9, of which 8 were waited for; matrix products, arithmetic and copies ran while one was open for 2% of the time, Pallas kernels for 0%

profile of v4, /device:TPU:0, one launch (start us, length us, event | category | flops | bytes accessed | tf_op | source)
XLA Modules:
  0.0 58.7 jit_solution(14379234435759349081)
XLA Ops:
  0.6 1.6 %shard_map.95 = (f32[128,128]{1,0:T(8,128)}, f32[64,128]{1,0:T(8,128)}, f32[32,4,128]{2,1,0:T(4,128)}) custom-call(s32[2,2,4]{2,1,0:T(2,128)} %counts.1, f32[3,2,2,4,128]{4,3,2,1,0:T(4,128)} %local.1, f32[2,2,4,128]{3,2,1,0:T(4,128)} %charges.1, f32[2,2,4,128]{3,2,1,0:T(4,128)} %radii.1, s32[2,2,4,128]{3,2,1,0:T(4,128)} %slots.1, f32[12,24]{1,0:T(8,128)} %poses.1, ...), custom_call_target="tpu_custom_call" | custom-call | tf_op jit(solution)/shard_map/pallas_call | solution.py:517
  2.2 2.4 %collective-permute-start = (f32[64,128]{1,0:T(8,128)}, f32[64,128]{1,0:T(8,128)S(1)}, u32[]{:S(2)}, u32[]{:S(2)}) collective-permute-start(f32[64,128]{1,0:T(8,128)} %get-tuple-element.11), channel_id=1, source_target_pairs={{4,0},{8,4},{12,8},{0,12},{5,1},{9,5},{13,9},{1,13},{6,2},{10,6},{... | collective-permute-start | bytes 98312 | tf_op jit(solution)/shard_map/ppermute | solution.py:495
  4.6 0.8 %copy_dynamic-update-slice_fusion = f32[2,3,4,8,128]{4,3,1,0,2:T(8,128)S(1)} fusion(f32[2,2,4,8,128]{4,3,2,1,0:T(8,128)} %bitcast.10), kind=kLoop, calls=%fused_computation | loop fusion | bytes 131072
  5.4 1.1 %collective-permute-done.first_halo = f32[64,128]{1,0:T(8,128)S(1)} collective-permute-done((f32[64,128]{1,0:T(8,128)}, f32[64,128]{1,0:T(8,128)S(1)}, u32[]{:S(2)}, u32[]{:S(2)}) %collective-permute-start) | collective-permute-done | bytes 32800 | tf_op jit(solution)/shard_map/ppermute | solution.py:495
  6.5 1.6 %collective-permute-start.1 = (f32[96,128]{1,0:T(8,128)S(1)}, f32[96,128]{1,0:T(8,128)S(1)}, u32[]{:S(2)}, u32[]{:S(2)}) collective-permute-start(f32[96,128]{1,0:T(8,128)S(1)} %bitcast.14), channel_id=1, source_target_pairs={{16,0},{0,16},{17,1},{1,17},{18,2},{2,18},{19,3},{3,19},{20,4},{4,... | collective-permute-start | bytes 147464 | tf_op jit(solution)/shard_map/ppermute | solution.py:495
  8.1 4.8 %all-to-all-start = ((f32[32,4,128]{2,1,0:T(4,128)}), f32[32,4,128]{2,1,0:T(4,128)S(1)}, u32[]{:S(2)}, u32[]{:S(2)}) async-start(f32[32,4,128]{2,1,0:T(4,128)} %get-tuple-element.12), calls=%async_computation | async-start | bytes 131072 | tf_op jit(solution)/shard_map/all_to_all | solution.py:528
  12.9 0.0 collective-permute-done.1.second_halo
  12.9 0.0 copy-start
  12.9 3.7 %collective-permute-start.2 = (f32[72,128]{1,0:T(8,128)S(1)}, f32[72,128]{1,0:T(8,128)S(1)}, u32[]{:S(2)}, u32[]{:S(2)}) collective-permute-start(f32[72,128]{1,0:T(8,128)S(1)} %bitcast.15), channel_id=1, source_target_pairs={{1,0},{2,1},{3,2},{0,3},{5,4},{6,5},{7,6},{4,7},{9,8},{10,9},{11,1... | collective-permute-start | bytes 110600 | tf_op jit(solution)/shard_map/ppermute | solution.py:495
  16.6 0.1 pad_add_fusion.coords
  16.6 1.6 %collective-permute-done.2.third_halo = f32[72,128]{1,0:T(8,128)S(1)} collective-permute-done((f32[72,128]{1,0:T(8,128)S(1)}, f32[72,128]{1,0:T(8,128)S(1)}, u32[]{:S(2)}, u32[]{:S(2)}) %collective-permute-start.2) | collective-permute-done | bytes 36896 | tf_op jit(solution)/shard_map/ppermute | solution.py:495
  18.2 2.5 %all-to-all-done = f32[32,4,128]{2,1,0:T(4,128)S(1)} async-done(((f32[32,4,128]{2,1,0:T(4,128)}), f32[32,4,128]{2,1,0:T(4,128)S(1)}, u32[]{:S(2)}, u32[]{:S(2)}) %all-to-all-start) | async-done | bytes 65568 | tf_op jit(solution)/shard_map/all_to_all | solution.py:528
  20.7 0.0 copy-done
  20.7 18.3 %shard_map.96 = (f32[6,8,128]{2,1,0:T(8,128)S(1)}, f32[20,8,128]{2,1,0:T(8,128)S(1)}, f32[128,128]{1,0:T(8,128)S(1)}) custom-call(s32[3]{0:T(128)S(1)} %pad_add_fusion.coords, f32[128,128]{1,0:T(8,128)S(1)} %copy-done, f32[64,128]{1,0:T(8,128)S(1)} %collective-permute-done.first_halo, f32[96,128]{1,0:T(8,128)S(1)} %collective-permute-done.1.second_halo, ...), custom_call_target="tpu_custom_call" | custom-call | tf_op jit(solution)/shard_map/pallas_call | solution.py:465
  39.0 0.1 collective-permute-start.3
  39.1 1.2 %collective-permute-done.3 = f32[6,8,128]{2,1,0:T(8,128)S(1)} collective-permute-done((f32[6,8,128]{2,1,0:T(8,128)S(1)}, f32[6,8,128]{2,1,0:T(8,128)S(1)}, u32[]{:S(2)}, u32[]{:S(2)}) %collective-permute-start.3) | collective-permute-done | bytes 24608 | tf_op jit(solution)/shard_map/ppermute | solution.py:499
  40.3 1.9 %collective-permute-start.4 = (f32[6,8,128]{2,1,0:T(8,128)S(1)}, f32[6,8,128]{2,1,0:T(8,128)S(1)}, u32[]{:S(2)}, u32[]{:S(2)}) collective-permute-start(f32[6,8,128]{2,1,0:T(8,128)S(1)} %add.12), channel_id=1, source_target_pairs={{8,0},{12,4},{0,8},{4,12},{9,1},{13,5},{1,9},{5,13},{10,2},{14,6},... | collective-permute-start | bytes 73736 | tf_op jit(solution)/shard_map/ppermute | solution.py:499
  42.2 1.9 %collective-permute-done.4 = f32[6,8,128]{2,1,0:T(8,128)S(1)} collective-permute-done((f32[6,8,128]{2,1,0:T(8,128)S(1)}, f32[6,8,128]{2,1,0:T(8,128)S(1)}, u32[]{:S(2)}, u32[]{:S(2)}) %collective-permute-start.4) | collective-permute-done | bytes 24608 | tf_op jit(solution)/shard_map/ppermute | solution.py:499
  44.1 2.7 %collective-permute-start.5 = (f32[6,8,128]{2,1,0:T(8,128)S(1)}, f32[6,8,128]{2,1,0:T(8,128)S(1)}, u32[]{:S(2)}, u32[]{:S(2)}) collective-permute-start(f32[6,8,128]{2,1,0:T(8,128)S(1)} %add.13), channel_id=1, source_target_pairs={{16,0},{0,16},{17,1},{1,17},{18,2},{2,18},{19,3},{3,19},{20,4},{4,... | collective-permute-start | bytes 73736 | tf_op jit(solution)/shard_map/ppermute | solution.py:499
  46.8 1.8 %collective-permute-done.5 = f32[6,8,128]{2,1,0:T(8,128)S(1)} collective-permute-done((f32[6,8,128]{2,1,0:T(8,128)S(1)}, f32[6,8,128]{2,1,0:T(8,128)S(1)}, u32[]{:S(2)}, u32[]{:S(2)}) %collective-permute-start.5) | collective-permute-done | bytes 24608 | tf_op jit(solution)/shard_map/ppermute | solution.py:499
  48.6 0.8 %collective-permute-start.6 = (f32[6,8,128]{2,1,0:T(8,128)S(1)}, f32[6,8,128]{2,1,0:T(8,128)S(1)}, u32[]{:S(2)}, u32[]{:S(2)}) collective-permute-start(f32[6,8,128]{2,1,0:T(8,128)S(1)} %add.14), channel_id=1, source_target_pairs={{1,0},{0,1},{3,2},{2,3},{5,4},{4,5},{7,6},{6,7},{9,8},{8,9},{11,10... | collective-permute-start | bytes 73736 | tf_op jit(solution)/shard_map/ppermute | solution.py:499
  49.5 3.0 %collective-permute-done.6 = f32[6,8,128]{2,1,0:T(8,128)S(1)} collective-permute-done((f32[6,8,128]{2,1,0:T(8,128)S(1)}, f32[6,8,128]{2,1,0:T(8,128)S(1)}, u32[]{:S(2)}, u32[]{:S(2)}) %collective-permute-start.6) | collective-permute-done | bytes 24608 | tf_op jit(solution)/shard_map/ppermute | solution.py:499
  52.5 1.0 %collective-permute-start.7 = (f32[6,8,128]{2,1,0:T(8,128)S(1)}, f32[6,8,128]{2,1,0:T(8,128)S(1)}, u32[]{:S(2)}, u32[]{:S(2)}) collective-permute-start(f32[6,8,128]{2,1,0:T(8,128)S(1)} %add.15.totals), channel_id=1, source_target_pairs={{2,0},{3,1},{0,2},{1,3},{6,4},{7,5},{4,6},{5,7},{10,8},{11,9},{8,1... | collective-permute-start | bytes 73736 | tf_op jit(solution)/shard_map/ppermute | solution.py:499
  53.5 3.8 %collective-permute-done.7.others = f32[6,8,128]{2,1,0:T(8,128)S(1)} collective-permute-done((f32[6,8,128]{2,1,0:T(8,128)S(1)}, f32[6,8,128]{2,1,0:T(8,128)S(1)}, u32[]{:S(2)}, u32[]{:S(2)}) %collective-permute-start.7) | collective-permute-done | bytes 24608 | tf_op jit(solution)/shard_map/ppermute | solution.py:499
  57.2 1.5 %shard_map.97 = (f32[12,24]{1,0:T(8,128)}, f32[3,16,128]{2,1,0:T(8,128)}) custom-call(s32[3]{0:T(128)S(1)} %pad_add_fusion.coords, f32[128,128]{1,0:T(8,128)S(1)} %get-tuple-element.13.own, f32[20,8,128]{2,1,0:T(8,128)S(1)} %get-tuple-element.14.table, f32[6,8,128]{2,1,0:T(8,128)S(1)} %add.15.totals, f32[6,8,128]{2,1,0:T(8,128)S(1)} %collective-permute-done.7.others), custom_call_target="tpu_custom_call" | custom-call | tf_op jit(solution)/shard_map/pallas_call | solution.py:550
  (8 shorter events, 0.0 us)
Async XLA Ops:
  2.2 4.3 %collective-permute-start = (f32[64,128]{1,0:T(8,128)}, f32[64,128]{1,0:T(8,128)S(1)}, u32[]{:S(2)}, u32[]{:S(2)}) collective-permute-start(f32[64,128]{1,0:T(8,128)} %get-tuple-element.11), channel_id=1, source_target_pairs={{4,0},{8,4},{12,8},{0,12},{5,1},{9,5},{13,9},{1,13},{6,2},{10,6},{... | collective-permute-start | bytes 98312 | tf_op jit(solution)/shard_map/ppermute | solution.py:495
  6.5 6.3 %collective-permute-start.1 = (f32[96,128]{1,0:T(8,128)S(1)}, f32[96,128]{1,0:T(8,128)S(1)}, u32[]{:S(2)}, u32[]{:S(2)}) collective-permute-start(f32[96,128]{1,0:T(8,128)S(1)} %bitcast.14), channel_id=1, source_target_pairs={{16,0},{0,16},{17,1},{1,17},{18,2},{2,18},{19,3},{3,19},{20,4},{4,... | collective-permute-start | bytes 147464 | tf_op jit(solution)/shard_map/ppermute | solution.py:495
  8.1 12.6 %all-to-all-start = ((f32[32,4,128]{2,1,0:T(4,128)}), f32[32,4,128]{2,1,0:T(4,128)S(1)}, u32[]{:S(2)}, u32[]{:S(2)}) async-start(f32[32,4,128]{2,1,0:T(4,128)} %get-tuple-element.12), calls=%async_computation | async-start | bytes 131072 | tf_op jit(solution)/shard_map/all_to_all | solution.py:528
  12.9 7.8 %copy-start = (f32[128,128]{1,0:T(8,128)S(1)}, f32[128,128]{1,0:T(8,128)}, u32[]{:S(2)}) copy-start(f32[128,128]{1,0:T(8,128)} %get-tuple-element.10.own) | copy-start | bytes 196612
  12.9 5.3 %collective-permute-start.2 = (f32[72,128]{1,0:T(8,128)S(1)}, f32[72,128]{1,0:T(8,128)S(1)}, u32[]{:S(2)}, u32[]{:S(2)}) collective-permute-start(f32[72,128]{1,0:T(8,128)S(1)} %bitcast.15), channel_id=1, source_target_pairs={{1,0},{2,1},{3,2},{0,3},{5,4},{6,5},{7,6},{4,7},{9,8},{10,9},{11,1... | collective-permute-start | bytes 110600 | tf_op jit(solution)/shard_map/ppermute | solution.py:495
  39.0 1.3 %collective-permute-start.3 = (f32[6,8,128]{2,1,0:T(8,128)S(1)}, f32[6,8,128]{2,1,0:T(8,128)S(1)}, u32[]{:S(2)}, u32[]{:S(2)}) collective-permute-start(f32[6,8,128]{2,1,0:T(8,128)S(1)} %get-tuple-element.15), channel_id=1, source_target_pairs={{4,0},{0,4},{12,8},{8,12},{5,1},{1,5},{13,9},{9,13},{6,2},{2,6},{1... | collective-permute-start | bytes 73736 | tf_op jit(solution)/shard_map/ppermute | solution.py:499
  40.3 3.8 %collective-permute-start.4 = (f32[6,8,128]{2,1,0:T(8,128)S(1)}, f32[6,8,128]{2,1,0:T(8,128)S(1)}, u32[]{:S(2)}, u32[]{:S(2)}) collective-permute-start(f32[6,8,128]{2,1,0:T(8,128)S(1)} %add.12), channel_id=1, source_target_pairs={{8,0},{12,4},{0,8},{4,12},{9,1},{13,5},{1,9},{5,13},{10,2},{14,6},... | collective-permute-start | bytes 73736 | tf_op jit(solution)/shard_map/ppermute | solution.py:499
  44.1 4.5 %collective-permute-start.5 = (f32[6,8,128]{2,1,0:T(8,128)S(1)}, f32[6,8,128]{2,1,0:T(8,128)S(1)}, u32[]{:S(2)}, u32[]{:S(2)}) collective-permute-start(f32[6,8,128]{2,1,0:T(8,128)S(1)} %add.13), channel_id=1, source_target_pairs={{16,0},{0,16},{17,1},{1,17},{18,2},{2,18},{19,3},{3,19},{20,4},{4,... | collective-permute-start | bytes 73736 | tf_op jit(solution)/shard_map/ppermute | solution.py:499
  48.6 3.8 %collective-permute-start.6 = (f32[6,8,128]{2,1,0:T(8,128)S(1)}, f32[6,8,128]{2,1,0:T(8,128)S(1)}, u32[]{:S(2)}, u32[]{:S(2)}) collective-permute-start(f32[6,8,128]{2,1,0:T(8,128)S(1)} %add.14), channel_id=1, source_target_pairs={{1,0},{0,1},{3,2},{2,3},{5,4},{4,5},{7,6},{6,7},{9,8},{8,9},{11,10... | collective-permute-start | bytes 73736 | tf_op jit(solution)/shard_map/ppermute | solution.py:499
  52.5 4.7 %collective-permute-start.7 = (f32[6,8,128]{2,1,0:T(8,128)S(1)}, f32[6,8,128]{2,1,0:T(8,128)S(1)}, u32[]{:S(2)}, u32[]{:S(2)}) collective-permute-start(f32[6,8,128]{2,1,0:T(8,128)S(1)} %add.15.totals), channel_id=1, source_target_pairs={{2,0},{3,1},{0,2},{1,3},{6,4},{7,5},{4,6},{5,7},{10,8},{11,9},{8,1... | collective-permute-start | bytes 73736 | tf_op jit(solution)/shard_map/ppermute | solution.py:499

commit v5 on v4

--- a/solution.py
+++ b/solution.py
@@ -28,7 +28,7 @@
 i32 = jnp.int32
 
 T_ALL = (4, 4, 4, 4, 4, 4, 2, 2, 2, 2, 2, 2)
-SP, FO, GA = 12, 6, 16
+SP, FO, GA = 24, 8, 48
 HALO_ORDER = (1, 0, 2)
 SMALL_VMEM = 8 * 1024 * 1024
 PAIR_VMEM = 24 * 1024 * 1024
@@ -540,7 +540,7 @@
     totals, table, kept = pair_sums(sizes, coords, own, *halos, packed)
 
     others = jnp.zeros_like(totals)
-    for axis in ("gy", "gx", "gz"):
+    for axis in ("gz", "gy", "gx"):
         step = 1
         while step < lax.axis_size(axis):
             totals = totals + others

time: 58.7 us -> 58.2 us (level); the launches traced: 58.7 us -> 59.3 us
  starting transfers between devices: 18.9 us -> 20.5 us
  Pallas kernels: 21.3 us -> 20 us
    ppermute x5, starting transfers between devices: 6.51 us -> 8.08 us  [from_partner(): lax.ppermute(block, axis, [(i ^ mask, i) for i in range(lax.axis_size(axi...]
    pallas_call x1, Pallas kernels: 18.3 us -> 17 us  [pair_sums(): pl.pallas_call(functools.partial(pair_kernel, sizes), out_shape=(jax.Shap...]
where the time goes in v5:
time: 58.2 us; the launch traced here: 59.3 us
  starting transfers between devices  20.5 us (35%)
  Pallas kernels  20 us (34%)
  waiting for transfers between devices  17.1 us (29%)
  local copies, waits for them, and re-layouts  0.86 us (1%)
  between operations  0.7 us (1%)
    pallas_call x1, Pallas kernels, pair_sums(): pl.pallas_call(functools.partial(pair_kernel, sizes), out_shape=(jax.Shap...  17 us
    ppermute x5, waiting for transfers between devices, from_partner(): lax.ppermute(block, axis, [(i ^ mask, i) for i in range(lax.axis_size(axi...  12 us
    ppermute x5, starting transfers between devices, from_partner(): lax.ppermute(block, axis, [(i ^ mask, i) for i in range(lax.axis_size(axi...  8.08 us
    ppermute x3, starting transfers between devices, from_next(): lax.ppermute(block, axis, [((i + 1) % count, i) for i in range(count)])  7.63 us
    all_to_all x1, starting transfers between devices, per_device(): packed = lax.all_to_all(bodies, axes, 0, 0).reshape(devices * PACKED, LANES)  4.76 us
    ppermute x3, waiting for transfers between devices, from_next(): lax.ppermute(block, axis, [((i + 1) % count, i) for i in range(count)])  2.63 us
    all_to_all x1, waiting for transfers between devices, per_device(): packed = lax.all_to_all(bodies, axes, 0, 0).reshape(devices * PACKED, LANES)  2.47 us
    pallas_call x1, Pallas kernels, per_device(): pl.pallas_call(functools.partial(prep_kernel, (cells_x, cells_y, cells_z,...  1.56 us
  transfers between devices with their start and end apart: 9, of which 8 were waited for; matrix products, arithmetic and copies ran while one was open for 2% of the time, Pallas kernels for 0%

profile of v5, /device:TPU:0, one launch (start us, length us, event | category | flops | bytes accessed | tf_op | source)
XLA Modules:
  0.0 59.3 jit_solution(1064071600245037439)
XLA Ops:
  0.6 1.6 %shard_map.95 = (f32[128,128]{1,0:T(8,128)}, f32[64,128]{1,0:T(8,128)}, f32[32,4,128]{2,1,0:T(4,128)}) custom-call(s32[2,2,4]{2,1,0:T(2,128)} %counts.1, f32[3,2,2,4,128]{4,3,2,1,0:T(4,128)} %local.1, f32[2,2,4,128]{3,2,1,0:T(4,128)} %charges.1, f32[2,2,4,128]{3,2,1,0:T(4,128)} %radii.1, s32[2,2,4,128]{3,2,1,0:T(4,128)} %slots.1, f32[12,24]{1,0:T(8,128)} %poses.1, ...), custom_call_target="tpu_custom_call" | custom-call | tf_op jit(solution)/shard_map/pallas_call | solution.py:517
  2.2 2.4 %collective-permute-start = (f32[64,128]{1,0:T(8,128)}, f32[64,128]{1,0:T(8,128)S(1)}, u32[]{:S(2)}, u32[]{:S(2)}) collective-permute-start(f32[64,128]{1,0:T(8,128)} %get-tuple-element.11), channel_id=1, source_target_pairs={{4,0},{8,4},{12,8},{0,12},{5,1},{9,5},{13,9},{1,13},{6,2},{10,6},{... | collective-permute-start | bytes 98312 | tf_op jit(solution)/shard_map/ppermute | solution.py:495
  4.6 0.8 %copy_dynamic-update-slice_fusion = f32[2,3,4,8,128]{4,3,1,0,2:T(8,128)S(1)} fusion(f32[2,2,4,8,128]{4,3,2,1,0:T(8,128)} %bitcast.10), kind=kLoop, calls=%fused_computation | loop fusion | bytes 131072
  5.4 1.1 %collective-permute-done.first_halo = f32[64,128]{1,0:T(8,128)S(1)} collective-permute-done((f32[64,128]{1,0:T(8,128)}, f32[64,128]{1,0:T(8,128)S(1)}, u32[]{:S(2)}, u32[]{:S(2)}) %collective-permute-start) | collective-permute-done | bytes 32800 | tf_op jit(solution)/shard_map/ppermute | solution.py:495
  6.5 1.6 %collective-permute-start.1 = (f32[96,128]{1,0:T(8,128)S(1)}, f32[96,128]{1,0:T(8,128)S(1)}, u32[]{:S(2)}, u32[]{:S(2)}) collective-permute-start(f32[96,128]{1,0:T(8,128)S(1)} %bitcast.14), channel_id=1, source_target_pairs={{16,0},{0,16},{17,1},{1,17},{18,2},{2,18},{19,3},{3,19},{20,4},{4,... | collective-permute-start | bytes 147464 | tf_op jit(solution)/shard_map/ppermute | solution.py:495
  8.1 4.8 %all-to-all-start = ((f32[32,4,128]{2,1,0:T(4,128)}), f32[32,4,128]{2,1,0:T(4,128)S(1)}, u32[]{:S(2)}, u32[]{:S(2)}) async-start(f32[32,4,128]{2,1,0:T(4,128)} %get-tuple-element.12), calls=%async_computation | async-start | bytes 131072 | tf_op jit(solution)/shard_map/all_to_all | solution.py:528
  12.9 0.0 collective-permute-done.1.second_halo
  12.9 0.0 copy-start
  12.9 3.7 %collective-permute-start.2 = (f32[72,128]{1,0:T(8,128)S(1)}, f32[72,128]{1,0:T(8,128)S(1)}, u32[]{:S(2)}, u32[]{:S(2)}) collective-permute-start(f32[72,128]{1,0:T(8,128)S(1)} %bitcast.15), channel_id=1, source_target_pairs={{1,0},{2,1},{3,2},{0,3},{5,4},{6,5},{7,6},{4,7},{9,8},{10,9},{11,1... | collective-permute-start | bytes 110600 | tf_op jit(solution)/shard_map/ppermute | solution.py:495
  16.6 0.1 pad_add_fusion.coords
  16.6 1.6 %collective-permute-done.2.third_halo = f32[72,128]{1,0:T(8,128)S(1)} collective-permute-done((f32[72,128]{1,0:T(8,128)S(1)}, f32[72,128]{1,0:T(8,128)S(1)}, u32[]{:S(2)}, u32[]{:S(2)}) %collective-permute-start.2) | collective-permute-done | bytes 36896 | tf_op jit(solution)/shard_map/ppermute | solution.py:495
  18.2 2.5 %all-to-all-done = f32[32,4,128]{2,1,0:T(4,128)S(1)} async-done(((f32[32,4,128]{2,1,0:T(4,128)}), f32[32,4,128]{2,1,0:T(4,128)S(1)}, u32[]{:S(2)}, u32[]{:S(2)}) %all-to-all-start) | async-done | bytes 65568 | tf_op jit(solution)/shard_map/all_to_all | solution.py:528
  20.7 0.0 copy-done
  20.7 17.0 %shard_map.96 = (f32[6,8,128]{2,1,0:T(8,128)S(1)}, f32[20,8,128]{2,1,0:T(8,128)S(1)}, f32[128,128]{1,0:T(8,128)S(1)}) custom-call(s32[3]{0:T(128)S(1)} %pad_add_fusion.coords, f32[128,128]{1,0:T(8,128)S(1)} %copy-done, f32[64,128]{1,0:T(8,128)S(1)} %collective-permute-done.first_halo, f32[96,128]{1,0:T(8,128)S(1)} %collective-permute-done.1.second_halo, ...), custom_call_target="tpu_custom_call" | custom-call | tf_op jit(solution)/shard_map/pallas_call | solution.py:465
  37.7 1.4 %collective-permute-start.3 = (f32[6,8,128]{2,1,0:T(8,128)S(1)}, f32[6,8,128]{2,1,0:T(8,128)S(1)}, u32[]{:S(2)}, u32[]{:S(2)}) collective-permute-start(f32[6,8,128]{2,1,0:T(8,128)S(1)} %get-tuple-element.15), channel_id=1, source_target_pairs={{1,0},{0,1},{3,2},{2,3},{5,4},{4,5},{7,6},{6,7},{9,8},{8,9},{11,10... | collective-permute-start | bytes 73736 | tf_op jit(solution)/shard_map/ppermute | solution.py:499
  39.1 2.5 %collective-permute-done.3 = f32[6,8,128]{2,1,0:T(8,128)S(1)} collective-permute-done((f32[6,8,128]{2,1,0:T(8,128)S(1)}, f32[6,8,128]{2,1,0:T(8,128)S(1)}, u32[]{:S(2)}, u32[]{:S(2)}) %collective-permute-start.3) | collective-permute-done | bytes 24608 | tf_op jit(solution)/shard_map/ppermute | solution.py:499
  41.6 1.9 %collective-permute-start.4 = (f32[6,8,128]{2,1,0:T(8,128)S(1)}, f32[6,8,128]{2,1,0:T(8,128)S(1)}, u32[]{:S(2)}, u32[]{:S(2)}) collective-permute-start(f32[6,8,128]{2,1,0:T(8,128)S(1)} %add.12), channel_id=1, source_target_pairs={{2,0},{3,1},{0,2},{1,3},{6,4},{7,5},{4,6},{5,7},{10,8},{11,9},{8,1... | collective-permute-start | bytes 73736 | tf_op jit(solution)/shard_map/ppermute | solution.py:499
  43.4 2.9 %collective-permute-done.4 = f32[6,8,128]{2,1,0:T(8,128)S(1)} collective-permute-done((f32[6,8,128]{2,1,0:T(8,128)S(1)}, f32[6,8,128]{2,1,0:T(8,128)S(1)}, u32[]{:S(2)}, u32[]{:S(2)}) %collective-permute-start.4) | collective-permute-done | bytes 24608 | tf_op jit(solution)/shard_map/ppermute | solution.py:499
  46.3 0.1 collective-permute-start.5
  46.4 1.1 %collective-permute-done.5 = f32[6,8,128]{2,1,0:T(8,128)S(1)} collective-permute-done((f32[6,8,128]{2,1,0:T(8,128)S(1)}, f32[6,8,128]{2,1,0:T(8,128)S(1)}, u32[]{:S(2)}, u32[]{:S(2)}) %collective-permute-start.5) | collective-permute-done | bytes 24608 | tf_op jit(solution)/shard_map/ppermute | solution.py:499
  47.5 4.7 %collective-permute-start.6 = (f32[6,8,128]{2,1,0:T(8,128)S(1)}, f32[6,8,128]{2,1,0:T(8,128)S(1)}, u32[]{:S(2)}, u32[]{:S(2)}) collective-permute-start(f32[6,8,128]{2,1,0:T(8,128)S(1)} %add.14), channel_id=1, source_target_pairs={{8,0},{12,4},{0,8},{4,12},{9,1},{13,5},{1,9},{5,13},{10,2},{14,6},... | collective-permute-start | bytes 73736 | tf_op jit(solution)/shard_map/ppermute | solution.py:499
  52.2 1.8 %collective-permute-done.6 = f32[6,8,128]{2,1,0:T(8,128)S(1)} collective-permute-done((f32[6,8,128]{2,1,0:T(8,128)S(1)}, f32[6,8,128]{2,1,0:T(8,128)S(1)}, u32[]{:S(2)}, u32[]{:S(2)}) %collective-permute-start.6) | collective-permute-done | bytes 24608 | tf_op jit(solution)/shard_map/ppermute | solution.py:499
  54.0 0.0 collective-permute-start.7
  54.0 3.8 %collective-permute-done.7.others = f32[6,8,128]{2,1,0:T(8,128)S(1)} collective-permute-done((f32[6,8,128]{2,1,0:T(8,128)S(1)}, f32[6,8,128]{2,1,0:T(8,128)S(1)}, u32[]{:S(2)}, u32[]{:S(2)}) %collective-permute-start.7) | collective-permute-done | bytes 24608 | tf_op jit(solution)/shard_map/ppermute | solution.py:499
  57.8 1.5 %shard_map.97 = (f32[12,24]{1,0:T(8,128)}, f32[3,16,128]{2,1,0:T(8,128)}) custom-call(s32[3]{0:T(128)S(1)} %pad_add_fusion.coords, f32[128,128]{1,0:T(8,128)S(1)} %get-tuple-element.13.own, f32[20,8,128]{2,1,0:T(8,128)S(1)} %get-tuple-element.14.table, f32[6,8,128]{2,1,0:T(8,128)S(1)} %add.15.totals, f32[6,8,128]{2,1,0:T(8,128)S(1)} %collective-permute-done.7.others), custom_call_target="tpu_custom_call" | custom-call | tf_op jit(solution)/shard_map/pallas_call | solution.py:550
  (8 shorter events, 0.0 us)
Async XLA Ops:
  2.2 4.3 %collective-permute-start = (f32[64,128]{1,0:T(8,128)}, f32[64,128]{1,0:T(8,128)S(1)}, u32[]{:S(2)}, u32[]{:S(2)}) collective-permute-start(f32[64,128]{1,0:T(8,128)} %get-tuple-element.11), channel_id=1, source_target_pairs={{4,0},{8,4},{12,8},{0,12},{5,1},{9,5},{13,9},{1,13},{6,2},{10,6},{... | collective-permute-start | bytes 98312 | tf_op jit(solution)/shard_map/ppermute | solution.py:495
  6.5 6.3 %collective-permute-start.1 = (f32[96,128]{1,0:T(8,128)S(1)}, f32[96,128]{1,0:T(8,128)S(1)}, u32[]{:S(2)}, u32[]{:S(2)}) collective-permute-start(f32[96,128]{1,0:T(8,128)S(1)} %bitcast.14), channel_id=1, source_target_pairs={{16,0},{0,16},{17,1},{1,17},{18,2},{2,18},{19,3},{3,19},{20,4},{4,... | collective-permute-start | bytes 147464 | tf_op jit(solution)/shard_map/ppermute | solution.py:495
  8.1 12.6 %all-to-all-start = ((f32[32,4,128]{2,1,0:T(4,128)}), f32[32,4,128]{2,1,0:T(4,128)S(1)}, u32[]{:S(2)}, u32[]{:S(2)}) async-start(f32[32,4,128]{2,1,0:T(4,128)} %get-tuple-element.12), calls=%async_computation | async-start | bytes 131072 | tf_op jit(solution)/shard_map/all_to_all | solution.py:528
  12.9 7.8 %copy-start = (f32[128,128]{1,0:T(8,128)S(1)}, f32[128,128]{1,0:T(8,128)}, u32[]{:S(2)}) copy-start(f32[128,128]{1,0:T(8,128)} %get-tuple-element.10.own) | copy-start | bytes 196612
  12.9 5.3 %collective-permute-start.2 = (f32[72,128]{1,0:T(8,128)S(1)}, f32[72,128]{1,0:T(8,128)S(1)}, u32[]{:S(2)}, u32[]{:S(2)}) collective-permute-start(f32[72,128]{1,0:T(8,128)S(1)} %bitcast.15), channel_id=1, source_target_pairs={{1,0},{2,1},{3,2},{0,3},{5,4},{6,5},{7,6},{4,7},{9,8},{10,9},{11,1... | collective-permute-start | bytes 110600 | tf_op jit(solution)/shard_map/ppermute | solution.py:495
  37.7 3.9 %collective-permute-start.3 = (f32[6,8,128]{2,1,0:T(8,128)S(1)}, f32[6,8,128]{2,1,0:T(8,128)S(1)}, u32[]{:S(2)}, u32[]{:S(2)}) collective-permute-start(f32[6,8,128]{2,1,0:T(8,128)S(1)} %get-tuple-element.15), channel_id=1, source_target_pairs={{1,0},{0,1},{3,2},{2,3},{5,4},{4,5},{7,6},{6,7},{9,8},{8,9},{11,10... | collective-permute-start | bytes 73736 | tf_op jit(solution)/shard_map/ppermute | solution.py:499
  41.6 4.7 %collective-permute-start.4 = (f32[6,8,128]{2,1,0:T(8,128)S(1)}, f32[6,8,128]{2,1,0:T(8,128)S(1)}, u32[]{:S(2)}, u32[]{:S(2)}) collective-permute-start(f32[6,8,128]{2,1,0:T(8,128)S(1)} %add.12), channel_id=1, source_target_pairs={{2,0},{3,1},{0,2},{1,3},{6,4},{7,5},{4,6},{5,7},{10,8},{11,9},{8,1... | collective-permute-start | bytes 73736 | tf_op jit(solution)/shard_map/ppermute | solution.py:499
  46.3 1.2 %collective-permute-start.5 = (f32[6,8,128]{2,1,0:T(8,128)S(1)}, f32[6,8,128]{2,1,0:T(8,128)S(1)}, u32[]{:S(2)}, u32[]{:S(2)}) collective-permute-start(f32[6,8,128]{2,1,0:T(8,128)S(1)} %add.13), channel_id=1, source_target_pairs={{4,0},{0,4},{12,8},{8,12},{5,1},{1,5},{13,9},{9,13},{6,2},{2,6},{1... | collective-permute-start | bytes 73736 | tf_op jit(solution)/shard_map/ppermute | solution.py:499
  47.5 6.5 %collective-permute-start.6 = (f32[6,8,128]{2,1,0:T(8,128)S(1)}, f32[6,8,128]{2,1,0:T(8,128)S(1)}, u32[]{:S(2)}, u32[]{:S(2)}) collective-permute-start(f32[6,8,128]{2,1,0:T(8,128)S(1)} %add.14), channel_id=1, source_target_pairs={{8,0},{12,4},{0,8},{4,12},{9,1},{13,5},{1,9},{5,13},{10,2},{14,6},... | collective-permute-start | bytes 73736 | tf_op jit(solution)/shard_map/ppermute | solution.py:499
  54.0 3.8 %collective-permute-start.7 = (f32[6,8,128]{2,1,0:T(8,128)S(1)}, f32[6,8,128]{2,1,0:T(8,128)S(1)}, u32[]{:S(2)}, u32[]{:S(2)}) collective-permute-start(f32[6,8,128]{2,1,0:T(8,128)S(1)} %add.15.totals), channel_id=1, source_target_pairs={{16,0},{0,16},{17,1},{1,17},{18,2},{2,18},{19,3},{3,19},{20,4},{4,... | collective-permute-start | bytes 73736 | tf_op jit(solution)/shard_map/ppermute | solution.py:499
